TPU v7x, 32 devices: a whole 2x2x4 slice. The times are simulated.
32 devices in a mesh: tmpl: 8 (over y, x, core), stn: 4 (over z).
Axes of the slice: x: 2, y: 2, z: 4, core: 2. Of those that a mesh axis runs over, the one named last changes fastest.
Arguments:
- data: bfloat16 [2, 24, 3, 1024], P(None, 'stn', None, 'tmpl'), may hold values from -6 to 6
- waves: bfloat16 [24, 128, 3, 300], P('stn', 'tmpl'), may hold values from -6 to 6
- slot_group: int32 [24, 128, 1], P('stn', 'tmpl'), may hold values from 0 to 7; in each aligned block of 16 rows (0 to 15, 16 to 31, ..., all dimensions but the last counted through in order) at most 4 rows name the same one
- slot_local: int32 [24, 128], P('stn', 'tmpl'), may hold values from 0 to 63
- moveout: int32 [24, 128], P('stn', 'tmpl'), may hold values from 0 to 469
- chan_mask: int32 [24, 3], P('stn'), may hold values 0 or 1
Outputs:
- scores: float32 [2, 512, 256], P(None, ('tmpl', 'stn'))
Inputs may be any that keep to these rules, and one draw needn't show every extreme that they name: `slot_group`: among the 16 slots k*16 to (k+1)*16 - 1 of one station, no template group is named more than 4 times.
All inputs are finite; a program needn't handle non-finite values. No bound on the sum of `chan_mask` on one device may be relied on, other than what follows from the above.
Results may differ from a plain program's by a relative error of at most 0.0029.
Values may be sent and summed in bfloat16 or wider, within the bound.
No kernel may reach another device: no remote copies, remote signals or barrier semaphores. Data moves between devices by JAX's collectives and lax.ppermute only.
A program may use at most 128 MiB of HBM per device.

v0:
```python
import jax
import jax.numpy as jnp
from jax import lax
from jax.sharding import PartitionSpec as P

NK = 256
TPD = 16


epsilon = 1e-06


def hankel(series, tap_count, lag_count):
    width = series.shape[-1]
    repeats = (1,) * (series.ndim - 1) + (tap_count + 1,)
    tiled = jnp.tile(series, repeats)[..., : tap_count * (width + 1)]
    return tiled.reshape(series.shape[:-1] + (tap_count, width + 1))[..., :lag_count]


def shift_rows(values, offsets):
    lag_index = offsets[..., None] + jnp.arange(NK, dtype=jnp.int32)
    return jnp.take_along_axis(values, lag_index, axis=-1)


def body(data, waves, slot_group, slot_local, moveout, chan_mask):
    samples = lax.all_gather(data, "tmpl", axis=3, tiled=True)
    blocks, stations_here, components, width = samples.shape
    slots = waves.shape[1]
    tap_count = waves.shape[3]
    lag_count = width - tap_count + 1
    tmpl_count = lax.axis_size("tmpl")
    slot_most = max(2, 2 * slots // tmpl_count)
    capacity = stations_here * slot_most
    slot_total = tmpl_count * capacity
    per_group = TPD * lax.axis_size("stn")
    group_size = 2
    group_count = stations_here // group_size
    stacked_data = jnp.moveaxis(
        samples.reshape(blocks, group_count, group_size, components, width), 1, 0
    )
    stacked_waves = waves.reshape(group_count, group_size, slots, components, tap_count)
    stacked_mask = chan_mask.reshape(group_count, group_size, components).astype(jnp.float32)

    def correlate(inputs):
        station_data, station_waves, station_mask = inputs
        hankel_rows = hankel(station_data, tap_count, lag_count)
        squares = station_data.astype(jnp.float32) ** 2
        running = jnp.cumsum(squares, axis=-1)
        padded = jnp.concatenate(
            [jnp.zeros(running.shape[:-1] + (1,), jnp.float32), running], axis=-1
        )
        data_power = (
            padded[..., tap_count : tap_count + lag_count] - padded[..., :lag_count]
        ) / tap_count
        wave_power = (
            jnp.einsum(
                "spcj,spcj->spc", station_waves, station_waves, preferred_element_type=jnp.float32
            )
            / tap_count
        )
        numerator = jnp.einsum(
            "spcj,bscjk->spbck", station_waves, hankel_rows, preferred_element_type=jnp.float32
        )
        denominator = (
            tap_count
            * jnp.sqrt(wave_power + epsilon)[:, :, None, :, None]
            * jnp.sqrt(jnp.moveaxis(data_power, 0, 1) + epsilon)[:, None]
        )
        channel_sum = jnp.sum(
            numerator / denominator * station_mask[:, None, None, :, None], axis=3
        )
        scaled = channel_sum / jnp.maximum(jnp.sum(station_mask, axis=-1), 1.0)[:, None, None, None]
        return scaled.astype(jnp.bfloat16)

    row_count = stations_here * slots
    corr_rows = lax.map(correlate, (stacked_data, stacked_waves, stacked_mask)).reshape(
        row_count, blocks, lag_count
    )
    group_ids = slot_group[..., 0]
    same_group = group_ids[:, :, None] == group_ids[:, None, :]
    earlier = jnp.arange(slots)[None, :] < jnp.arange(slots)[:, None]
    slot_rank = jnp.sum((same_group & earlier[None]).astype(jnp.int32), axis=2)
    position = (
        group_ids * capacity
        + jnp.arange(stations_here, dtype=jnp.int32)[:, None] * slot_most
        + slot_rank
    ).reshape(row_count)
    local_ids = slot_local.reshape(row_count)
    shift_by = moveout.reshape(row_count)
    id_rows = jnp.full((slot_total,), -1, jnp.int32).at[position].set(local_ids)
    id_rows = jnp.broadcast_to(
        id_rows.reshape(tmpl_count, capacity, 1), (tmpl_count, capacity, blocks)
    )
    template_axis = jnp.arange(per_group, dtype=jnp.int32)
    offsets = jnp.broadcast_to(shift_by[:, None], (row_count, blocks))
    shifted = shift_rows(corr_rows, offsets)
    send_rows = jnp.zeros((slot_total, blocks, NK), jnp.bfloat16).at[position].set(shifted)
    send_rows = send_rows.reshape(tmpl_count, capacity, blocks, NK)
    values = lax.all_to_all(send_rows, "tmpl", split_axis=0, concat_axis=0, tiled=True)
    template_ids = lax.all_to_all(id_rows, "tmpl", split_axis=0, concat_axis=0, tiled=True)
    items = values.shape[2]
    accumulate_template_ids = template_ids.reshape(slot_total, items)
    onehot = (
        jnp.transpose(accumulate_template_ids)[:, None, :] == template_axis[None, :, None]
    ).astype(jnp.bfloat16)
    stack_sums = jnp.einsum(
        "btq,qbk->btk",
        onehot,
        values.reshape(slot_total, items, NK),
        preferred_element_type=jnp.float32,
    )
    counts = jnp.sum(onehot, axis=2, dtype=jnp.float32)
    stack_sums, counts = (stack_sums, counts)
    owned_sums, owned_counts = (
        lax.psum_scatter(stack_sums, "stn", scatter_dimension=1, tiled=True),
        lax.psum_scatter(counts, "stn", scatter_dimension=1, tiled=True),
    )
    return (
        jnp.sqrt(jnp.float32(tap_count))
        * owned_sums
        / jnp.sqrt(jnp.maximum(owned_counts, 1.0))[..., None]
    )


def solution(mesh):
    in_specs = (
        P(None, "stn", None, "tmpl"),
        P("stn", "tmpl", None, None),
        P("stn", "tmpl", None),
        P("stn", "tmpl"),
        P("stn", "tmpl"),
        P("stn", None),
    )
    out_specs = P(None, ("tmpl", "stn"), None)
    return jax.shard_map(body, mesh=mesh, in_specs=in_specs, out_specs=out_specs, check_vma=False)
```

profile of v0, /device:TPU:0, one launch (start us, length us, event | category | flops | bytes accessed | tf_op | source)
XLA Modules:
  0.0 706.6 jit_solution(5635774270373269156)
XLA Ops:
  6.5 0.7 copy.84
  7.2 0.7 multiply_reduce_fusion
  7.9 0.2 convert_reduce_fusion.1
  8.5 0.8 reshape.167
  9.3 0.9 scatter_custom_fusion
  10.2 0.6 broadcast_in_dim.21
  10.8 5.2 all-to-all-start
  16.0 0.8 broadcast_in_dim_reshape.3
  16.8 0.3 fusion.26
  17.1 0.1 copy.68
  17.2 9.7 %all_gather.3 = bf16[2,6,3,1024]{3,0,2,1:T(2,128)(2,1)S(1)} all-gather(bf16[2,6,3,128]{3,0,2,1:T(2,128)(2,1)} %param.8), channel_id=1, replica_groups=mesh['tmpl'=8,'stn'=4] {'tmpl'}, dimensions={3}, use_global_device_ids=true | all-gather | bytes 82944 | tf_op jit(solution)/shard_map/all_gather | solution.py:26
  27.0 0.7 convert_element_type.31
  27.6 0.1 copy.51
  27.7 152.6 %while.10 = (s32[]{:T(128)}, bf16[3,2,16,2,725]{4,3,2,1,0:T(2,128)(2,1)S(1)}, bf16[3,2,2,3,1024]{4,1,3,2,0:T(2,128)(2,1)S(1)}, bf16[3,2,16,3,300]{4,2,3,1,0:T(8,...) while((s32[]{:T(128)}, bf16[3,2,16,2,725]{4,3,2,1,0:T(2,128)(2,1)S(1)}, ...), condition=%wide.region_7.8_spmd, body=%wide.region_2.0_spmd.sunk | while | flops 85834096 | bytes 59822800 | solution.py:76
  27.9 3.4 reduce-window.12
  31.3 0.1 copy.98
  31.5 1.1 reduce-window.13
  32.7 0.2 sqrt_bitcast_fusion.2
  32.9 3.9 tile.13
  36.8 9.1 %tile.14 = bf16[2,2,3,308224]{3,1,2,0:T(2,128)(2,1)} reshape(bf16[2,2,3,301,1024]{4,3,1,2,0:T(8,128)(2,1)} %tile.13) | data formatting | bytes 14794752 | tf_op jit(solution)/shard_map/while/body/eval_jaxpr/tile | solution.py:16
  46.0 7.4 %slice.48 = bf16[2,2,3,307500]{3,1,2,0:T(2,128)(2,1)} slice(bf16[2,2,3,308224]{3,1,2,0:T(2,128)(2,1)} %tile.14), slice={[0:2], [0:2], [0:3], [0:307500]} | slice | bytes 14760000 | tf_op jit(solution)/shard_map/while/body/eval_jaxpr/slice | solution.py:16
  53.4 21.2 %reshape.187 = bf16[2,2,3,300,1025]{4,3,1,2,0:T(8,128)(2,1)} reshape(bf16[2,2,3,307500]{3,1,2,0:T(2,128)(2,1)} %slice.48) | data formatting | bytes 14760000 | tf_op jit(solution)/shard_map/while/body/eval_jaxpr/reshape | solution.py:17
  74.6 0.1 fusion.46
  74.7 0.1 fusion.45
  74.9 3.5 fusion.47
  78.5 0.1 copy_dynamic-update-slice_fusion.2
  78.7 3.4 reduce-window.12
  82.2 0.1 copy.98
  82.4 1.1 reduce-window.13
  83.6 0.2 sqrt_bitcast_fusion.2
  83.8 3.9 tile.13
  87.7 9.1 %tile.14 = bf16[2,2,3,308224]{3,1,2,0:T(2,128)(2,1)} reshape(bf16[2,2,3,301,1024]{4,3,1,2,0:T(8,128)(2,1)} %tile.13) | data formatting | bytes 14794752 | tf_op jit(solution)/shard_map/while/body/eval_jaxpr/tile | solution.py:16
  96.9 7.4 %slice.48 = bf16[2,2,3,307500]{3,1,2,0:T(2,128)(2,1)} slice(bf16[2,2,3,308224]{3,1,2,0:T(2,128)(2,1)} %tile.14), slice={[0:2], [0:2], [0:3], [0:307500]} | slice | bytes 14760000 | tf_op jit(solution)/shard_map/while/body/eval_jaxpr/slice | solution.py:16
  104.3 21.2 %reshape.187 = bf16[2,2,3,300,1025]{4,3,1,2,0:T(8,128)(2,1)} reshape(bf16[2,2,3,307500]{3,1,2,0:T(2,128)(2,1)} %slice.48) | data formatting | bytes 14760000 | tf_op jit(solution)/shard_map/while/body/eval_jaxpr/reshape | solution.py:17
  125.5 0.1 fusion.46
  125.6 0.1 fusion.45
  125.7 3.5 fusion.47
  129.4 0.1 copy_dynamic-update-slice_fusion.2
  129.6 3.4 reduce-window.12
  133.1 0.1 copy.98
  133.2 1.1 reduce-window.13
  134.4 0.2 sqrt_bitcast_fusion.2
  134.6 3.9 tile.13
  138.6 9.1 %tile.14 = bf16[2,2,3,308224]{3,1,2,0:T(2,128)(2,1)} reshape(bf16[2,2,3,301,1024]{4,3,1,2,0:T(8,128)(2,1)} %tile.13) | data formatting | bytes 14794752 | tf_op jit(solution)/shard_map/while/body/eval_jaxpr/tile | solution.py:16
  147.7 7.4 %slice.48 = bf16[2,2,3,307500]{3,1,2,0:T(2,128)(2,1)} slice(bf16[2,2,3,308224]{3,1,2,0:T(2,128)(2,1)} %tile.14), slice={[0:2], [0:2], [0:3], [0:307500]} | slice | bytes 14760000 | tf_op jit(solution)/shard_map/while/body/eval_jaxpr/slice | solution.py:16
  155.2 21.2 %reshape.187 = bf16[2,2,3,300,1025]{4,3,1,2,0:T(8,128)(2,1)} reshape(bf16[2,2,3,307500]{3,1,2,0:T(2,128)(2,1)} %slice.48) | data formatting | bytes 14760000 | tf_op jit(solution)/shard_map/while/body/eval_jaxpr/reshape | solution.py:17
  176.4 0.1 fusion.46
  176.5 0.1 fusion.45
  176.6 3.5 fusion.47
  180.2 0.1 copy_dynamic-update-slice_fusion.2
  180.3 466.6 %gather_fusion = bf16[49152]{0:T(1024)(128)(2,1)S(1)} fusion(bf16[96,2,725]{2,1,0:T(2,128)(2,1)S(1)} %bitcast.76, s32[49152]{0:T(1024)S(1)} %bitcast.77), kind=kCustom, calls=%fused_computation | custom fusion | bytes 786432 | tf_op jit(solution)/shard_map/jit(take_along_axis)/gather | solution.py:22
  647.0 0.3 and_select_fusion
  647.3 0.1 broadcast_in_dim.22
  647.4 3.4 scatter_fusion
  650.8 0.7 copy.54
  651.5 3.4 all-to-all-start.1
  655.1 0.1 convert_reduce_fusion
  655.2 0.7 copy.61
  656.0 5.1 all-to-all-done.1
  661.1 0.8 fusion.28
  661.9 16.6 %reduce-scatter.7.cloned.1.call-done = f32[16,2]{1,0:T(8,128)} async-done(((f32[64,2]{1,0:T(8,128)}), f32[16,2]{1,0:T(8,128)}) %reduce-scatter.7.cloned.1.call-update) | async-done | bytes 144
  678.6 0.8 copy.62
  679.4 19.0 %reduce-scatter.5.cloned.1.call-done = f32[2,16,256]{2,1,0:T(8,128)} async-done(((f32[2,64,256]{2,1,0:T(8,128)}), f32[2,16,256]{2,1,0:T(8,128)}) %reduce-scatter.5.cloned.1.call-update) | async-done | bytes 32784 | tf_op jit(solution)/shard_map/reduce_scatter | solution.py:115
  698.3 1.4 multiply_divide_fusion
  (68 shorter events, 2.0 us)
Async XLA Ops:
  10.8 640.7 %all-to-all-start = ((s32[8,24,2]{1,2,0:T(2,128)}), s32[8,24,2]{1,2,0:T(2,128)S(1)}, u32[]{:S(2)}, u32[]{:S(2)}) async-start(s32[8,24,2]{1,2,0:T(2,128)} %broadcast_in_dim.21), calls=%async_computation | async-start | bytes 16384 | tf_op jit(solution)/shard_map/all_to_all | solution.py:100
  53.4 21.2 %copy-start = (bf16[3,2,16,3,300]{4,2,3,1,0:T(8,128)(2,1)S(1)}, bf16[3,2,16,3,300]{4,2,3,1,0:T(8,128)(2,1)}, u32[]{:S(2)}) copy-start(bf16[3,2,16,3,300]{4,2,3,1,0:T(8,128)(2,1)} %get-tuple-element.117) | copy-start | bytes 518404 | tf_op jit(solution)/shard_map/while
  104.3 21.2 %copy-start = (bf16[3,2,16,3,300]{4,2,3,1,0:T(8,128)(2,1)S(1)}, bf16[3,2,16,3,300]{4,2,3,1,0:T(8,128)(2,1)}, u32[]{:S(2)}) copy-start(bf16[3,2,16,3,300]{4,2,3,1,0:T(8,128)(2,1)} %get-tuple-element.117) | copy-start | bytes 518404 | tf_op jit(solution)/shard_map/while
  155.2 21.2 %copy-start = (bf16[3,2,16,3,300]{4,2,3,1,0:T(8,128)(2,1)S(1)}, bf16[3,2,16,3,300]{4,2,3,1,0:T(8,128)(2,1)}, u32[]{:S(2)}) copy-start(bf16[3,2,16,3,300]{4,2,3,1,0:T(8,128)(2,1)} %get-tuple-element.117) | copy-start | bytes 518404 | tf_op jit(solution)/shard_map/while
  651.5 9.6 %all-to-all-start.1 = ((bf16[8,24,2,256]{3,1,2,0:T(8,128)(2,1)}), bf16[8,24,2,256]{3,1,2,0:T(8,128)(2,1)S(1)}, u32[]{:S(2)}, u32[]{:S(2)}) async-start(bf16[8,24,2,256]{3,1,2,0:T(8,128)(2,1)} %copy.54), calls=%async_computation.1 | async-start | bytes 393216 | tf_op jit(solution)/shard_map/all_to_all | solution.py:99
  654.9 23.6 %reduce-scatter.7.cloned.1.call-start = ((), (), s32[]{:S(2)}) async-start(), calls=%async_computation.5 | async-start | bytes 40960
  655.9 42.4 %reduce-scatter.5.cloned.1.call-start = ((), (), s32[]{:S(2)}) async-start(), calls=%async_computation.4 | async-start | bytes 163840 | tf_op jit(solution)/shard_map/reduce_scatter | solution.py:115
Sparse Core Ops, SparseCore 0:
  658.0 20.5 reduce-scatter.6
  680.9 17.3 reduce-scatter.4
where the time goes:
time: 708 us; the launch traced here: 707 us
  local copies, waits for them, and re-layouts  603 us (85%)
  waiting for transfers between devices  40.8 us (6%)
  other arithmetic  19 us (3%)
  between operations  13.5 us (2%)
  matrix products  11.3 us (2%)
  blocking collectives  9.72 us (1%)
  starting transfers between devices  8.65 us (1%)
    gather x2, local copies, waits for them, and re-layouts, shift_rows(): return jnp.take_along_axis(values, lag_index, axis=-1)  467 us
    reshape x3, local copies, waits for them, and re-layouts, hankel(): tiled.reshape(series.shape[:-1] + (tap_count, width + 1))[..., :lag_count]  63.6 us
    another operation x6, local copies, waits for them, and re-layouts, hankel(): tiled = jnp.tile(series, repeats)[..., :tap_count * (width + 1)]  39.3 us
    slice x3, local copies, waits for them, and re-layouts, hankel(): tiled = jnp.tile(series, repeats)[..., :tap_count * (width + 1)]  22.3 us
    reduce_scatter x1, waiting for transfers between devices, body(): lax.psum_scatter(stack_sums, 'stn', scatter_dimension=1, tiled=True)  19 us
    unnamed x3, waiting for transfers between devices  16.7 us
  transfers between devices with their start and end apart: 4, of which 3 were waited for; matrix products, arithmetic and copies ran while one was open for 89% of the time, Pallas kernels for 0%

commit v1 on v0

v1 whole, which is shorter than its diff:
```python
import functools

import jax
import jax.numpy as jnp
from jax import lax
from jax.experimental import pallas as pl
from jax.experimental.pallas import tpu as pltpu
from jax.sharding import PartitionSpec as P

NK = 256
TPD = 16
LANES = 128
SHIFTS = 16

epsilon = 1e-06


def ceil_to(value, multiple):
    return -(-value // multiple) * multiple


def column_of(row):
    n = row.shape[1]
    eye = lax.broadcasted_iota(jnp.int32, (n, n), 0) == lax.broadcasted_iota(jnp.int32, (n, n), 1)
    return jnp.sum(jnp.where(eye, jnp.broadcast_to(row, (n, n)), 0), axis=1, keepdims=True)


def chunk_plan(taps, components):
    whole = taps // LANES
    tail = taps - whole * LANES
    per_tail = (LANES - 3) // tail
    return whole, tail, per_tail, ceil_to(components, per_tail) // per_tail


def pack_kernel(dims, with_data, *refs):
    ins = refs[: 5 if with_data else 4]
    send_ref = refs[len(ins)]
    held = refs[len(ins) + 1 : 2 * len(ins) + 1]
    sems = refs[-1]
    copies = [pltpu.make_async_copy(ins[i], held[i], sems.at[i]) for i in range(len(ins))]
    for copy in copies:
        copy.start()
    waves_ref, group_ref, local_ref, moveout_ref = held[-4:]
    n, stations, slots, components, taps, most, rows = dims
    count = stations * slots
    whole, tail, per_tail, tails = chunk_plan(taps, components)

    def flat(ref, three):
        pieces = [ref[s] if three else ref[s : s + 1, :] for s in range(stations)]
        return jnp.concatenate(pieces, axis=1)

    for copy in copies[-3:]:
        copy.wait()
    group = flat(group_ref, True)
    local = flat(local_ref, False)
    moveout = flat(moveout_ref, False)
    group_col = column_of(group)
    upper = lax.broadcasted_iota(jnp.int32, (count, count), 0)
    lower = lax.broadcasted_iota(jnp.int32, (count, count), 1)
    same = (upper // slots == lower // slots) & (upper < lower)
    rank = jnp.sum(jnp.where(same & (group_col == group), 1, 0), axis=0, keepdims=True)
    station = lax.broadcasted_iota(jnp.int32, (1, count), 1) // slots
    position = group * rows + station * most + rank
    place = lax.broadcasted_iota(jnp.int32, (n * rows, count), 0) == position
    place = jnp.where(place, 1.0, 0.0).astype(jnp.bfloat16)

    lane = lax.broadcasted_iota(jnp.int32, (count, LANES), 1)
    meta = jnp.where(lane == LANES - 1, column_of(local) + 1, 0)
    meta = jnp.where(lane == LANES - 2, column_of(moveout // LANES), meta)
    meta = jnp.where(lane == LANES - 3, column_of(moveout % LANES), meta)
    meta = meta.astype(jnp.float32).astype(jnp.bfloat16)

    for copy in copies[:-3]:
        copy.wait()
    waves = [
        jnp.concatenate([waves_ref[s * components + c] for s in range(stations)], axis=0)
        for c in range(components)
    ]
    placed = [
        jnp.dot(place, waves[c][:, : whole * LANES], preferred_element_type=jnp.float32)
        for c in range(components)
    ]
    ends = []
    for e in range(tails):
        pieces = [waves[c][:, whole * LANES :] for c in range(e * per_tail, min((e + 1) * per_tail, components))]
        used = tail * len(pieces)
        pieces.append(
            meta[:, used:] if e == 0 else jnp.zeros((count, LANES - used), jnp.bfloat16)
        )
        ends.append(jnp.concatenate(pieces, axis=1))
    ends = jnp.dot(place, jnp.concatenate(ends, axis=1), preferred_element_type=jnp.float32)
    if with_data:
        samples = held[0][...].astype(jnp.float32)
        samples = samples.reshape(samples.shape[0] * samples.shape[1], LANES)
        extra = send_ref.shape[1] - (components * whole + tails) * rows - samples.shape[0]
        samples = jnp.concatenate([samples, jnp.zeros((extra, LANES), jnp.float32)], axis=0)
    for g in range(n):
        mine = slice(g * rows, (g + 1) * rows)
        pieces = [
            placed[c][mine, a * LANES : (a + 1) * LANES] for c in range(components) for a in range(whole)
        ]
        pieces += [ends[mine, e * LANES : (e + 1) * LANES] for e in range(tails)]
        if with_data:
            pieces.append(samples)
        send_ref[g] = jnp.concatenate(pieces, axis=0).astype(jnp.bfloat16)


def correlate_kernel(dims, with_data, *refs):
    if with_data:
        recv_ref, mask_ref, *refs = refs
    else:
        recv_ref, data_ref, mask_ref, *refs = refs
    *out_refs, dsh_ref, rd_ref, ws_ref, rw_ref, meta_ref, sh_ref, stack_ref = refs
    n, stations, blocks, components, taps, most, rows, width, per_group = dims
    whole, tail, per_tail, tails = chunk_plan(taps, components)
    chunks = whole + 1
    sent = components * whole + tails
    total = n * rows
    here = n * most
    lag_tiles = ceil_to(width - taps + 1, LANES) // LANES
    lag_width = lag_tiles * LANES
    series = stations * components * blocks
    series_rows = ceil_to(series, 8)

    if with_data:
        first = sent * rows
        x = [recv_ref[i, first:, :].astype(jnp.float32)[:series_rows] for i in range(n)]
        x = jnp.concatenate(x, axis=1)
    else:
        x = data_ref[...].astype(jnp.float32)
        x = jnp.concatenate([x, jnp.zeros((series_rows - series, width), jnp.float32)], axis=0)
    for r in range(SHIFTS):
        moved = pltpu.roll(x, width - r, 1) if r else x
        for t in range(width // LANES):
            dsh_ref[t, r * series_rows : (r + 1) * series_rows, :] = moved[:, t * LANES : (t + 1) * LANES]

    def ahead(values, by):
        return pltpu.roll(values, width - by, 1)

    sums = {1: x * x}
    size = 1
    while 2 * size <= taps:
        sums[2 * size] = sums[size] + ahead(sums[size], size)
        size = 2 * size
    power = sums[size]
    start = size
    while start < taps:
        size = size // 2
        if taps - start >= size:
            power = power + ahead(sums[size], start)
            start += size
    scale = lax.rsqrt(power / taps + epsilon)
    row = lax.broadcasted_iota(jnp.int32, (series_rows, LANES), 0)
    factor = jnp.zeros((series_rows, LANES), jnp.float32)
    for s in range(stations):
        used = [mask_ref[s, c] for c in range(components)]
        total_used = jnp.maximum(functools.reduce(lambda p, q: p + q, used), 1)
        for c in range(components):
            at = (s * components + c) * blocks
            mine = (row >= at) & (row < at + blocks)
            value = jnp.full((series_rows, LANES), used[c]).astype(jnp.float32)
            value = value / jnp.full((series_rows, LANES), total_used).astype(jnp.float32)
            factor = jnp.where(mine, value, factor)
    for t in range(lag_tiles):
        rd_ref[:, t * LANES : (t + 1) * LANES] = scale[:, t * LANES : (t + 1) * LANES] * factor

    target = lax.broadcasted_iota(jnp.int32, (stations * here, total), 0)
    source = lax.broadcasted_iota(jnp.int32, (stations * here, total), 1)
    wanted = (target % here // most) * rows + (target // here) * most + target % most
    order = jnp.where(source == wanted, 1.0, 0.0).astype(jnp.bfloat16)
    lane = lax.broadcasted_iota(jnp.int32, (stations * here, LANES), 1)
    blocks_in = [recv_ref[i, : ceil_to(sent * rows, 16), :].astype(jnp.float32) for i in range(n)]

    def received(k):
        piece = jnp.concatenate([blocks_in[i][k * rows : (k + 1) * rows] for i in range(n)], axis=0)
        return jnp.dot(order, piece.astype(jnp.bfloat16), preferred_element_type=jnp.float32)

    ends = [received(components * whole + e) for e in range(tails)]
    meta_ref[...] = ends[0]
    for c in range(components):
        pieces = [received(c * whole + a) for a in range(whole)]
        end, before = ends[c // per_tail], (c % per_tail) * tail
        end = pltpu.roll(end, LANES - before, 1) if before else end
        pieces.append(jnp.where(lane < tail, end, 0.0))
        squares = functools.reduce(lambda p, q: p + q, [piece * piece for piece in pieces])
        for a in range(chunks):
            at = (c * chunks + a) * LANES
            ws_ref[:, at : at + LANES] = pieces[a].astype(jnp.bfloat16)
        wave_power = jnp.sum(squares, axis=1, keepdims=True) / taps
        rw_ref[:, c * LANES : (c + 1) * LANES] = jnp.broadcast_to(
            lax.rsqrt(wave_power + epsilon) / taps, (stations * here, LANES)
        )

    depth = (chunks - 1) * LANES + ceil_to(tail, 16)
    lane_here = lax.broadcasted_iota(jnp.int32, (here, LANES), 1)

    @pl.loop(0, stations)
    def _(s):
        rows_here = pl.ds(pl.multiple_of(s * here, here), here)
        meta = meta_ref[rows_here, :]
        tiles_over = meta[:, LANES - 2 : LANES - 1].astype(jnp.int32)
        lanes_over = meta[:, LANES - 3 : LANES - 2].astype(jnp.int32)
        index = lane_here + lanes_over
        within = index < LANES
        index = jnp.bitwise_and(index, LANES - 1)
        for b in range(blocks):
            total_corr = [jnp.zeros((here, LANES), jnp.float32) for _ in range(lag_tiles)]
            for c in range(components):
                at = (s * components + c) * blocks + b
                low = [
                    dsh_ref[t, pl.ds(at, SHIFTS, stride=series_rows), :] for t in range(width // LANES)
                ]
                low = jnp.concatenate(low, axis=1).astype(jnp.bfloat16)
                pieces = [low] + [pltpu.roll(low, width - q, 1) for q in range(SHIFTS, LANES, SHIFTS)]
                shifted = jnp.concatenate(pieces, axis=0)
                hankel = jnp.concatenate(
                    [
                        shifted[: min(LANES, depth - a * LANES), a * LANES : a * LANES + lag_width]
                        for a in range(chunks)
                    ],
                    axis=0,
                )
                w = ws_ref[rows_here, c * chunks * LANES : c * chunks * LANES + depth]
                numerator = jnp.dot(w, hankel, preferred_element_type=jnp.float32)
                over_wave = rw_ref[rows_here, c * LANES : (c + 1) * LANES]
                over_data = rd_ref[pl.ds(at, 1), :]
                for t in range(lag_tiles):
                    cut = slice(t * LANES, (t + 1) * LANES)
                    total_corr[t] = total_corr[t] + numerator[:, cut] * over_wave * over_data[:, cut]
            windows = []
            for t in range(NK // LANES + 1):
                window = total_corr[t]
                for h in range(1, lag_tiles - NK // LANES):
                    if t + h < lag_tiles:
                        window = jnp.where(tiles_over == h, total_corr[t + h], window)
                windows.append(jnp.take_along_axis(window, index, axis=1))
            for t in range(NK // LANES):
                aligned = jnp.where(within, windows[t], windows[t + 1])
                at = b * NK + t * LANES
                sh_ref[rows_here, at : at + LANES] = aligned.astype(jnp.bfloat16)

    slot = lax.broadcasted_iota(jnp.int32, (stations * here, LANES), 0)
    half = (slot < stations * here // 2) == (lane < LANES // 2)
    sh_ref[:, blocks * NK :] = jnp.where(half, 1.0, 0.0).astype(jnp.bfloat16)
    local = meta_ref[:, LANES - 1 :].astype(jnp.int32) - 1
    template = lax.broadcasted_iota(jnp.int32, (stations * here, per_group), 1)
    onehot = jnp.where(local == template, 1.0, 0.0).astype(jnp.bfloat16)
    stack_ref[...] = lax.dot_general(
        onehot, sh_ref[...], (((0,), (0,)), ((), ())), preferred_element_type=jnp.float32
    )
    me = lax.axis_index("stn")
    for d, out_ref in enumerate(out_refs):
        owner = lax.rem(me + d, len(out_refs))
        theirs = pl.ds(pl.multiple_of(owner * TPD, TPD), TPD)
        out_ref[...] = stack_ref[theirs, :].astype(jnp.bfloat16)


def finish_kernel(taps, blocks, *refs):
    *parts_refs, out_ref = refs
    total = functools.reduce(lambda p, q: p + q, [ref[...].astype(jnp.float32) for ref in parts_refs])
    first, middle = blocks * NK, blocks * NK + LANES // 2
    count = total[:, first : first + 1] + total[:, middle : middle + 1]
    scale = jnp.sqrt(jnp.float32(taps)) / jnp.sqrt(jnp.maximum(count, 1.0))
    for b in range(blocks):
        out_ref[b] = total[:, b * NK : (b + 1) * NK] * scale


def body(data, waves, slot_group, slot_local, moveout, chan_mask):
    blocks, stations, components, width_here = data.shape
    slots, taps = waves.shape[1], waves.shape[3]
    n = lax.axis_size("tmpl")
    owners = lax.axis_size("stn")
    per_group = TPD * owners
    width = width_here * n
    most = max(2, 2 * slots // n)
    rows = ceil_to(stations * most, 8)
    whole, tail, per_tail, tails = chunk_plan(taps, components)
    series = stations * components * blocks
    series_rows = ceil_to(series, 8)
    with_data = width_here == LANES
    here = n * most

    waves = jnp.transpose(waves, (0, 2, 1, 3)).reshape(stations * components, slots, taps)
    groups = jnp.transpose(slot_group, (0, 2, 1))
    samples = jnp.transpose(data, (1, 2, 0, 3)).reshape(stations * components, blocks, width_here)
    block_rows = (components * whole + tails) * rows + (series_rows if with_data else 0)
    block_rows = ceil_to(block_rows, 16)
    ins = ([samples] if with_data else []) + [waves, groups, slot_local, moveout]
    send = pl.pallas_call(
        functools.partial(
            pack_kernel, (n, stations, slots, components, taps, most, rows), with_data
        ),
        out_shape=jax.ShapeDtypeStruct((n, block_rows, LANES), jnp.bfloat16),
        in_specs=[pl.BlockSpec(memory_space=pltpu.HBM)] * len(ins),
        scratch_shapes=[pltpu.VMEM(x.shape, x.dtype) for x in ins]
        + [pltpu.SemaphoreType.DMA((len(ins),))],
        compiler_params=pltpu.CompilerParams(vmem_limit_bytes=60 << 20),
        name="pack",
    )(*ins)
    received = lax.all_to_all(send, "tmpl", split_axis=0, concat_axis=0, tiled=True)
    if not with_data:
        samples = lax.all_gather(samples.reshape(series, width_here), "tmpl", axis=1, tiled=True)
    vmem = pl.BlockSpec(memory_space=pltpu.VMEM)
    partial_stacks = pl.pallas_call(
        functools.partial(
            correlate_kernel,
            (n, stations, blocks, components, taps, most, rows, width, per_group),
            with_data,
        ),
        out_shape=[jax.ShapeDtypeStruct((TPD, blocks * NK + LANES), jnp.bfloat16)] * owners,
        in_specs=[vmem] * (1 if with_data else 2) + [pl.BlockSpec(memory_space=pltpu.SMEM)],
        scratch_shapes=[
            pltpu.VMEM((width // LANES, SHIFTS * series_rows, LANES), jnp.float32),
            pltpu.VMEM((series_rows, ceil_to(width - taps + 1, LANES)), jnp.float32),
            pltpu.VMEM((stations * here, components * (whole + 1) * LANES), jnp.bfloat16),
            pltpu.VMEM((stations * here, components * LANES), jnp.float32),
            pltpu.VMEM((stations * here, LANES), jnp.float32),
            pltpu.VMEM((stations * here, blocks * NK + LANES), jnp.bfloat16),
            pltpu.VMEM((per_group, blocks * NK + LANES), jnp.float32),
        ],
        compiler_params=pltpu.CompilerParams(vmem_limit_bytes=40 << 20),
        name="correlate",
    )(received, *([] if with_data else [samples]), chan_mask)
    parts = [partial_stacks[0]]
    for d in range(1, owners):
        step = [(i, (i + d) % owners) for i in range(owners)]
        parts.append(lax.ppermute(partial_stacks[d], "stn", step))
    return pl.pallas_call(
        functools.partial(finish_kernel, taps, blocks),
        out_shape=jax.ShapeDtypeStruct((blocks, TPD, NK), jnp.float32),
        name="finish",
    )(*parts)


def solution(mesh):
    in_specs = (
        P(None, "stn", None, "tmpl"),
        P("stn", "tmpl", None, None),
        P("stn", "tmpl", None),
        P("stn", "tmpl"),
        P("stn", "tmpl"),
        P("stn", None),
    )
    out_specs = P(None, ("tmpl", "stn"), None)
    return jax.shard_map(body, mesh=mesh, in_specs=in_specs, out_specs=out_specs, check_vma=False)
```

time: 708 us -> 34.6 us (0.05)
  local copies, waits for them, and re-layouts: 603 us -> 1.3 us
  waiting for transfers between devices: 40.8 us -> 11.7 us
  other arithmetic: 19 us -> 0 us
  between operations: 13.5 us -> 0.04 us
  matrix products: 11.3 us -> 0 us
  Pallas kernels: 0 us -> 10.6 us
  blocking collectives: 9.72 us -> 0 us
    gather x2 -> x0, local copies, waits for them, and re-layouts: 467 us -> none  [shift_rows(): return jnp.take_along_axis(values, lag_index, axis=-1)]
    reshape x6 -> x0, local copies, waits for them, and re-layouts: 65.2 us -> none  [the longest x3 63.6 us: hankel(): tiled.reshape(series.shape[:-1] + (tap_count, width + 1))[..., :lag_count]]
    another operation x16 -> x0, local copies, waits for them, and re-layouts: 40.1 us -> none  [the longest x6 39.3 us: hankel(): tiled = jnp.tile(series, repeats)[..., :tap_count * (width + 1)]]
    slice x9 -> x0, local copies, waits for them, and re-layouts: 23 us -> none  [the longest x3 22.3 us: hankel(): tiled = jnp.tile(series, repeats)[..., :tap_count * (width + 1)]]
    reduce_scatter x1 -> x0, waiting for transfers between devices: 19 us -> none  [body(): lax.psum_scatter(stack_sums, 'stn', scatter_dimension=1, tiled=True)]
    unnamed x3 -> x0, waiting for transfers between devices: 16.7 us -> none
    another operation x9 -> x0, other arithmetic: 13.6 us -> none
    dot_general x4 -> x0, matrix products: 11.3 us -> none  [the longest x3 10.5 us: correlate(): jnp.einsum('spcj,bscjk->spbck', station_waves, hankel_rows, preferred_ele...]
  transfers between devices with their start and end apart: 4 -> 4, of which waited for: 3 -> 4; matrix products, arithmetic and copies ran while one was open for 89% -> 0% of each run, Pallas kernels for 0% -> 0%
where the time goes in v1:
time: 34.6 us; the launch traced here: 34.4 us
  waiting for transfers between devices  11.7 us (34%)
  starting transfers between devices  10.7 us (31%)
  Pallas kernels  10.6 us (31%)
  local copies, waits for them, and re-layouts  1.3 us (4%)
    all_to_all x1, waiting for transfers between devices, body(): lax.all_to_all(send, 'tmpl', split_axis=0, concat_axis=0, tiled=True)  9.29 us
    pallas_call x1, Pallas kernels, body(): pl.pallas_call(functools.partial(correlate_kernel, (n, stations, blocks,...  6.85 us
    ppermute x3, starting transfers between devices, body(): parts.append(lax.ppermute(partial_stacks[d], 'stn', step))  5.52 us
    all_to_all x1, starting transfers between devices, body(): lax.all_to_all(send, 'tmpl', split_axis=0, concat_axis=0, tiled=True)  5.18 us
    ppermute x3, waiting for transfers between devices, body(): parts.append(lax.ppermute(partial_stacks[d], 'stn', step))  2.43 us
    pallas_call x1, Pallas kernels, body(): pl.pallas_call(functools.partial(pack_kernel, (n, stations, slots, compon...  2.2 us
    pallas_call x1, Pallas kernels, body(): pl.pallas_call(functools.partial(finish_kernel, taps, blocks), out_shape=...  1.55 us
    unnamed x11, local copies, waits for them, and re-layouts  1.3 us
  transfers between devices with their start and end apart: 4, of which 4 were waited for; matrix products, arithmetic and copies ran while one was open for 0% of the time, Pallas kernels for 0%

profile of v1, /device:TPU:0, one launch (start us, length us, event | category | flops | bytes accessed | tf_op | source)
XLA Modules:
  0.0 34.4 jit_solution(16605908520953684722)
XLA Ops:
  0.0 2.2 %pack.1 = bf16[8,240,128]{2,1,0:T(8,128)(2,1)} custom-call(bf16[18,2,128]{2,1,0:T(2,128)(2,1)} %bitcast.8, bf16[18,16,300]{2,1,0:T(8,128)(2,1)} %bitcast.7, s32[6,1,16]{2,1,0:T(1,128)} %bitcast.9, s32[6,16]{1,0:T(8,128)} %refs_3_.1, s32[6,16]{1,0:T(8,128)} %refs_4_.1), custom_call_target="tpu_custom_call" | custom-call | tf_op jit(solution)/shard_map/pack/pallas_call | solution.py:289
  2.2 0.0 copy-start.4
  2.2 5.2 %all-to-all-start = ((bf16[8,240,128]{2,1,0:T(8,128)(2,1)}), bf16[8,240,128]{2,1,0:T(8,128)(2,1)S(1)}, u32[]{:S(2)}, u32[]{:S(2)}) async-start(bf16[8,240,128]{2,1,0:T(8,128)(2,1)} %pack.1), calls=%async_computation | async-start | bytes 983040 | tf_op jit(solution)/shard_map/all_to_all | solution.py:300
  7.4 0.0 copy-done.4
  7.4 0.1 copy.7.refs_1_
  7.5 9.3 %all-to-all-done.refs_0_ = bf16[8,240,128]{2,1,0:T(8,128)(2,1)S(1)} async-done(((bf16[8,240,128]{2,1,0:T(8,128)(2,1)}), bf16[8,240,128]{2,1,0:T(8,128)(2,1)S(1)}, u32[]{:S(2)}, u32[]{:S(2)}) %all-to-all-start) | async-done | bytes 491552 | tf_op jit(solution)/shard_map/all_to_all | solution.py:300
  16.8 6.8 %correlate.1 = (bf16[16,640]{1,0:T(8,128)(2,1)S(1)}, bf16[16,640]{1,0:T(8,128)(2,1)S(1)}, bf16[16,640]{1,0:T(8,128)(2,1)S(1)}, bf16[16,640]{1,0:T(8,128)(2,1)S(1)}) custom-call(bf16[8,240,128]{2,1,0:T(8,128)(2,1)S(1)} %all-to-all-done.refs_0_, s32[6,3]{1,0:T(8,128)S(1)} %copy.7.refs_1_), custom_call_target="tpu_custom_call" | custom-call | tf_op jit(solution)/shard_map/correlate/pallas_call | solution.py:304
  23.6 0.0 copy-start
  23.7 0.6 %copy-done = bf16[16,640]{1,0:T(8,128)(2,1)} copy-done((bf16[16,640]{1,0:T(8,128)(2,1)}, bf16[16,640]{1,0:T(8,128)(2,1)S(1)}, u32[]{:S(2)}) %copy-start) | copy-done | bytes 20504
  24.3 1.6 %collective-permute-start = (bf16[16,640]{1,0:T(8,128)(2,1)S(1)}, bf16[16,640]{1,0:T(8,128)(2,1)S(1)}, u32[]{:S(2)}, u32[]{:S(2)}) collective-permute-start(bf16[16,640]{1,0:T(8,128)(2,1)S(1)} %get-tuple-element.10), channel_id=1, source_target_pairs={{0,1},{1,2},{2,3},{3,0},{4,5},{5,6},{6,7},{7,4},{8,9},{9,10},{10,1... | collective-permute-start | bytes 61448 | tf_op jit(solution)/shard_map/ppermute | solution.py:327
  25.8 2.6 %collective-permute-start.1 = (bf16[16,640]{1,0:T(8,128)(2,1)S(1)}, bf16[16,640]{1,0:T(8,128)(2,1)S(1)}, u32[]{:S(2)}, u32[]{:S(2)}) collective-permute-start(bf16[16,640]{1,0:T(8,128)(2,1)S(1)} %get-tuple-element.11), channel_id=1, source_target_pairs={{0,2},{1,3},{2,0},{3,1},{4,6},{5,7},{6,4},{7,5},{8,10},{9,11},{10,... | collective-permute-start | bytes 61448 | tf_op jit(solution)/shard_map/ppermute | solution.py:327
  28.4 1.3 %collective-permute-start.2 = (bf16[16,640]{1,0:T(8,128)(2,1)S(1)}, bf16[16,640]{1,0:T(8,128)(2,1)S(1)}, u32[]{:S(2)}, u32[]{:S(2)}) collective-permute-start(bf16[16,640]{1,0:T(8,128)(2,1)S(1)} %get-tuple-element.12), channel_id=1, source_target_pairs={{0,3},{1,0},{2,1},{3,2},{4,7},{5,4},{6,5},{7,6},{8,11},{9,8},{10,9... | collective-permute-start | bytes 61448 | tf_op jit(solution)/shard_map/ppermute | solution.py:327
  29.8 0.1 collective-permute-done.refs_1_
  29.8 0.0 copy-start.1
  29.8 0.7 %collective-permute-done.1.refs_2_ = bf16[16,640]{1,0:T(8,128)(2,1)S(1)} collective-permute-done((bf16[16,640]{1,0:T(8,128)(2,1)S(1)}, bf16[16,640]{1,0:T(8,128)(2,1)S(1)}, u32[]{:S(2)}, u32[]{:S(2)}) %collective-permute-start.1) | collective-permute-done | bytes 20512 | tf_op jit(solution)/shard_map/ppermute | solution.py:327
  30.5 0.0 copy-start.2
  30.5 1.7 %collective-permute-done.2.refs_3_ = bf16[16,640]{1,0:T(8,128)(2,1)S(1)} collective-permute-done((bf16[16,640]{1,0:T(8,128)(2,1)S(1)}, bf16[16,640]{1,0:T(8,128)(2,1)S(1)}, u32[]{:S(2)}, u32[]{:S(2)}) %collective-permute-start.2) | collective-permute-done | bytes 20512 | tf_op jit(solution)/shard_map/ppermute | solution.py:327
  32.2 0.0 copy-start.3
  32.2 0.0 copy-done.1
  32.2 0.0 copy-done.2
  32.2 0.6 %copy-done.3 = bf16[16,640]{1,0:T(8,128)(2,1)} copy-done((bf16[16,640]{1,0:T(8,128)(2,1)}, bf16[16,640]{1,0:T(8,128)(2,1)S(1)}, u32[]{:S(2)}) %copy-start.3) | copy-done | bytes 20504
  32.8 1.6 %finish.1 = f32[2,16,256]{2,1,0:T(8,128)} custom-call(bf16[16,640]{1,0:T(8,128)(2,1)} %copy-done, bf16[16,640]{1,0:T(8,128)(2,1)} %copy-done.1, bf16[16,640]{1,0:T(8,128)(2,1)} %copy-done.2, bf16[16,640]{1,0:T(8,128)(2,1)} %copy-done.3), custom_call_target="tpu_custom_call" | custom-call | tf_op jit(solution)/shard_map/finish/pallas_call | solution.py:328
Async XLA Ops:
  2.2 5.2 %copy-start.4 = (s32[6,3]{0,1:T(4,128)S(1)}, s32[6,3]{0,1:T(4,128)}, u32[]{:S(2)}) copy-start(s32[6,3]{0,1:T(4,128)} %param.11) | copy-start | bytes 220
  2.2 14.6 %all-to-all-start = ((bf16[8,240,128]{2,1,0:T(8,128)(2,1)}), bf16[8,240,128]{2,1,0:T(8,128)(2,1)S(1)}, u32[]{:S(2)}, u32[]{:S(2)}) async-start(bf16[8,240,128]{2,1,0:T(8,128)(2,1)} %pack.1), calls=%async_computation | async-start | bytes 983040 | tf_op jit(solution)/shard_map/all_to_all | solution.py:300
  23.6 0.6 %copy-start = (bf16[16,640]{1,0:T(8,128)(2,1)}, bf16[16,640]{1,0:T(8,128)(2,1)S(1)}, u32[]{:S(2)}) copy-start(bf16[16,640]{1,0:T(8,128)(2,1)S(1)} %get-tuple-element.9.refs_0_) | copy-start | bytes 61444
  24.3 5.6 %collective-permute-start = (bf16[16,640]{1,0:T(8,128)(2,1)S(1)}, bf16[16,640]{1,0:T(8,128)(2,1)S(1)}, u32[]{:S(2)}, u32[]{:S(2)}) collective-permute-start(bf16[16,640]{1,0:T(8,128)(2,1)S(1)} %get-tuple-element.10), channel_id=1, source_target_pairs={{0,1},{1,2},{2,3},{3,0},{4,5},{5,6},{6,7},{7,4},{8,9},{9,10},{10,1... | collective-permute-start | bytes 61448 | tf_op jit(solution)/shard_map/ppermute | solution.py:327
  25.8 4.7 %collective-permute-start.1 = (bf16[16,640]{1,0:T(8,128)(2,1)S(1)}, bf16[16,640]{1,0:T(8,128)(2,1)S(1)}, u32[]{:S(2)}, u32[]{:S(2)}) collective-permute-start(bf16[16,640]{1,0:T(8,128)(2,1)S(1)} %get-tuple-element.11), channel_id=1, source_target_pairs={{0,2},{1,3},{2,0},{3,1},{4,6},{5,7},{6,4},{7,5},{8,10},{9,11},{10,... | collective-permute-start | bytes 61448 | tf_op jit(solution)/shard_map/ppermute | solution.py:327
  28.4 3.8 %collective-permute-start.2 = (bf16[16,640]{1,0:T(8,128)(2,1)S(1)}, bf16[16,640]{1,0:T(8,128)(2,1)S(1)}, u32[]{:S(2)}, u32[]{:S(2)}) collective-permute-start(bf16[16,640]{1,0:T(8,128)(2,1)S(1)} %get-tuple-element.12), channel_id=1, source_target_pairs={{0,3},{1,0},{2,1},{3,2},{4,7},{5,4},{6,5},{7,6},{8,11},{9,8},{10,9... | collective-permute-start | bytes 61448 | tf_op jit(solution)/shard_map/ppermute | solution.py:327
  29.8 2.4 %copy-start.1 = (bf16[16,640]{1,0:T(8,128)(2,1)}, bf16[16,640]{1,0:T(8,128)(2,1)S(1)}, u32[]{:S(2)}) copy-start(bf16[16,640]{1,0:T(8,128)(2,1)S(1)} %collective-permute-done.refs_1_) | copy-start | bytes 61444
  30.5 1.7 %copy-start.2 = (bf16[16,640]{1,0:T(8,128)(2,1)}, bf16[16,640]{1,0:T(8,128)(2,1)S(1)}, u32[]{:S(2)}) copy-start(bf16[16,640]{1,0:T(8,128)(2,1)S(1)} %collective-permute-done.1.refs_2_) | copy-start | bytes 61444
  32.2 0.6 %copy-start.3 = (bf16[16,640]{1,0:T(8,128)(2,1)}, bf16[16,640]{1,0:T(8,128)(2,1)S(1)}, u32[]{:S(2)}) copy-start(bf16[16,640]{1,0:T(8,128)(2,1)S(1)} %collective-permute-done.2.refs_3_) | copy-start | bytes 61444

commit v2 on v1

--- a/solution.py
+++ b/solution.py
@@ -33,15 +33,15 @@
 
 
 def pack_kernel(dims, with_data, *refs):
+    n, stations, slots, components, taps, most, rows = dims
     ins = refs[: 5 if with_data else 4]
-    send_ref = refs[len(ins)]
-    held = refs[len(ins) + 1 : 2 * len(ins) + 1]
+    send_refs = refs[len(ins) : len(ins) + n]
+    held = refs[len(ins) + n : -1]
     sems = refs[-1]
     copies = [pltpu.make_async_copy(ins[i], held[i], sems.at[i]) for i in range(len(ins))]
     for copy in copies:
         copy.start()
     waves_ref, group_ref, local_ref, moveout_ref = held[-4:]
-    n, stations, slots, components, taps, most, rows = dims
     count = stations * slots
     whole, tail, per_tail, tails = chunk_plan(taps, components)
 
@@ -60,7 +60,8 @@
     same = (upper // slots == lower // slots) & (upper < lower)
     rank = jnp.sum(jnp.where(same & (group_col == group), 1, 0), axis=0, keepdims=True)
     station = lax.broadcasted_iota(jnp.int32, (1, count), 1) // slots
-    position = group * rows + station * most + rank
+    partner = group ^ lax.axis_index("tmpl")
+    position = partner * rows + station * most + rank
     place = lax.broadcasted_iota(jnp.int32, (n * rows, count), 0) == position
     place = jnp.where(place, 1.0, 0.0).astype(jnp.bfloat16)
 
@@ -92,7 +93,7 @@
     if with_data:
         samples = held[0][...].astype(jnp.float32)
         samples = samples.reshape(samples.shape[0] * samples.shape[1], LANES)
-        extra = send_ref.shape[1] - (components * whole + tails) * rows - samples.shape[0]
+        extra = send_refs[0].shape[0] - (components * whole + tails) * rows - samples.shape[0]
         samples = jnp.concatenate([samples, jnp.zeros((extra, LANES), jnp.float32)], axis=0)
     for g in range(n):
         mine = slice(g * rows, (g + 1) * rows)
@@ -102,30 +103,31 @@
         pieces += [ends[mine, e * LANES : (e + 1) * LANES] for e in range(tails)]
         if with_data:
             pieces.append(samples)
-        send_ref[g] = jnp.concatenate(pieces, axis=0).astype(jnp.bfloat16)
+        send_refs[g][...] = jnp.concatenate(pieces, axis=0).astype(jnp.bfloat16)
 
 
 def correlate_kernel(dims, with_data, *refs):
     if with_data:
-        recv_ref, mask_ref, *refs = refs
+        mask_ref, *refs = refs
     else:
-        recv_ref, data_ref, mask_ref, *refs = refs
-    *out_refs, dsh_ref, rd_ref, ws_ref, rw_ref, meta_ref, sh_ref, stack_ref = refs
+        data_ref, mask_ref, *refs = refs
     n, stations, blocks, components, taps, most, rows, width, per_group = dims
+    recv_refs, refs = refs[:n], refs[n:]
+    *out_refs, x_ref, dsh_ref, rd_ref, ws_ref, rw_ref, meta_ref, sh_ref, stack_ref = refs
     whole, tail, per_tail, tails = chunk_plan(taps, components)
     chunks = whole + 1
     sent = components * whole + tails
     total = n * rows
     here = n * most
     lag_tiles = ceil_to(width - taps + 1, LANES) // LANES
-    lag_width = lag_tiles * LANES
     series = stations * components * blocks
     series_rows = ceil_to(series, 8)
 
     if with_data:
         first = sent * rows
-        x = [recv_ref[i, first:, :].astype(jnp.float32)[:series_rows] for i in range(n)]
-        x = jnp.concatenate(x, axis=1)
+        for i in range(n):
+            x_ref[lax.axis_index("tmpl") ^ i] = recv_refs[i][first:, :].astype(jnp.float32)[:series_rows]
+        x = jnp.concatenate([x_ref[i] for i in range(n)], axis=1)
     else:
         x = data_ref[...].astype(jnp.float32)
         x = jnp.concatenate([x, jnp.zeros((series_rows - series, width), jnp.float32)], axis=0)
@@ -169,7 +171,7 @@
     wanted = (target % here // most) * rows + (target // here) * most + target % most
     order = jnp.where(source == wanted, 1.0, 0.0).astype(jnp.bfloat16)
     lane = lax.broadcasted_iota(jnp.int32, (stations * here, LANES), 1)
-    blocks_in = [recv_ref[i, : ceil_to(sent * rows, 16), :].astype(jnp.float32) for i in range(n)]
+    blocks_in = [ref[: ceil_to(sent * rows, 16), :].astype(jnp.float32) for ref in recv_refs]
 
     def received(k):
         piece = jnp.concatenate([blocks_in[i][k * rows : (k + 1) * rows] for i in range(n)], axis=0)
@@ -184,19 +186,18 @@
         pieces.append(jnp.where(lane < tail, end, 0.0))
         squares = functools.reduce(lambda p, q: p + q, [piece * piece for piece in pieces])
         for a in range(chunks):
-            at = (c * chunks + a) * LANES
-            ws_ref[:, at : at + LANES] = pieces[a].astype(jnp.bfloat16)
+            for s in range(stations):
+                at = ((s * components + c) * chunks + a) * here
+                ws_ref[at : at + here, :] = pieces[a][s * here : (s + 1) * here].astype(jnp.bfloat16)
         wave_power = jnp.sum(squares, axis=1, keepdims=True) / taps
         rw_ref[:, c * LANES : (c + 1) * LANES] = jnp.broadcast_to(
             lax.rsqrt(wave_power + epsilon) / taps, (stations * here, LANES)
         )
 
-    depth = (chunks - 1) * LANES + ceil_to(tail, 16)
     lane_here = lax.broadcasted_iota(jnp.int32, (here, LANES), 1)
 
-    @pl.loop(0, stations)
-    def _(s):
-        rows_here = pl.ds(pl.multiple_of(s * here, here), here)
+    for s in range(stations):
+        rows_here = slice(s * here, (s + 1) * here)
         meta = meta_ref[rows_here, :]
         tiles_over = meta[:, LANES - 2 : LANES - 1].astype(jnp.int32)
         lanes_over = meta[:, LANES - 3 : LANES - 2].astype(jnp.int32)
@@ -213,20 +214,19 @@
                 low = jnp.concatenate(low, axis=1).astype(jnp.bfloat16)
                 pieces = [low] + [pltpu.roll(low, width - q, 1) for q in range(SHIFTS, LANES, SHIFTS)]
                 shifted = jnp.concatenate(pieces, axis=0)
-                hankel = jnp.concatenate(
-                    [
-                        shifted[: min(LANES, depth - a * LANES), a * LANES : a * LANES + lag_width]
+                first = (s * components + c) * chunks * here
+                w = ws_ref[first : first + chunks * here, :]
+                numerator = jnp.dot(w, shifted, preferred_element_type=jnp.float32)
+                over_wave = rw_ref[rows_here, c * LANES : (c + 1) * LANES]
+                over_data = rd_ref[at : at + 1, :]
+                for t in range(lag_tiles):
+                    pieces = [
+                        numerator[a * here : (a + 1) * here, (t + a) * LANES : (t + a + 1) * LANES]
                         for a in range(chunks)
-                    ],
-                    axis=0,
-                )
-                w = ws_ref[rows_here, c * chunks * LANES : c * chunks * LANES + depth]
-                numerator = jnp.dot(w, hankel, preferred_element_type=jnp.float32)
-                over_wave = rw_ref[rows_here, c * LANES : (c + 1) * LANES]
-                over_data = rd_ref[pl.ds(at, 1), :]
-                for t in range(lag_tiles):
-                    cut = slice(t * LANES, (t + 1) * LANES)
-                    total_corr[t] = total_corr[t] + numerator[:, cut] * over_wave * over_data[:, cut]
+                    ]
+                    summed = functools.reduce(lambda p, q: p + q, pieces)
+                    over = over_data[:, t * LANES : (t + 1) * LANES]
+                    total_corr[t] = total_corr[t] + summed * over_wave * over
             windows = []
             for t in range(NK // LANES + 1):
                 window = total_corr[t]
@@ -290,14 +290,16 @@
         functools.partial(
             pack_kernel, (n, stations, slots, components, taps, most, rows), with_data
         ),
-        out_shape=jax.ShapeDtypeStruct((n, block_rows, LANES), jnp.bfloat16),
+        out_shape=[jax.ShapeDtypeStruct((block_rows, LANES), jnp.bfloat16)] * n,
         in_specs=[pl.BlockSpec(memory_space=pltpu.HBM)] * len(ins),
         scratch_shapes=[pltpu.VMEM(x.shape, x.dtype) for x in ins]
         + [pltpu.SemaphoreType.DMA((len(ins),))],
         compiler_params=pltpu.CompilerParams(vmem_limit_bytes=60 << 20),
         name="pack",
     )(*ins)
-    received = lax.all_to_all(send, "tmpl", split_axis=0, concat_axis=0, tiled=True)
+    received = [send[0]] + [None] * (n - 1)
+    for d in range(n - 1, 0, -1):
+        received[d] = lax.ppermute(send[d], "tmpl", [(i, i ^ d) for i in range(n)])
     if not with_data:
         samples = lax.all_gather(samples.reshape(series, width_here), "tmpl", axis=1, tiled=True)
     vmem = pl.BlockSpec(memory_space=pltpu.VMEM)
@@ -308,11 +310,12 @@
             with_data,
         ),
         out_shape=[jax.ShapeDtypeStruct((TPD, blocks * NK + LANES), jnp.bfloat16)] * owners,
-        in_specs=[vmem] * (1 if with_data else 2) + [pl.BlockSpec(memory_space=pltpu.SMEM)],
+        in_specs=[vmem] * (0 if with_data else 1) + [pl.BlockSpec(memory_space=pltpu.SMEM)] + [vmem] * n,
         scratch_shapes=[
+            pltpu.VMEM((width // LANES, series_rows, LANES), jnp.float32),
             pltpu.VMEM((width // LANES, SHIFTS * series_rows, LANES), jnp.float32),
             pltpu.VMEM((series_rows, ceil_to(width - taps + 1, LANES)), jnp.float32),
-            pltpu.VMEM((stations * here, components * (whole + 1) * LANES), jnp.bfloat16),
+            pltpu.VMEM((stations * components * (whole + 1) * here, LANES), jnp.bfloat16),
             pltpu.VMEM((stations * here, components * LANES), jnp.float32),
             pltpu.VMEM((stations * here, LANES), jnp.float32),
             pltpu.VMEM((stations * here, blocks * NK + LANES), jnp.bfloat16),
@@ -320,7 +323,7 @@
         ],
         compiler_params=pltpu.CompilerParams(vmem_limit_bytes=40 << 20),
         name="correlate",
-    )(received, *([] if with_data else [samples]), chan_mask)
+    )(*([] if with_data else [samples]), chan_mask, *received)
     parts = [partial_stacks[0]]
     for d in range(1, owners):
         step = [(i, (i + d) % owners) for i in range(owners)]
@@ -328,6 +331,7 @@
     return pl.pallas_call(
         functools.partial(finish_kernel, taps, blocks),
         out_shape=jax.ShapeDtypeStruct((blocks, TPD, NK), jnp.float32),
+        compiler_params=pltpu.CompilerParams(vmem_limit_bytes=4 << 20),
         name="finish",
     )(*parts)
 

time: 34.6 us -> 31.9 us (0.922)
  waiting for transfers between devices: 11.7 us -> 7.16 us
  starting transfers between devices: 10.7 us -> 13.4 us
  Pallas kernels: 10.6 us -> 10.1 us
  local copies, waits for them, and re-layouts: 1.3 us -> 0.92 us
    all_to_all x1 -> x0, waiting for transfers between devices: 9.29 us -> none  [body(): lax.all_to_all(send, 'tmpl', split_axis=0, concat_axis=0, tiled=True)]
    ppermute x0 -> x7, starting transfers between devices: none -> 7.86 us  [body(): received[d] = lax.ppermute(send[d], 'tmpl', [(i, i ^ d) for i in range(n)])]
    all_to_all x1 -> x0, starting transfers between devices: 5.18 us -> none  [body(): lax.all_to_all(send, 'tmpl', split_axis=0, concat_axis=0, tiled=True)]
    ppermute x0 -> x7, waiting for transfers between devices: none -> 4.74 us  [body(): received[d] = lax.ppermute(send[d], 'tmpl', [(i, i ^ d) for i in range(n)])]
    pallas_call x1, Pallas kernels: 1.55 us -> 0.78 us  [body(): pl.pallas_call(functools.partial(finish_kernel, taps, blocks), out_shape=...]
    unnamed x11 -> x5, local copies, waits for them, and re-layouts: 1.3 us -> 0.92 us
    pallas_call x1, Pallas kernels: 6.85 us -> 7.2 us  [body(): pl.pallas_call(functools.partial(correlate_kernel, (n, stations, blocks,...]
  transfers between devices with their start and end apart: 4 -> 10, of which waited for: 4 -> 5; matrix products, arithmetic and copies ran while one was open for 0% -> 0% of each run, Pallas kernels for 0% -> 0%
where the time goes in v2:
time: 31.9 us; the launch traced here: 31.7 us
  starting transfers between devices  13.4 us (42%)
  Pallas kernels  10.1 us (32%)
  waiting for transfers between devices  7.16 us (22%)
  local copies, waits for them, and re-layouts  0.92 us (3%)
    ppermute x7, starting transfers between devices, body(): received[d] = lax.ppermute(send[d], 'tmpl', [(i, i ^ d) for i in range(n)])  7.86 us
    pallas_call x1, Pallas kernels, body(): pl.pallas_call(functools.partial(correlate_kernel, (n, stations, blocks,...  7.2 us
    ppermute x3, starting transfers between devices, body(): parts.append(lax.ppermute(partial_stacks[d], 'stn', step))  5.57 us
    ppermute x7, waiting for transfers between devices, body(): received[d] = lax.ppermute(send[d], 'tmpl', [(i, i ^ d) for i in range(n)])  4.74 us
    ppermute x3, waiting for transfers between devices, body(): parts.append(lax.ppermute(partial_stacks[d], 'stn', step))  2.43 us
    pallas_call x1, Pallas kernels, body(): pl.pallas_call(functools.partial(pack_kernel, (n, stations, slots, compon...  2.16 us
    unnamed x5, local copies, waits for them, and re-layouts  0.92 us
    pallas_call x1, Pallas kernels, body(): pl.pallas_call(functools.partial(finish_kernel, taps, blocks), out_shape=...  0.78 us
  transfers between devices with their start and end apart: 10, of which 5 were waited for; matrix products, arithmetic and copies ran while one was open for 0% of the time, Pallas kernels for 0%

profile of v2, /device:TPU:0, one launch (start us, length us, event | category | flops | bytes accessed | tf_op | source)
XLA Modules:
  0.0 31.7 jit_solution(14208966269963398924)
XLA Ops:
  0.0 2.2 %pack.1 = (bf16[240,128]{1,0:T(8,128)(2,1)}, bf16[240,128]{1,0:T(8,128)(2,1)}, bf16[240,128]{1,0:T(8,128)(2,1)}, bf16[240,128]{1,0:T(8,128)(2,1)}, bf16[240,128]...) custom-call(bf16[18,2,128]{2,1,0:T(2,128)(2,1)} %bitcast.8, ...), custom_call_target="tpu_custom_call" | custom-call | tf_op jit(solution)/shard_map/pack/pallas_call | solution.py:289
  2.2 0.5 %collective-permute-start = (bf16[240,128]{1,0:T(8,128)(2,1)}, bf16[240,128]{1,0:T(8,128)(2,1)S(1)}, u32[]{:S(2)}, u32[]{:S(2)}) collective-permute-start(bf16[240,128]{1,0:T(8,128)(2,1)} %get-tuple-element.18), channel_id=1, source_target_pairs={{0,4},{4,0},{8,12},{12,8},{16,20},{20,16},{24,28},{28,24},{1,5},{5... | collective-permute-start | bytes 184328 | tf_op jit(solution)/shard_map/ppermute | solution.py:302
  2.7 2.6 %collective-permute-start.1 = (bf16[240,128]{1,0:T(8,128)(2,1)}, bf16[240,128]{1,0:T(8,128)(2,1)S(1)}, u32[]{:S(2)}, u32[]{:S(2)}) collective-permute-start(bf16[240,128]{1,0:T(8,128)(2,1)} %get-tuple-element.19), channel_id=1, source_target_pairs={{0,8},{4,12},{8,0},{12,4},{16,24},{20,28},{24,16},{28,20},{1,9},{5... | collective-permute-start | bytes 184328 | tf_op jit(solution)/shard_map/ppermute | solution.py:302
  5.3 0.1 collective-permute-start.2
  5.3 1.8 %collective-permute-start.3 = (bf16[240,128]{1,0:T(8,128)(2,1)}, bf16[240,128]{1,0:T(8,128)(2,1)S(1)}, u32[]{:S(2)}, u32[]{:S(2)}) collective-permute-start(bf16[240,128]{1,0:T(8,128)(2,1)} %get-tuple-element.21), channel_id=1, source_target_pairs={{0,16},{4,20},{8,24},{12,28},{16,0},{20,4},{24,8},{28,12},{1,17},{... | collective-permute-start | bytes 184328 | tf_op jit(solution)/shard_map/ppermute | solution.py:302
  7.1 0.0 copy-start.1
  7.1 0.0 collective-permute-start.4
  7.1 0.0 collective-permute-done.refs_2_
  7.1 2.6 %collective-permute-start.5 = (bf16[240,128]{1,0:T(8,128)(2,1)}, bf16[240,128]{1,0:T(8,128)(2,1)S(1)}, u32[]{:S(2)}, u32[]{:S(2)}) collective-permute-start(bf16[240,128]{1,0:T(8,128)(2,1)} %get-tuple-element.23), channel_id=1, source_target_pairs={{0,24},{4,28},{8,16},{12,20},{16,8},{20,12},{24,0},{28,4},{1,25},{... | collective-permute-start | bytes 184328 | tf_op jit(solution)/shard_map/ppermute | solution.py:302
  9.7 0.0 collective-permute-done.1.refs_3_
  9.7 0.3 %collective-permute-start.6 = (bf16[240,128]{1,0:T(8,128)(2,1)}, bf16[240,128]{1,0:T(8,128)(2,1)S(1)}, u32[]{:S(2)}, u32[]{:S(2)}) collective-permute-start(bf16[240,128]{1,0:T(8,128)(2,1)} %get-tuple-element.24), channel_id=1, source_target_pairs={{0,28},{4,24},{8,20},{12,16},{16,12},{20,8},{24,4},{28,0},{1,29},{... | collective-permute-start | bytes 184328 | tf_op jit(solution)/shard_map/ppermute | solution.py:302
  10.0 0.0 copy-done.1
  10.0 0.1 copy.7.refs_0_
  10.1 0.0 collective-permute-done.2.refs_4_
  10.1 0.0 collective-permute-done.3.refs_5_
  10.1 2.5 %collective-permute-done.4.refs_6_ = bf16[240,128]{1,0:T(8,128)(2,1)S(1)} collective-permute-done((bf16[240,128]{1,0:T(8,128)(2,1)}, bf16[240,128]{1,0:T(8,128)(2,1)S(1)}, u32[]{:S(2)}, u32[]{:S(2)}) %collective-permute-start.4) | collective-permute-done | bytes 61472 | tf_op jit(solution)/shard_map/ppermute | solution.py:302
  12.7 0.0 collective-permute-done.5.refs_7_
  12.7 2.2 %collective-permute-done.6.refs_8_ = bf16[240,128]{1,0:T(8,128)(2,1)S(1)} collective-permute-done((bf16[240,128]{1,0:T(8,128)(2,1)}, bf16[240,128]{1,0:T(8,128)(2,1)S(1)}, u32[]{:S(2)}, u32[]{:S(2)}) %collective-permute-start.6) | collective-permute-done | bytes 61472 | tf_op jit(solution)/shard_map/ppermute | solution.py:302
  14.9 0.0 copy-start
  14.9 0.8 %copy-done = bf16[240,128]{1,0:T(8,128)(2,1)S(1)} copy-done((bf16[240,128]{1,0:T(8,128)(2,1)S(1)}, bf16[240,128]{1,0:T(8,128)(2,1)}, u32[]{:S(2)}) %copy-start) | copy-done | bytes 61464
  15.7 7.2 %correlate.1 = (bf16[16,640]{1,0:T(8,128)(2,1)S(1)}, bf16[16,640]{1,0:T(8,128)(2,1)S(1)}, bf16[16,640]{1,0:T(8,128)(2,1)S(1)}, bf16[16,640]{1,0:T(8,128)(2,1)S(1)}) custom-call(s32[6,3]{1,0:T(8,128)S(1)} %copy.7.refs_0_, bf16[240,128]{1,0:T(8,128)(2,1)S(1)} %copy-done, bf16[240,128]{1,0:T(8,128)(2,1)S(1)} %collective-permute-done.refs_2_, ...), custom_call_target="tpu_custom_call" | custom-call | tf_op jit(solution)/shard_map/correlate/pallas_call | solution.py:306
  22.9 1.6 %collective-permute-start.7 = (bf16[16,640]{1,0:T(8,128)(2,1)S(1)}, bf16[16,640]{1,0:T(8,128)(2,1)S(1)}, u32[]{:S(2)}, u32[]{:S(2)}) collective-permute-start(bf16[16,640]{1,0:T(8,128)(2,1)S(1)} %get-tuple-element.26), channel_id=1, source_target_pairs={{0,1},{1,2},{2,3},{3,0},{4,5},{5,6},{6,7},{7,4},{8,9},{9,10},{10,1... | collective-permute-start | bytes 61448 | tf_op jit(solution)/shard_map/ppermute | solution.py:330
  24.5 2.6 %collective-permute-start.8 = (bf16[16,640]{1,0:T(8,128)(2,1)S(1)}, bf16[16,640]{1,0:T(8,128)(2,1)S(1)}, u32[]{:S(2)}, u32[]{:S(2)}) collective-permute-start(bf16[16,640]{1,0:T(8,128)(2,1)S(1)} %get-tuple-element.27), channel_id=1, source_target_pairs={{0,2},{1,3},{2,0},{3,1},{4,6},{5,7},{6,4},{7,5},{8,10},{9,11},{10,... | collective-permute-start | bytes 61448 | tf_op jit(solution)/shard_map/ppermute | solution.py:330
  27.1 1.4 %collective-permute-start.9 = (bf16[16,640]{1,0:T(8,128)(2,1)S(1)}, bf16[16,640]{1,0:T(8,128)(2,1)S(1)}, u32[]{:S(2)}, u32[]{:S(2)}) collective-permute-start(bf16[16,640]{1,0:T(8,128)(2,1)S(1)} %get-tuple-element.28), channel_id=1, source_target_pairs={{0,3},{1,0},{2,1},{3,2},{4,7},{5,4},{6,5},{7,6},{8,11},{9,8},{10,9... | collective-permute-start | bytes 61448 | tf_op jit(solution)/shard_map/ppermute | solution.py:330
  28.5 0.1 collective-permute-done.7.refs_1_
  28.5 1.0 %collective-permute-done.8.refs_2_ = bf16[16,640]{1,0:T(8,128)(2,1)S(1)} collective-permute-done((bf16[16,640]{1,0:T(8,128)(2,1)S(1)}, bf16[16,640]{1,0:T(8,128)(2,1)S(1)}, u32[]{:S(2)}, u32[]{:S(2)}) %collective-permute-start.8) | collective-permute-done | bytes 20512 | tf_op jit(solution)/shard_map/ppermute | solution.py:330
  29.5 1.4 %collective-permute-done.9.refs_3_ = bf16[16,640]{1,0:T(8,128)(2,1)S(1)} collective-permute-done((bf16[16,640]{1,0:T(8,128)(2,1)S(1)}, bf16[16,640]{1,0:T(8,128)(2,1)S(1)}, u32[]{:S(2)}, u32[]{:S(2)}) %collective-permute-start.9) | collective-permute-done | bytes 20512 | tf_op jit(solution)/shard_map/ppermute | solution.py:330
  30.9 0.8 %finish.1 = f32[2,16,256]{2,1,0:T(8,128)} custom-call(bf16[16,640]{1,0:T(8,128)(2,1)S(1)} %get-tuple-element.25.refs_0_, bf16[16,640]{1,0:T(8,128)(2,1)S(1)} %collective-permute-done.7.refs_1_, bf16[16,640]{1,0:T(8,128)(2,1)S(1)} %collective-permute-done.8.refs_2_, bf16[16,640]{1,0:T(8,128)(2,1)S(1)} %collective-permute-done.9.refs_3_), custom_call_target="tpu_custom_call" | custom-call | tf_op jit(solution)/shard_map/finish/pallas_call | solution.py:331
Async XLA Ops:
  2.2 4.9 %collective-permute-start = (bf16[240,128]{1,0:T(8,128)(2,1)}, bf16[240,128]{1,0:T(8,128)(2,1)S(1)}, u32[]{:S(2)}, u32[]{:S(2)}) collective-permute-start(bf16[240,128]{1,0:T(8,128)(2,1)} %get-tuple-element.18), channel_id=1, source_target_pairs={{0,4},{4,0},{8,12},{12,8},{16,20},{20,16},{24,28},{28,24},{1,5},{5... | collective-permute-start | bytes 184328 | tf_op jit(solution)/shard_map/ppermute | solution.py:302
  2.7 7.0 %collective-permute-start.1 = (bf16[240,128]{1,0:T(8,128)(2,1)}, bf16[240,128]{1,0:T(8,128)(2,1)S(1)}, u32[]{:S(2)}, u32[]{:S(2)}) collective-permute-start(bf16[240,128]{1,0:T(8,128)(2,1)} %get-tuple-element.19), channel_id=1, source_target_pairs={{0,8},{4,12},{8,0},{12,4},{16,24},{20,28},{24,16},{28,20},{1,9},{5... | collective-permute-start | bytes 184328 | tf_op jit(solution)/shard_map/ppermute | solution.py:302
  5.3 4.9 %collective-permute-start.2 = (bf16[240,128]{1,0:T(8,128)(2,1)}, bf16[240,128]{1,0:T(8,128)(2,1)S(1)}, u32[]{:S(2)}, u32[]{:S(2)}) collective-permute-start(bf16[240,128]{1,0:T(8,128)(2,1)} %get-tuple-element.20), channel_id=1, source_target_pairs={{0,12},{4,8},{8,4},{12,0},{16,28},{20,24},{24,20},{28,16},{1,13},{... | collective-permute-start | bytes 184328 | tf_op jit(solution)/shard_map/ppermute | solution.py:302
  5.3 4.8 %collective-permute-start.3 = (bf16[240,128]{1,0:T(8,128)(2,1)}, bf16[240,128]{1,0:T(8,128)(2,1)S(1)}, u32[]{:S(2)}, u32[]{:S(2)}) collective-permute-start(bf16[240,128]{1,0:T(8,128)(2,1)} %get-tuple-element.21), channel_id=1, source_target_pairs={{0,16},{4,20},{8,24},{12,28},{16,0},{20,4},{24,8},{28,12},{1,17},{... | collective-permute-start | bytes 184328 | tf_op jit(solution)/shard_map/ppermute | solution.py:302
  7.1 3.0 %copy-start.1 = (s32[6,3]{0,1:T(4,128)S(1)}, s32[6,3]{0,1:T(4,128)}, u32[]{:S(2)}) copy-start(s32[6,3]{0,1:T(4,128)} %param.11) | copy-start | bytes 220
  7.1 5.6 %collective-permute-start.4 = (bf16[240,128]{1,0:T(8,128)(2,1)}, bf16[240,128]{1,0:T(8,128)(2,1)S(1)}, u32[]{:S(2)}, u32[]{:S(2)}) collective-permute-start(bf16[240,128]{1,0:T(8,128)(2,1)} %get-tuple-element.22), channel_id=1, source_target_pairs={{0,20},{4,16},{8,28},{12,24},{16,4},{20,0},{24,12},{28,8},{1,21},{... | collective-permute-start | bytes 184328 | tf_op jit(solution)/shard_map/ppermute | solution.py:302
  7.1 5.6 %collective-permute-start.5 = (bf16[240,128]{1,0:T(8,128)(2,1)}, bf16[240,128]{1,0:T(8,128)(2,1)S(1)}, u32[]{:S(2)}, u32[]{:S(2)}) collective-permute-start(bf16[240,128]{1,0:T(8,128)(2,1)} %get-tuple-element.23), channel_id=1, source_target_pairs={{0,24},{4,28},{8,16},{12,20},{16,8},{20,12},{24,0},{28,4},{1,25},{... | collective-permute-start | bytes 184328 | tf_op jit(solution)/shard_map/ppermute | solution.py:302
  9.7 5.2 %collective-permute-start.6 = (bf16[240,128]{1,0:T(8,128)(2,1)}, bf16[240,128]{1,0:T(8,128)(2,1)S(1)}, u32[]{:S(2)}, u32[]{:S(2)}) collective-permute-start(bf16[240,128]{1,0:T(8,128)(2,1)} %get-tuple-element.24), channel_id=1, source_target_pairs={{0,28},{4,24},{8,20},{12,16},{16,12},{20,8},{24,4},{28,0},{1,29},{... | collective-permute-start | bytes 184328 | tf_op jit(solution)/shard_map/ppermute | solution.py:302
  14.9 0.8 %copy-start = (bf16[240,128]{1,0:T(8,128)(2,1)S(1)}, bf16[240,128]{1,0:T(8,128)(2,1)}, u32[]{:S(2)}) copy-start(bf16[240,128]{1,0:T(8,128)(2,1)} %get-tuple-element.17.refs_1_) | copy-start | bytes 184324
  22.9 5.6 %collective-permute-start.7 = (bf16[16,640]{1,0:T(8,128)(2,1)S(1)}, bf16[16,640]{1,0:T(8,128)(2,1)S(1)}, u32[]{:S(2)}, u32[]{:S(2)}) collective-permute-start(bf16[16,640]{1,0:T(8,128)(2,1)S(1)} %get-tuple-element.26), channel_id=1, source_target_pairs={{0,1},{1,2},{2,3},{3,0},{4,5},{5,6},{6,7},{7,4},{8,9},{9,10},{10,1... | collective-permute-start | bytes 61448 | tf_op jit(solution)/shard_map/ppermute | solution.py:330
  24.5 5.0 %collective-permute-start.8 = (bf16[16,640]{1,0:T(8,128)(2,1)S(1)}, bf16[16,640]{1,0:T(8,128)(2,1)S(1)}, u32[]{:S(2)}, u32[]{:S(2)}) collective-permute-start(bf16[16,640]{1,0:T(8,128)(2,1)S(1)} %get-tuple-element.27), channel_id=1, source_target_pairs={{0,2},{1,3},{2,0},{3,1},{4,6},{5,7},{6,4},{7,5},{8,10},{9,11},{10,... | collective-permute-start | bytes 61448 | tf_op jit(solution)/shard_map/ppermute | solution.py:330
  27.1 3.8 %collective-permute-start.9 = (bf16[16,640]{1,0:T(8,128)(2,1)S(1)}, bf16[16,640]{1,0:T(8,128)(2,1)S(1)}, u32[]{:S(2)}, u32[]{:S(2)}) collective-permute-start(bf16[16,640]{1,0:T(8,128)(2,1)S(1)} %get-tuple-element.28), channel_id=1, source_target_pairs={{0,3},{1,0},{2,1},{3,2},{4,7},{5,4},{6,5},{7,6},{8,11},{9,8},{10,9... | collective-permute-start | bytes 61448 | tf_op jit(solution)/shard_map/ppermute | solution.py:330

commit v3 on v2

--- a/solution.py
+++ b/solution.py
@@ -17,6 +17,22 @@
 
 def ceil_to(value, multiple):
     return -(-value // multiple) * multiple
+
+
+def quotient(values, divisor):
+    if divisor & (divisor - 1):
+        return values // divisor
+    return lax.shift_right_logical(values, divisor.bit_length() - 1)
+
+
+def remainder(values, divisor):
+    if divisor & (divisor - 1):
+        return values % divisor
+    return values & (divisor - 1)
+
+
+def partners(n):
+    return [0] + list(range(n - 1, 0, -1))
 
 
 def column_of(row):
@@ -57,9 +73,9 @@
     group_col = column_of(group)
     upper = lax.broadcasted_iota(jnp.int32, (count, count), 0)
     lower = lax.broadcasted_iota(jnp.int32, (count, count), 1)
-    same = (upper // slots == lower // slots) & (upper < lower)
+    same = (quotient(upper, slots) == quotient(lower, slots)) & (upper < lower)
     rank = jnp.sum(jnp.where(same & (group_col == group), 1, 0), axis=0, keepdims=True)
-    station = lax.broadcasted_iota(jnp.int32, (1, count), 1) // slots
+    station = quotient(lax.broadcasted_iota(jnp.int32, (1, count), 1), slots)
     partner = group ^ lax.axis_index("tmpl")
     position = partner * rows + station * most + rank
     place = lax.broadcasted_iota(jnp.int32, (n * rows, count), 0) == position
@@ -67,8 +83,8 @@
 
     lane = lax.broadcasted_iota(jnp.int32, (count, LANES), 1)
     meta = jnp.where(lane == LANES - 1, column_of(local) + 1, 0)
-    meta = jnp.where(lane == LANES - 2, column_of(moveout // LANES), meta)
-    meta = jnp.where(lane == LANES - 3, column_of(moveout % LANES), meta)
+    meta = jnp.where(lane == LANES - 2, column_of(quotient(moveout, LANES)), meta)
+    meta = jnp.where(lane == LANES - 3, column_of(remainder(moveout, LANES)), meta)
     meta = meta.astype(jnp.float32).astype(jnp.bfloat16)
 
     for copy in copies[:-3]:
@@ -95,7 +111,7 @@
         samples = samples.reshape(samples.shape[0] * samples.shape[1], LANES)
         extra = send_refs[0].shape[0] - (components * whole + tails) * rows - samples.shape[0]
         samples = jnp.concatenate([samples, jnp.zeros((extra, LANES), jnp.float32)], axis=0)
-    for g in range(n):
+    for g, send_ref in zip(partners(n), send_refs):
         mine = slice(g * rows, (g + 1) * rows)
         pieces = [
             placed[c][mine, a * LANES : (a + 1) * LANES] for c in range(components) for a in range(whole)
@@ -103,7 +119,7 @@
         pieces += [ends[mine, e * LANES : (e + 1) * LANES] for e in range(tails)]
         if with_data:
             pieces.append(samples)
-        send_refs[g][...] = jnp.concatenate(pieces, axis=0).astype(jnp.bfloat16)
+        send_ref[...] = jnp.concatenate(pieces, axis=0).astype(jnp.bfloat16)
 
 
 def correlate_kernel(dims, with_data, *refs):
@@ -120,13 +136,14 @@
     total = n * rows
     here = n * most
     lag_tiles = ceil_to(width - taps + 1, LANES) // LANES
+    lag_width = lag_tiles * LANES
     series = stations * components * blocks
     series_rows = ceil_to(series, 8)
 
     if with_data:
         first = sent * rows
-        for i in range(n):
-            x_ref[lax.axis_index("tmpl") ^ i] = recv_refs[i][first:, :].astype(jnp.float32)[:series_rows]
+        for d, recv_ref in zip(partners(n), recv_refs):
+            x_ref[lax.axis_index("tmpl") ^ d] = recv_ref[first:, :].astype(jnp.float32)[:series_rows]
         x = jnp.concatenate([x_ref[i] for i in range(n)], axis=1)
     else:
         x = data_ref[...].astype(jnp.float32)
@@ -168,7 +185,11 @@
 
     target = lax.broadcasted_iota(jnp.int32, (stations * here, total), 0)
     source = lax.broadcasted_iota(jnp.int32, (stations * here, total), 1)
-    wanted = (target % here // most) * rows + (target // here) * most + target % most
+    wanted = (
+        quotient(remainder(target, here), most) * rows
+        + quotient(target, here) * most
+        + remainder(target, most)
+    )
     order = jnp.where(source == wanted, 1.0, 0.0).astype(jnp.bfloat16)
     lane = lax.broadcasted_iota(jnp.int32, (stations * here, LANES), 1)
     blocks_in = [ref[: ceil_to(sent * rows, 16), :].astype(jnp.float32) for ref in recv_refs]
@@ -186,14 +207,14 @@
         pieces.append(jnp.where(lane < tail, end, 0.0))
         squares = functools.reduce(lambda p, q: p + q, [piece * piece for piece in pieces])
         for a in range(chunks):
-            for s in range(stations):
-                at = ((s * components + c) * chunks + a) * here
-                ws_ref[at : at + here, :] = pieces[a][s * here : (s + 1) * here].astype(jnp.bfloat16)
+            at = (c * chunks + a) * LANES
+            ws_ref[:, at : at + LANES] = pieces[a].astype(jnp.bfloat16)
         wave_power = jnp.sum(squares, axis=1, keepdims=True) / taps
         rw_ref[:, c * LANES : (c + 1) * LANES] = jnp.broadcast_to(
             lax.rsqrt(wave_power + epsilon) / taps, (stations * here, LANES)
         )
 
+    depth = (chunks - 1) * LANES + ceil_to(tail, 16)
     lane_here = lax.broadcasted_iota(jnp.int32, (here, LANES), 1)
 
     for s in range(stations):
@@ -214,19 +235,20 @@
                 low = jnp.concatenate(low, axis=1).astype(jnp.bfloat16)
                 pieces = [low] + [pltpu.roll(low, width - q, 1) for q in range(SHIFTS, LANES, SHIFTS)]
                 shifted = jnp.concatenate(pieces, axis=0)
-                first = (s * components + c) * chunks * here
-                w = ws_ref[first : first + chunks * here, :]
-                numerator = jnp.dot(w, shifted, preferred_element_type=jnp.float32)
+                hankel = jnp.concatenate(
+                    [
+                        shifted[: min(LANES, depth - a * LANES), a * LANES : a * LANES + lag_width]
+                        for a in range(chunks)
+                    ],
+                    axis=0,
+                )
+                w = ws_ref[rows_here, c * chunks * LANES : c * chunks * LANES + depth]
+                numerator = jnp.dot(w, hankel, preferred_element_type=jnp.float32)
                 over_wave = rw_ref[rows_here, c * LANES : (c + 1) * LANES]
                 over_data = rd_ref[at : at + 1, :]
                 for t in range(lag_tiles):
-                    pieces = [
-                        numerator[a * here : (a + 1) * here, (t + a) * LANES : (t + a + 1) * LANES]
-                        for a in range(chunks)
-                    ]
-                    summed = functools.reduce(lambda p, q: p + q, pieces)
-                    over = over_data[:, t * LANES : (t + 1) * LANES]
-                    total_corr[t] = total_corr[t] + summed * over_wave * over
+                    cut = slice(t * LANES, (t + 1) * LANES)
+                    total_corr[t] = total_corr[t] + numerator[:, cut] * over_wave * over_data[:, cut]
             windows = []
             for t in range(NK // LANES + 1):
                 window = total_corr[t]
@@ -249,8 +271,8 @@
         onehot, sh_ref[...], (((0,), (0,)), ((), ())), preferred_element_type=jnp.float32
     )
     me = lax.axis_index("stn")
-    for d, out_ref in enumerate(out_refs):
-        owner = lax.rem(me + d, len(out_refs))
+    for d, out_ref in zip(partners(len(out_refs)), out_refs):
+        owner = me ^ d
         theirs = pl.ds(pl.multiple_of(owner * TPD, TPD), TPD)
         out_ref[...] = stack_ref[theirs, :].astype(jnp.bfloat16)
 
@@ -286,6 +308,7 @@
     block_rows = (components * whole + tails) * rows + (series_rows if with_data else 0)
     block_rows = ceil_to(block_rows, 16)
     ins = ([samples] if with_data else []) + [waves, groups, slot_local, moveout]
+    ins = [pltpu.with_memory_space_constraint(x, pltpu.HBM) for x in ins]
     send = pl.pallas_call(
         functools.partial(
             pack_kernel, (n, stations, slots, components, taps, most, rows), with_data
@@ -294,12 +317,13 @@
         in_specs=[pl.BlockSpec(memory_space=pltpu.HBM)] * len(ins),
         scratch_shapes=[pltpu.VMEM(x.shape, x.dtype) for x in ins]
         + [pltpu.SemaphoreType.DMA((len(ins),))],
-        compiler_params=pltpu.CompilerParams(vmem_limit_bytes=60 << 20),
+        compiler_params=pltpu.CompilerParams(vmem_limit_bytes=24 << 20),
         name="pack",
     )(*ins)
-    received = [send[0]] + [None] * (n - 1)
-    for d in range(n - 1, 0, -1):
-        received[d] = lax.ppermute(send[d], "tmpl", [(i, i ^ d) for i in range(n)])
+    received = [
+        lax.ppermute(block, "tmpl", [(i, i ^ d) for i in range(n)]) if d else block
+        for d, block in zip(partners(n), send)
+    ]
     if not with_data:
         samples = lax.all_gather(samples.reshape(series, width_here), "tmpl", axis=1, tiled=True)
     vmem = pl.BlockSpec(memory_space=pltpu.VMEM)
@@ -315,7 +339,7 @@
             pltpu.VMEM((width // LANES, series_rows, LANES), jnp.float32),
             pltpu.VMEM((width // LANES, SHIFTS * series_rows, LANES), jnp.float32),
             pltpu.VMEM((series_rows, ceil_to(width - taps + 1, LANES)), jnp.float32),
-            pltpu.VMEM((stations * components * (whole + 1) * here, LANES), jnp.bfloat16),
+            pltpu.VMEM((stations * here, components * (whole + 1) * LANES), jnp.bfloat16),
             pltpu.VMEM((stations * here, components * LANES), jnp.float32),
             pltpu.VMEM((stations * here, LANES), jnp.float32),
             pltpu.VMEM((stations * here, blocks * NK + LANES), jnp.bfloat16),
@@ -324,10 +348,10 @@
         compiler_params=pltpu.CompilerParams(vmem_limit_bytes=40 << 20),
         name="correlate",
     )(*([] if with_data else [samples]), chan_mask, *received)
-    parts = [partial_stacks[0]]
-    for d in range(1, owners):
-        step = [(i, (i + d) % owners) for i in range(owners)]
-        parts.append(lax.ppermute(partial_stacks[d], "stn", step))
+    parts = [
+        lax.ppermute(part, "stn", [(i, i ^ d) for i in range(owners)]) if d else part
+        for d, part in zip(partners(owners), partial_stacks)
+    ]
     return pl.pallas_call(
         functools.partial(finish_kernel, taps, blocks),
         out_shape=jax.ShapeDtypeStruct((blocks, TPD, NK), jnp.float32),

time: 31.9 us -> 28.8 us (0.903)
  Pallas kernels: 10.1 us -> 8.67 us
  local copies, waits for them, and re-layouts: 0.92 us -> 0.1 us
  starting transfers between devices: 13.4 us -> 12.7 us
    unnamed x5 -> x3, local copies, waits for them, and re-layouts: 0.92 us -> 0.1 us
    ppermute x10, starting transfers between devices: 13.4 us -> 12.7 us  [the longest x7 8.2 us: body(): lax.ppermute(block, 'tmpl', [(i, i ^ d) for i in range(n)])]
    pallas_call x1, Pallas kernels: 2.16 us -> 1.41 us  [body(): pl.pallas_call(functools.partial(pack_kernel, (n, stations, slots, compon...]
    pallas_call x1, Pallas kernels: 7.2 us -> 6.49 us  [body(): pl.pallas_call(functools.partial(correlate_kernel, (n, stations, blocks,...]
  transfers between devices with their start and end apart: 10 -> 10, of which waited for: 5 -> 6; matrix products, arithmetic and copies ran while one was open for 0% -> 0% of each run, Pallas kernels for 0% -> 0%
where the time goes in v3:
time: 28.8 us; the launch traced here: 28.6 us
  starting transfers between devices  12.7 us (44%)
  Pallas kernels  8.67 us (30%)
  waiting for transfers between devices  7.13 us (25%)
    ppermute x7, starting transfers between devices, body(): lax.ppermute(block, 'tmpl', [(i, i ^ d) for i in range(n)])  8.2 us
    pallas_call x1, Pallas kernels, body(): pl.pallas_call(functools.partial(correlate_kernel, (n, stations, blocks,...  6.49 us
    ppermute x3, starting transfers between devices, body(): lax.ppermute(part, 'stn', [(i, i ^ d) for i in range(owners)])  4.45 us
    ppermute x3, waiting for transfers between devices, body(): lax.ppermute(part, 'stn', [(i, i ^ d) for i in range(owners)])  3.97 us
    ppermute x7, waiting for transfers between devices, body(): lax.ppermute(block, 'tmpl', [(i, i ^ d) for i in range(n)])  3.16 us
    pallas_call x1, Pallas kernels, body(): pl.pallas_call(functools.partial(pack_kernel, (n, stations, slots, compon...  1.41 us
    pallas_call x1, Pallas kernels, body(): pl.pallas_call(functools.partial(finish_kernel, taps, blocks), out_shape=...  0.78 us
  transfers between devices with their start and end apart: 10, of which 6 were waited for; matrix products, arithmetic and copies ran while one was open for 0% of the time, Pallas kernels for 0%

profile of v3, /device:TPU:0, one launch (start us, length us, event | category | flops | bytes accessed | tf_op | source)
XLA Modules:
  0.0 28.6 jit_solution(7531432804781524330)
XLA Ops:
  0.0 1.4 %pack.1 = (bf16[240,128]{1,0:T(8,128)(2,1)S(1)}, bf16[240,128]{1,0:T(8,128)(2,1)S(1)}, bf16[240,128]{1,0:T(8,128)(2,1)S(1)}, bf16[240,128]{1,0:T(8,128)(2,1)S(1)...) custom-call(bf16[18,2,128]{2,1,0:T(2,128)(2,1)} %bitcast.8, ...), custom_call_target="tpu_custom_call" | custom-call | tf_op jit(solution)/shard_map/pack/pallas_call | solution.py:312
  1.4 3.4 %collective-permute-start = (bf16[240,128]{1,0:T(8,128)(2,1)S(1)}, bf16[240,128]{1,0:T(8,128)(2,1)S(1)}, u32[]{:S(2)}, u32[]{:S(2)}) collective-permute-start(bf16[240,128]{1,0:T(8,128)(2,1)S(1)} %get-tuple-element.18), channel_id=1, source_target_pairs={{0,28},{4,24},{8,20},{12,16},{16,12},{20,8},{24,4},{28,0},{1,29},{... | collective-permute-start | bytes 184328 | tf_op jit(solution)/shard_map/ppermute | solution.py:324
  4.8 0.6 %collective-permute-start.1 = (bf16[240,128]{1,0:T(8,128)(2,1)S(1)}, bf16[240,128]{1,0:T(8,128)(2,1)S(1)}, u32[]{:S(2)}, u32[]{:S(2)}) collective-permute-start(bf16[240,128]{1,0:T(8,128)(2,1)S(1)} %get-tuple-element.19), channel_id=1, source_target_pairs={{0,24},{4,28},{8,16},{12,20},{16,8},{20,12},{24,0},{28,4},{1,25},{... | collective-permute-start | bytes 184328 | tf_op jit(solution)/shard_map/ppermute | solution.py:324
  5.5 1.4 %collective-permute-start.2 = (bf16[240,128]{1,0:T(8,128)(2,1)S(1)}, bf16[240,128]{1,0:T(8,128)(2,1)S(1)}, u32[]{:S(2)}, u32[]{:S(2)}) collective-permute-start(bf16[240,128]{1,0:T(8,128)(2,1)S(1)} %get-tuple-element.20), channel_id=1, source_target_pairs={{0,20},{4,16},{8,28},{12,24},{16,4},{20,0},{24,12},{28,8},{1,21},{... | collective-permute-start | bytes 184328 | tf_op jit(solution)/shard_map/ppermute | solution.py:324
  6.8 0.3 collective-permute-start.3
  7.1 0.0 copy-start
  7.1 1.1 %collective-permute-start.4 = (bf16[240,128]{1,0:T(8,128)(2,1)S(1)}, bf16[240,128]{1,0:T(8,128)(2,1)S(1)}, u32[]{:S(2)}, u32[]{:S(2)}) collective-permute-start(bf16[240,128]{1,0:T(8,128)(2,1)S(1)} %get-tuple-element.22), channel_id=1, source_target_pairs={{0,12},{4,8},{8,4},{12,0},{16,28},{20,24},{24,20},{28,16},{1,13},{... | collective-permute-start | bytes 184328 | tf_op jit(solution)/shard_map/ppermute | solution.py:324
  8.3 0.0 collective-permute-done.refs_2_
  8.3 1.4 %collective-permute-start.5 = (bf16[240,128]{1,0:T(8,128)(2,1)S(1)}, bf16[240,128]{1,0:T(8,128)(2,1)S(1)}, u32[]{:S(2)}, u32[]{:S(2)}) collective-permute-start(bf16[240,128]{1,0:T(8,128)(2,1)S(1)} %get-tuple-element.23), channel_id=1, source_target_pairs={{0,8},{4,12},{8,0},{12,4},{16,24},{20,28},{24,16},{28,20},{1,9},{5... | collective-permute-start | bytes 184328 | tf_op jit(solution)/shard_map/ppermute | solution.py:324
  9.6 0.8 %collective-permute-done.1.refs_3_ = bf16[240,128]{1,0:T(8,128)(2,1)S(1)} collective-permute-done((bf16[240,128]{1,0:T(8,128)(2,1)S(1)}, bf16[240,128]{1,0:T(8,128)(2,1)S(1)}, u32[]{:S(2)}, u32[]{:S(2)}) %collective-permute-start.1) | collective-permute-done | bytes 61472 | tf_op jit(solution)/shard_map/ppermute | solution.py:324
  10.4 0.0 collective-permute-start.6
  10.4 0.0 copy-done
  10.4 0.1 copy.7.refs_0_
  10.5 0.4 %collective-permute-done.2.refs_4_ = bf16[240,128]{1,0:T(8,128)(2,1)S(1)} collective-permute-done((bf16[240,128]{1,0:T(8,128)(2,1)S(1)}, bf16[240,128]{1,0:T(8,128)(2,1)S(1)}, u32[]{:S(2)}, u32[]{:S(2)}) %collective-permute-start.2) | collective-permute-done | bytes 61472 | tf_op jit(solution)/shard_map/ppermute | solution.py:324
  10.9 1.5 %collective-permute-done.3.refs_5_ = bf16[240,128]{1,0:T(8,128)(2,1)S(1)} collective-permute-done((bf16[240,128]{1,0:T(8,128)(2,1)S(1)}, bf16[240,128]{1,0:T(8,128)(2,1)S(1)}, u32[]{:S(2)}, u32[]{:S(2)}) %collective-permute-start.3) | collective-permute-done | bytes 61472 | tf_op jit(solution)/shard_map/ppermute | solution.py:324
  12.4 0.0 collective-permute-done.4.refs_6_
  12.4 0.5 %collective-permute-done.5.refs_7_ = bf16[240,128]{1,0:T(8,128)(2,1)S(1)} collective-permute-done((bf16[240,128]{1,0:T(8,128)(2,1)S(1)}, bf16[240,128]{1,0:T(8,128)(2,1)S(1)}, u32[]{:S(2)}, u32[]{:S(2)}) %collective-permute-start.5) | collective-permute-done | bytes 61472 | tf_op jit(solution)/shard_map/ppermute | solution.py:324
  12.9 0.0 collective-permute-done.6.refs_8_
  12.9 6.5 %correlate.1 = (bf16[16,640]{1,0:T(8,128)(2,1)S(1)}, bf16[16,640]{1,0:T(8,128)(2,1)S(1)}, bf16[16,640]{1,0:T(8,128)(2,1)S(1)}, bf16[16,640]{1,0:T(8,128)(2,1)S(1)}) custom-call(s32[6,3]{1,0:T(8,128)S(1)} %copy.7.refs_0_, bf16[240,128]{1,0:T(8,128)(2,1)S(1)} %get-tuple-element.17.refs_1_, bf16[240,128]{1,0:T(8,128)(2,1)S(1)} %collective-permute-done.refs_2_, ...), custom_call_target="tpu_custom_call" | custom-call | tf_op jit(solution)/shard_map/correlate/pallas_call | solution.py:330
  19.4 3.7 %collective-permute-start.7 = (bf16[16,640]{1,0:T(8,128)(2,1)S(1)}, bf16[16,640]{1,0:T(8,128)(2,1)S(1)}, u32[]{:S(2)}, u32[]{:S(2)}) collective-permute-start(bf16[16,640]{1,0:T(8,128)(2,1)S(1)} %get-tuple-element.26), channel_id=1, source_target_pairs={{0,3},{1,2},{2,1},{3,0},{4,7},{5,6},{6,5},{7,4},{8,11},{9,10},{10,... | collective-permute-start | bytes 61448 | tf_op jit(solution)/shard_map/ppermute | solution.py:352
  23.1 0.0 collective-permute-start.8
  23.1 0.7 %collective-permute-start.9 = (bf16[16,640]{1,0:T(8,128)(2,1)S(1)}, bf16[16,640]{1,0:T(8,128)(2,1)S(1)}, u32[]{:S(2)}, u32[]{:S(2)}) collective-permute-start(bf16[16,640]{1,0:T(8,128)(2,1)S(1)} %get-tuple-element.28), channel_id=1, source_target_pairs={{0,1},{1,0},{2,3},{3,2},{4,5},{5,4},{6,7},{7,6},{8,9},{9,8},{10,11... | collective-permute-start | bytes 61448 | tf_op jit(solution)/shard_map/ppermute | solution.py:352
  23.8 1.2 %collective-permute-done.7.refs_1_ = bf16[16,640]{1,0:T(8,128)(2,1)S(1)} collective-permute-done((bf16[16,640]{1,0:T(8,128)(2,1)S(1)}, bf16[16,640]{1,0:T(8,128)(2,1)S(1)}, u32[]{:S(2)}, u32[]{:S(2)}) %collective-permute-start.7) | collective-permute-done | bytes 20512 | tf_op jit(solution)/shard_map/ppermute | solution.py:352
  25.0 2.8 %collective-permute-done.8.refs_2_ = bf16[16,640]{1,0:T(8,128)(2,1)S(1)} collective-permute-done((bf16[16,640]{1,0:T(8,128)(2,1)S(1)}, bf16[16,640]{1,0:T(8,128)(2,1)S(1)}, u32[]{:S(2)}, u32[]{:S(2)}) %collective-permute-start.8) | collective-permute-done | bytes 20512 | tf_op jit(solution)/shard_map/ppermute | solution.py:352
  27.8 0.0 collective-permute-done.9.refs_3_
  27.8 0.8 %finish.1 = f32[2,16,256]{2,1,0:T(8,128)} custom-call(bf16[16,640]{1,0:T(8,128)(2,1)S(1)} %get-tuple-element.25.refs_0_, bf16[16,640]{1,0:T(8,128)(2,1)S(1)} %collective-permute-done.7.refs_1_, bf16[16,640]{1,0:T(8,128)(2,1)S(1)} %collective-permute-done.8.refs_2_, bf16[16,640]{1,0:T(8,128)(2,1)S(1)} %collective-permute-done.9.refs_3_), custom_call_target="tpu_custom_call" | custom-call | tf_op jit(solution)/shard_map/finish/pallas_call | solution.py:355
Async XLA Ops:
  1.4 6.8 %collective-permute-start = (bf16[240,128]{1,0:T(8,128)(2,1)S(1)}, bf16[240,128]{1,0:T(8,128)(2,1)S(1)}, u32[]{:S(2)}, u32[]{:S(2)}) collective-permute-start(bf16[240,128]{1,0:T(8,128)(2,1)S(1)} %get-tuple-element.18), channel_id=1, source_target_pairs={{0,28},{4,24},{8,20},{12,16},{16,12},{20,8},{24,4},{28,0},{1,29},{... | collective-permute-start | bytes 184328 | tf_op jit(solution)/shard_map/ppermute | solution.py:324
  4.8 5.6 %collective-permute-start.1 = (bf16[240,128]{1,0:T(8,128)(2,1)S(1)}, bf16[240,128]{1,0:T(8,128)(2,1)S(1)}, u32[]{:S(2)}, u32[]{:S(2)}) collective-permute-start(bf16[240,128]{1,0:T(8,128)(2,1)S(1)} %get-tuple-element.19), channel_id=1, source_target_pairs={{0,24},{4,28},{8,16},{12,20},{16,8},{20,12},{24,0},{28,4},{1,25},{... | collective-permute-start | bytes 184328 | tf_op jit(solution)/shard_map/ppermute | solution.py:324
  5.5 5.4 %collective-permute-start.2 = (bf16[240,128]{1,0:T(8,128)(2,1)S(1)}, bf16[240,128]{1,0:T(8,128)(2,1)S(1)}, u32[]{:S(2)}, u32[]{:S(2)}) collective-permute-start(bf16[240,128]{1,0:T(8,128)(2,1)S(1)} %get-tuple-element.20), channel_id=1, source_target_pairs={{0,20},{4,16},{8,28},{12,24},{16,4},{20,0},{24,12},{28,8},{1,21},{... | collective-permute-start | bytes 184328 | tf_op jit(solution)/shard_map/ppermute | solution.py:324
  6.8 5.6 %collective-permute-start.3 = (bf16[240,128]{1,0:T(8,128)(2,1)S(1)}, bf16[240,128]{1,0:T(8,128)(2,1)S(1)}, u32[]{:S(2)}, u32[]{:S(2)}) collective-permute-start(bf16[240,128]{1,0:T(8,128)(2,1)S(1)} %get-tuple-element.21), channel_id=1, source_target_pairs={{0,16},{4,20},{8,24},{12,28},{16,0},{20,4},{24,8},{28,12},{1,17},{... | collective-permute-start | bytes 184328 | tf_op jit(solution)/shard_map/ppermute | solution.py:324
  7.1 3.3 %copy-start = (s32[6,3]{0,1:T(4,128)S(1)}, s32[6,3]{0,1:T(4,128)}, u32[]{:S(2)}) copy-start(s32[6,3]{0,1:T(4,128)} %param.11) | copy-start | bytes 220
  7.1 5.3 %collective-permute-start.4 = (bf16[240,128]{1,0:T(8,128)(2,1)S(1)}, bf16[240,128]{1,0:T(8,128)(2,1)S(1)}, u32[]{:S(2)}, u32[]{:S(2)}) collective-permute-start(bf16[240,128]{1,0:T(8,128)(2,1)S(1)} %get-tuple-element.22), channel_id=1, source_target_pairs={{0,12},{4,8},{8,4},{12,0},{16,28},{20,24},{24,20},{28,16},{1,13},{... | collective-permute-start | bytes 184328 | tf_op jit(solution)/shard_map/ppermute | solution.py:324
  8.3 4.6 %collective-permute-start.5 = (bf16[240,128]{1,0:T(8,128)(2,1)S(1)}, bf16[240,128]{1,0:T(8,128)(2,1)S(1)}, u32[]{:S(2)}, u32[]{:S(2)}) collective-permute-start(bf16[240,128]{1,0:T(8,128)(2,1)S(1)} %get-tuple-element.23), channel_id=1, source_target_pairs={{0,8},{4,12},{8,0},{12,4},{16,24},{20,28},{24,16},{28,20},{1,9},{5... | collective-permute-start | bytes 184328 | tf_op jit(solution)/shard_map/ppermute | solution.py:324
  10.4 2.5 %collective-permute-start.6 = (bf16[240,128]{1,0:T(8,128)(2,1)S(1)}, bf16[240,128]{1,0:T(8,128)(2,1)S(1)}, u32[]{:S(2)}, u32[]{:S(2)}) collective-permute-start(bf16[240,128]{1,0:T(8,128)(2,1)S(1)} %get-tuple-element.24), channel_id=1, source_target_pairs={{0,4},{4,0},{8,12},{12,8},{16,20},{20,16},{24,28},{28,24},{1,5},{5... | collective-permute-start | bytes 184328 | tf_op jit(solution)/shard_map/ppermute | solution.py:324
  19.4 5.6 %collective-permute-start.7 = (bf16[16,640]{1,0:T(8,128)(2,1)S(1)}, bf16[16,640]{1,0:T(8,128)(2,1)S(1)}, u32[]{:S(2)}, u32[]{:S(2)}) collective-permute-start(bf16[16,640]{1,0:T(8,128)(2,1)S(1)} %get-tuple-element.26), channel_id=1, source_target_pairs={{0,3},{1,2},{2,1},{3,0},{4,7},{5,6},{6,5},{7,4},{8,11},{9,10},{10,... | collective-permute-start | bytes 61448 | tf_op jit(solution)/shard_map/ppermute | solution.py:352
  23.1 4.7 %collective-permute-start.8 = (bf16[16,640]{1,0:T(8,128)(2,1)S(1)}, bf16[16,640]{1,0:T(8,128)(2,1)S(1)}, u32[]{:S(2)}, u32[]{:S(2)}) collective-permute-start(bf16[16,640]{1,0:T(8,128)(2,1)S(1)} %get-tuple-element.27), channel_id=1, source_target_pairs={{0,2},{1,3},{2,0},{3,1},{4,6},{5,7},{6,4},{7,5},{8,10},{9,11},{10,... | collective-permute-start | bytes 61448 | tf_op jit(solution)/shard_map/ppermute | solution.py:352
  23.1 4.7 %collective-permute-start.9 = (bf16[16,640]{1,0:T(8,128)(2,1)S(1)}, bf16[16,640]{1,0:T(8,128)(2,1)S(1)}, u32[]{:S(2)}, u32[]{:S(2)}) collective-permute-start(bf16[16,640]{1,0:T(8,128)(2,1)S(1)} %get-tuple-element.28), channel_id=1, source_target_pairs={{0,1},{1,0},{2,3},{3,2},{4,5},{5,4},{6,7},{7,6},{8,9},{9,8},{10,11... | collective-permute-start | bytes 61448 | tf_op jit(solution)/shard_map/ppermute | solution.py:352

commit v4 on v3

--- a/solution.py
+++ b/solution.py
@@ -10,7 +10,7 @@
 NK = 256
 TPD = 16
 LANES = 128
-SHIFTS = 16
+PHASES = 8
 
 epsilon = 1e-06
 
@@ -33,6 +33,14 @@
 
 def partners(n):
     return [0] + list(range(n - 1, 0, -1))
+
+
+def by_phase(samples):
+    old = lax.broadcasted_iota(jnp.int32, (LANES, LANES), 0)
+    new = lax.broadcasted_iota(jnp.int32, (LANES, LANES), 1)
+    each = LANES // PHASES
+    order = jnp.where(old == PHASES * remainder(new, each) + quotient(new, each), 1.0, 0.0)
+    return jnp.dot(samples, order.astype(jnp.bfloat16), preferred_element_type=jnp.float32)
 
 
 def column_of(row):
@@ -109,6 +117,7 @@
     if with_data:
         samples = held[0][...].astype(jnp.float32)
         samples = samples.reshape(samples.shape[0] * samples.shape[1], LANES)
+        samples = by_phase(samples.astype(jnp.bfloat16))
         extra = send_refs[0].shape[0] - (components * whole + tails) * rows - samples.shape[0]
         samples = jnp.concatenate([samples, jnp.zeros((extra, LANES), jnp.float32)], axis=0)
     for g, send_ref in zip(partners(n), send_refs):
@@ -129,59 +138,74 @@
         data_ref, mask_ref, *refs = refs
     n, stations, blocks, components, taps, most, rows, width, per_group = dims
     recv_refs, refs = refs[:n], refs[n:]
-    *out_refs, x_ref, dsh_ref, rd_ref, ws_ref, rw_ref, meta_ref, sh_ref, stack_ref = refs
+    *out_refs, x_ref, phase_ref, rd_ref, wave_ref, rw_ref, meta_ref, sh_ref, stack_ref = refs
     whole, tail, per_tail, tails = chunk_plan(taps, components)
-    chunks = whole + 1
     sent = components * whole + tails
     total = n * rows
     here = n * most
-    lag_tiles = ceil_to(width - taps + 1, LANES) // LANES
-    lag_width = lag_tiles * LANES
     series = stations * components * blocks
     series_rows = ceil_to(series, 8)
+    tiles = width // LANES
+    assert tiles == PHASES and taps % PHASES
 
     if with_data:
         first = sent * rows
         for d, recv_ref in zip(partners(n), recv_refs):
             x_ref[lax.axis_index("tmpl") ^ d] = recv_ref[first:, :].astype(jnp.float32)[:series_rows]
-        x = jnp.concatenate([x_ref[i] for i in range(n)], axis=1)
     else:
-        x = data_ref[...].astype(jnp.float32)
-        x = jnp.concatenate([x, jnp.zeros((series_rows - series, width), jnp.float32)], axis=0)
-    for r in range(SHIFTS):
-        moved = pltpu.roll(x, width - r, 1) if r else x
-        for t in range(width // LANES):
-            dsh_ref[t, r * series_rows : (r + 1) * series_rows, :] = moved[:, t * LANES : (t + 1) * LANES]
+        for i in range(tiles):
+            x_ref[i, :series, :] = by_phase(data_ref[:, i * LANES : (i + 1) * LANES])
+            x_ref[i, series:, :] = jnp.zeros((series_rows - series, LANES), jnp.float32)
+    each = LANES // PHASES
+    piece = quotient(lax.broadcasted_iota(jnp.int32, (series_rows, LANES), 1), each)
+    for r in range(PHASES):
+        phase = jnp.zeros((series_rows, LANES), jnp.float32)
+        for i in range(tiles):
+            by = each * ((i - r) % PHASES)
+            moved = pltpu.roll(x_ref[i], by, 1) if by else x_ref[i]
+            phase = jnp.where(piece == i, moved, phase)
+        phase_ref[pl.ds(r, series_rows, stride=PHASES), :] = phase
 
     def ahead(values, by):
-        return pltpu.roll(values, width - by, 1)
-
-    sums = {1: x * x}
+        return pltpu.roll(values, LANES - by, 1)
+
+    phase_rows = series_rows * PHASES
+    squares = phase_ref[...]
+    squares = squares * squares
+    r = remainder(lax.broadcasted_iota(jnp.int32, (phase_rows, LANES), 0), PHASES)
+    until, since = squares, squares
+    for step in (1, 2, 4):
+        until = until + jnp.where(r >= step, pltpu.roll(until, step, 0), 0.0)
+        since = since + jnp.where(r < PHASES - step, pltpu.roll(since, phase_rows - step, 0), 0.0)
+    block = until + since - squares
+    full, over = taps // PHASES, taps % PHASES - 1
+    sums = {1: block}
     size = 1
-    while 2 * size <= taps:
+    while 2 * size <= full - 1:
         sums[2 * size] = sums[size] + ahead(sums[size], size)
         size = 2 * size
-    power = sums[size]
-    start = size
-    while start < taps:
-        size = size // 2
-        if taps - start >= size:
+    power, start = since, 1
+    while start < full:
+        if start + size <= full:
             power = power + ahead(sums[size], start)
             start += size
+        size = size // 2
+    last = until
+    if over:
+        up, down = pltpu.roll(until, phase_rows - over, 0), pltpu.roll(until, PHASES - over, 0)
+        last = jnp.where(r < PHASES - over, up, down)
+    power = power + jnp.where(
+        r < PHASES - over, ahead(last, full), ahead(block, full) + ahead(last, full + 1)
+    )
     scale = lax.rsqrt(power / taps + epsilon)
-    row = lax.broadcasted_iota(jnp.int32, (series_rows, LANES), 0)
-    factor = jnp.zeros((series_rows, LANES), jnp.float32)
     for s in range(stations):
         used = [mask_ref[s, c] for c in range(components)]
         total_used = jnp.maximum(functools.reduce(lambda p, q: p + q, used), 1)
         for c in range(components):
-            at = (s * components + c) * blocks
-            mine = (row >= at) & (row < at + blocks)
-            value = jnp.full((series_rows, LANES), used[c]).astype(jnp.float32)
-            value = value / jnp.full((series_rows, LANES), total_used).astype(jnp.float32)
-            factor = jnp.where(mine, value, factor)
-    for t in range(lag_tiles):
-        rd_ref[:, t * LANES : (t + 1) * LANES] = scale[:, t * LANES : (t + 1) * LANES] * factor
+            mine = slice((s * components + c) * blocks * PHASES, (s * components + c + 1) * blocks * PHASES)
+            factor = jnp.full((blocks * PHASES, LANES), used[c]).astype(jnp.float32)
+            factor = factor / jnp.full((blocks * PHASES, LANES), total_used).astype(jnp.float32)
+            rd_ref[mine, :] = scale[mine, :] * factor
 
     target = lax.broadcasted_iota(jnp.int32, (stations * here, total), 0)
     source = lax.broadcasted_iota(jnp.int32, (stations * here, total), 1)
@@ -206,60 +230,68 @@
         end = pltpu.roll(end, LANES - before, 1) if before else end
         pieces.append(jnp.where(lane < tail, end, 0.0))
         squares = functools.reduce(lambda p, q: p + q, [piece * piece for piece in pieces])
-        for a in range(chunks):
-            at = (c * chunks + a) * LANES
-            ws_ref[:, at : at + LANES] = pieces[a].astype(jnp.bfloat16)
+        wave = jnp.concatenate([piece.astype(jnp.bfloat16) for piece in pieces], axis=1)
+        for p in range(PHASES):
+            moved = pltpu.roll(wave, p, 1) if p else wave
+            for s in range(stations):
+                at = ((s * components + c) * PHASES + p) * here
+                wave_ref[at : at + here, :] = moved[s * here : (s + 1) * here, :]
         wave_power = jnp.sum(squares, axis=1, keepdims=True) / taps
         rw_ref[:, c * LANES : (c + 1) * LANES] = jnp.broadcast_to(
             lax.rsqrt(wave_power + epsilon) / taps, (stations * here, LANES)
         )
 
-    depth = (chunks - 1) * LANES + ceil_to(tail, 16)
+    depth = ceil_to(taps + PHASES - 1, 2 * PHASES)
+    span = NK // PHASES
+    fit = LANES // span
     lane_here = lax.broadcasted_iota(jnp.int32, (here, LANES), 1)
+    column = quotient(lane_here, span)
 
     for s in range(stations):
         rows_here = slice(s * here, (s + 1) * here)
         meta = meta_ref[rows_here, :]
-        tiles_over = meta[:, LANES - 2 : LANES - 1].astype(jnp.int32)
-        lanes_over = meta[:, LANES - 3 : LANES - 2].astype(jnp.int32)
-        index = lane_here + lanes_over
-        within = index < LANES
-        index = jnp.bitwise_and(index, LANES - 1)
+        moved_by = meta[:, LANES - 2 : LANES - 1] * LANES + meta[:, LANES - 3 : LANES - 2]
+        moved_by = moved_by.astype(jnp.int32)
+        corr = [[None] * blocks for _ in range(PHASES)]
+        for c in range(components):
+            at = (s * components + c) * PHASES
+            shifted = []
+            for b in range(blocks):
+                low = phase_ref[at * blocks + b * PHASES : at * blocks + (b + 1) * PHASES, :]
+                low = jnp.concatenate([low, ahead(low, 1)], axis=0).astype(jnp.bfloat16)
+                low = [low] + [ahead(low, i) for i in range(2, depth // PHASES, 2)]
+                shifted.append(jnp.concatenate(low, axis=0))
+            shifted = jnp.concatenate(shifted, axis=1)
+            w = wave_ref[at * here : (at + PHASES) * here, :depth]
+            numerator = jnp.dot(w, shifted, preferred_element_type=jnp.float32)
+            over_wave = rw_ref[rows_here, c * LANES : (c + 1) * LANES]
+            for p in range(PHASES):
+                for b in range(blocks):
+                    term = numerator[p * here : (p + 1) * here, b * LANES : (b + 1) * LANES]
+                    row = at * blocks + b * PHASES + p
+                    term = term * over_wave * rd_ref[row : row + 1, :]
+                    corr[p][b] = term if c == 0 else corr[p][b] + term
+        step = PHASES // 2
+        while step:
+            chosen = (moved_by & step) != 0
+            ahead_of = [
+                corr[p + step] if p + step < PHASES else [ahead(v, 1) for v in corr[p + step - PHASES]]
+                for p in range(PHASES)
+            ]
+            corr = [
+                [jnp.where(chosen, ahead_of[p][b], corr[p][b]) for b in range(blocks)]
+                for p in range(PHASES)
+            ]
+            step = step // 2
+        index = remainder(lane_here, span) + quotient(moved_by, PHASES)
         for b in range(blocks):
-            total_corr = [jnp.zeros((here, LANES), jnp.float32) for _ in range(lag_tiles)]
-            for c in range(components):
-                at = (s * components + c) * blocks + b
-                low = [
-                    dsh_ref[t, pl.ds(at, SHIFTS, stride=series_rows), :] for t in range(width // LANES)
-                ]
-                low = jnp.concatenate(low, axis=1).astype(jnp.bfloat16)
-                pieces = [low] + [pltpu.roll(low, width - q, 1) for q in range(SHIFTS, LANES, SHIFTS)]
-                shifted = jnp.concatenate(pieces, axis=0)
-                hankel = jnp.concatenate(
-                    [
-                        shifted[: min(LANES, depth - a * LANES), a * LANES : a * LANES + lag_width]
-                        for a in range(chunks)
-                    ],
-                    axis=0,
-                )
-                w = ws_ref[rows_here, c * chunks * LANES : c * chunks * LANES + depth]
-                numerator = jnp.dot(w, hankel, preferred_element_type=jnp.float32)
-                over_wave = rw_ref[rows_here, c * LANES : (c + 1) * LANES]
-                over_data = rd_ref[at : at + 1, :]
-                for t in range(lag_tiles):
-                    cut = slice(t * LANES, (t + 1) * LANES)
-                    total_corr[t] = total_corr[t] + numerator[:, cut] * over_wave * over_data[:, cut]
-            windows = []
-            for t in range(NK // LANES + 1):
-                window = total_corr[t]
-                for h in range(1, lag_tiles - NK // LANES):
-                    if t + h < lag_tiles:
-                        window = jnp.where(tiles_over == h, total_corr[t + h], window)
-                windows.append(jnp.take_along_axis(window, index, axis=1))
-            for t in range(NK // LANES):
-                aligned = jnp.where(within, windows[t], windows[t + 1])
-                at = b * NK + t * LANES
-                sh_ref[rows_here, at : at + LANES] = aligned.astype(jnp.bfloat16)
+            for h in range(PHASES // fit):
+                packed = jnp.take_along_axis(corr[h * fit][b], index, axis=1)
+                for q in range(1, fit):
+                    taken = jnp.take_along_axis(corr[h * fit + q][b], index, axis=1)
+                    packed = jnp.where(column == q, taken, packed)
+                at = b * NK + h * LANES
+                sh_ref[rows_here, at : at + LANES] = packed.astype(jnp.bfloat16)
 
     slot = lax.broadcasted_iota(jnp.int32, (stations * here, LANES), 0)
     half = (slot < stations * here // 2) == (lane < LANES // 2)
@@ -267,9 +299,20 @@
     local = meta_ref[:, LANES - 1 :].astype(jnp.int32) - 1
     template = lax.broadcasted_iota(jnp.int32, (stations * here, per_group), 1)
     onehot = jnp.where(local == template, 1.0, 0.0).astype(jnp.bfloat16)
-    stack_ref[...] = lax.dot_general(
+    stacks = lax.dot_general(
         onehot, sh_ref[...], (((0,), (0,)), ((), ())), preferred_element_type=jnp.float32
     )
+    old = lax.broadcasted_iota(jnp.int32, (NK, NK), 0)
+    new = lax.broadcasted_iota(jnp.int32, (NK, NK), 1)
+    in_order = jnp.where(old == span * remainder(new, PHASES) + quotient(new, PHASES), 1.0, 0.0)
+    for b in range(blocks):
+        lags = slice(b * NK, (b + 1) * NK)
+        stack_ref[:, lags] = jnp.dot(
+            stacks[:, lags].astype(jnp.bfloat16),
+            in_order.astype(jnp.bfloat16),
+            preferred_element_type=jnp.float32,
+        )
+    stack_ref[:, blocks * NK :] = stacks[:, blocks * NK :]
     me = lax.axis_index("stn")
     for d, out_ref in zip(partners(len(out_refs)), out_refs):
         owner = me ^ d
@@ -337,9 +380,9 @@
         in_specs=[vmem] * (0 if with_data else 1) + [pl.BlockSpec(memory_space=pltpu.SMEM)] + [vmem] * n,
         scratch_shapes=[
             pltpu.VMEM((width // LANES, series_rows, LANES), jnp.float32),
-            pltpu.VMEM((width // LANES, SHIFTS * series_rows, LANES), jnp.float32),
-            pltpu.VMEM((series_rows, ceil_to(width - taps + 1, LANES)), jnp.float32),
-            pltpu.VMEM((stations * here, components * (whole + 1) * LANES), jnp.bfloat16),
+            pltpu.VMEM((series_rows * PHASES, LANES), jnp.float32),
+            pltpu.VMEM((series_rows * PHASES, LANES), jnp.float32),
+            pltpu.VMEM((stations * components * PHASES * here, (whole + 1) * LANES), jnp.bfloat16),
             pltpu.VMEM((stations * here, components * LANES), jnp.float32),
             pltpu.VMEM((stations * here, LANES), jnp.float32),
             pltpu.VMEM((stations * here, blocks * NK + LANES), jnp.bfloat16),

time: 28.8 us -> 30.2 us (1.049)
  Pallas kernels: 8.67 us -> 10.1 us
    pallas_call x1, Pallas kernels: 6.49 us -> 7.88 us  [body(): pl.pallas_call(functools.partial(correlate_kernel, (n, stations, blocks,...]
where the time goes in v4:
time: 30.2 us; the launch traced here: 30 us
  starting transfers between devices  12.6 us (42%)
  Pallas kernels  10.1 us (33%)
  waiting for transfers between devices  7.15 us (24%)
    ppermute x7, starting transfers between devices, body(): lax.ppermute(block, 'tmpl', [(i, i ^ d) for i in range(n)])  8.19 us
    pallas_call x1, Pallas kernels, body(): pl.pallas_call(functools.partial(correlate_kernel, (n, stations, blocks,...  7.88 us
    ppermute x3, starting transfers between devices, body(): lax.ppermute(part, 'stn', [(i, i ^ d) for i in range(owners)])  4.45 us
    ppermute x3, waiting for transfers between devices, body(): lax.ppermute(part, 'stn', [(i, i ^ d) for i in range(owners)])  3.98 us
    ppermute x7, waiting for transfers between devices, body(): lax.ppermute(block, 'tmpl', [(i, i ^ d) for i in range(n)])  3.17 us
    pallas_call x1, Pallas kernels, body(): pl.pallas_call(functools.partial(pack_kernel, (n, stations, slots, compon...  1.42 us
    pallas_call x1, Pallas kernels, body(): pl.pallas_call(functools.partial(finish_kernel, taps, blocks), out_shape=...  0.78 us
  transfers between devices with their start and end apart: 10, of which 6 were waited for; matrix products, arithmetic and copies ran while one was open for 0% of the time, Pallas kernels for 0%

profile of v4, /device:TPU:0, one launch (start us, length us, event | category | flops | bytes accessed | tf_op | source)
XLA Modules:
  0.0 30.0 jit_solution(17414170548961381184)
XLA Ops:
  0.0 1.4 %pack.1 = (bf16[240,128]{1,0:T(8,128)(2,1)S(1)}, bf16[240,128]{1,0:T(8,128)(2,1)S(1)}, bf16[240,128]{1,0:T(8,128)(2,1)S(1)}, bf16[240,128]{1,0:T(8,128)(2,1)S(1)...) custom-call(bf16[18,2,128]{2,1,0:T(2,128)(2,1)} %bitcast.8, ...), custom_call_target="tpu_custom_call" | custom-call | tf_op jit(solution)/shard_map/pack/pallas_call | solution.py:355
  1.4 3.4 %collective-permute-start = (bf16[240,128]{1,0:T(8,128)(2,1)S(1)}, bf16[240,128]{1,0:T(8,128)(2,1)S(1)}, u32[]{:S(2)}, u32[]{:S(2)}) collective-permute-start(bf16[240,128]{1,0:T(8,128)(2,1)S(1)} %get-tuple-element.18), channel_id=1, source_target_pairs={{0,28},{4,24},{8,20},{12,16},{16,12},{20,8},{24,4},{28,0},{1,29},{... | collective-permute-start | bytes 184328 | tf_op jit(solution)/shard_map/ppermute | solution.py:367
  4.8 0.6 %collective-permute-start.1 = (bf16[240,128]{1,0:T(8,128)(2,1)S(1)}, bf16[240,128]{1,0:T(8,128)(2,1)S(1)}, u32[]{:S(2)}, u32[]{:S(2)}) collective-permute-start(bf16[240,128]{1,0:T(8,128)(2,1)S(1)} %get-tuple-element.19), channel_id=1, source_target_pairs={{0,24},{4,28},{8,16},{12,20},{16,8},{20,12},{24,0},{28,4},{1,25},{... | collective-permute-start | bytes 184328 | tf_op jit(solution)/shard_map/ppermute | solution.py:367
  5.5 1.4 %collective-permute-start.2 = (bf16[240,128]{1,0:T(8,128)(2,1)S(1)}, bf16[240,128]{1,0:T(8,128)(2,1)S(1)}, u32[]{:S(2)}, u32[]{:S(2)}) collective-permute-start(bf16[240,128]{1,0:T(8,128)(2,1)S(1)} %get-tuple-element.20), channel_id=1, source_target_pairs={{0,20},{4,16},{8,28},{12,24},{16,4},{20,0},{24,12},{28,8},{1,21},{... | collective-permute-start | bytes 184328 | tf_op jit(solution)/shard_map/ppermute | solution.py:367
  6.9 0.3 collective-permute-start.3
  7.1 0.0 copy-start
  7.1 1.1 %collective-permute-start.4 = (bf16[240,128]{1,0:T(8,128)(2,1)S(1)}, bf16[240,128]{1,0:T(8,128)(2,1)S(1)}, u32[]{:S(2)}, u32[]{:S(2)}) collective-permute-start(bf16[240,128]{1,0:T(8,128)(2,1)S(1)} %get-tuple-element.22), channel_id=1, source_target_pairs={{0,12},{4,8},{8,4},{12,0},{16,28},{20,24},{24,20},{28,16},{1,13},{... | collective-permute-start | bytes 184328 | tf_op jit(solution)/shard_map/ppermute | solution.py:367
  8.3 0.0 collective-permute-done.refs_2_
  8.3 1.4 %collective-permute-start.5 = (bf16[240,128]{1,0:T(8,128)(2,1)S(1)}, bf16[240,128]{1,0:T(8,128)(2,1)S(1)}, u32[]{:S(2)}, u32[]{:S(2)}) collective-permute-start(bf16[240,128]{1,0:T(8,128)(2,1)S(1)} %get-tuple-element.23), channel_id=1, source_target_pairs={{0,8},{4,12},{8,0},{12,4},{16,24},{20,28},{24,16},{28,20},{1,9},{5... | collective-permute-start | bytes 184328 | tf_op jit(solution)/shard_map/ppermute | solution.py:367
  9.6 0.8 %collective-permute-done.1.refs_3_ = bf16[240,128]{1,0:T(8,128)(2,1)S(1)} collective-permute-done((bf16[240,128]{1,0:T(8,128)(2,1)S(1)}, bf16[240,128]{1,0:T(8,128)(2,1)S(1)}, u32[]{:S(2)}, u32[]{:S(2)}) %collective-permute-start.1) | collective-permute-done | bytes 61472 | tf_op jit(solution)/shard_map/ppermute | solution.py:367
  10.4 0.0 collective-permute-start.6
  10.4 0.0 copy-done
  10.4 0.1 copy.7.refs_0_
  10.5 0.4 %collective-permute-done.2.refs_4_ = bf16[240,128]{1,0:T(8,128)(2,1)S(1)} collective-permute-done((bf16[240,128]{1,0:T(8,128)(2,1)S(1)}, bf16[240,128]{1,0:T(8,128)(2,1)S(1)}, u32[]{:S(2)}, u32[]{:S(2)}) %collective-permute-start.2) | collective-permute-done | bytes 61472 | tf_op jit(solution)/shard_map/ppermute | solution.py:367
  10.9 1.5 %collective-permute-done.3.refs_5_ = bf16[240,128]{1,0:T(8,128)(2,1)S(1)} collective-permute-done((bf16[240,128]{1,0:T(8,128)(2,1)S(1)}, bf16[240,128]{1,0:T(8,128)(2,1)S(1)}, u32[]{:S(2)}, u32[]{:S(2)}) %collective-permute-start.3) | collective-permute-done | bytes 61472 | tf_op jit(solution)/shard_map/ppermute | solution.py:367
  12.4 0.0 collective-permute-done.4.refs_6_
  12.4 0.5 %collective-permute-done.5.refs_7_ = bf16[240,128]{1,0:T(8,128)(2,1)S(1)} collective-permute-done((bf16[240,128]{1,0:T(8,128)(2,1)S(1)}, bf16[240,128]{1,0:T(8,128)(2,1)S(1)}, u32[]{:S(2)}, u32[]{:S(2)}) %collective-permute-start.5) | collective-permute-done | bytes 61472 | tf_op jit(solution)/shard_map/ppermute | solution.py:367
  12.9 0.0 collective-permute-done.6.refs_8_
  12.9 7.9 %correlate.1 = (bf16[16,640]{1,0:T(8,128)(2,1)S(1)}, bf16[16,640]{1,0:T(8,128)(2,1)S(1)}, bf16[16,640]{1,0:T(8,128)(2,1)S(1)}, bf16[16,640]{1,0:T(8,128)(2,1)S(1)}) custom-call(s32[6,3]{1,0:T(8,128)S(1)} %copy.7.refs_0_, bf16[240,128]{1,0:T(8,128)(2,1)S(1)} %get-tuple-element.17.refs_1_, bf16[240,128]{1,0:T(8,128)(2,1)S(1)} %collective-permute-done.refs_2_, ...), custom_call_target="tpu_custom_call" | custom-call | tf_op jit(solution)/shard_map/correlate/pallas_call | solution.py:373
  20.8 3.7 %collective-permute-start.7 = (bf16[16,640]{1,0:T(8,128)(2,1)S(1)}, bf16[16,640]{1,0:T(8,128)(2,1)S(1)}, u32[]{:S(2)}, u32[]{:S(2)}) collective-permute-start(bf16[16,640]{1,0:T(8,128)(2,1)S(1)} %get-tuple-element.26), channel_id=1, source_target_pairs={{0,3},{1,2},{2,1},{3,0},{4,7},{5,6},{6,5},{7,4},{8,11},{9,10},{10,... | collective-permute-start | bytes 61448 | tf_op jit(solution)/shard_map/ppermute | solution.py:395
  24.5 0.0 collective-permute-start.8
  24.5 0.7 %collective-permute-start.9 = (bf16[16,640]{1,0:T(8,128)(2,1)S(1)}, bf16[16,640]{1,0:T(8,128)(2,1)S(1)}, u32[]{:S(2)}, u32[]{:S(2)}) collective-permute-start(bf16[16,640]{1,0:T(8,128)(2,1)S(1)} %get-tuple-element.28), channel_id=1, source_target_pairs={{0,1},{1,0},{2,3},{3,2},{4,5},{5,4},{6,7},{7,6},{8,9},{9,8},{10,11... | collective-permute-start | bytes 61448 | tf_op jit(solution)/shard_map/ppermute | solution.py:395
  25.2 1.2 %collective-permute-done.7.refs_1_ = bf16[16,640]{1,0:T(8,128)(2,1)S(1)} collective-permute-done((bf16[16,640]{1,0:T(8,128)(2,1)S(1)}, bf16[16,640]{1,0:T(8,128)(2,1)S(1)}, u32[]{:S(2)}, u32[]{:S(2)}) %collective-permute-start.7) | collective-permute-done | bytes 20512 | tf_op jit(solution)/shard_map/ppermute | solution.py:395
  26.4 2.8 %collective-permute-done.8.refs_2_ = bf16[16,640]{1,0:T(8,128)(2,1)S(1)} collective-permute-done((bf16[16,640]{1,0:T(8,128)(2,1)S(1)}, bf16[16,640]{1,0:T(8,128)(2,1)S(1)}, u32[]{:S(2)}, u32[]{:S(2)}) %collective-permute-start.8) | collective-permute-done | bytes 20512 | tf_op jit(solution)/shard_map/ppermute | solution.py:395
  29.2 0.0 collective-permute-done.9.refs_3_
  29.2 0.8 %finish.1 = f32[2,16,256]{2,1,0:T(8,128)} custom-call(bf16[16,640]{1,0:T(8,128)(2,1)S(1)} %get-tuple-element.25.refs_0_, bf16[16,640]{1,0:T(8,128)(2,1)S(1)} %collective-permute-done.7.refs_1_, bf16[16,640]{1,0:T(8,128)(2,1)S(1)} %collective-permute-done.8.refs_2_, bf16[16,640]{1,0:T(8,128)(2,1)S(1)} %collective-permute-done.9.refs_3_), custom_call_target="tpu_custom_call" | custom-call | tf_op jit(solution)/shard_map/finish/pallas_call | solution.py:398
Async XLA Ops:
  1.4 6.8 %collective-permute-start = (bf16[240,128]{1,0:T(8,128)(2,1)S(1)}, bf16[240,128]{1,0:T(8,128)(2,1)S(1)}, u32[]{:S(2)}, u32[]{:S(2)}) collective-permute-start(bf16[240,128]{1,0:T(8,128)(2,1)S(1)} %get-tuple-element.18), channel_id=1, source_target_pairs={{0,28},{4,24},{8,20},{12,16},{16,12},{20,8},{24,4},{28,0},{1,29},{... | collective-permute-start | bytes 184328 | tf_op jit(solution)/shard_map/ppermute | solution.py:367
  4.8 5.6 %collective-permute-start.1 = (bf16[240,128]{1,0:T(8,128)(2,1)S(1)}, bf16[240,128]{1,0:T(8,128)(2,1)S(1)}, u32[]{:S(2)}, u32[]{:S(2)}) collective-permute-start(bf16[240,128]{1,0:T(8,128)(2,1)S(1)} %get-tuple-element.19), channel_id=1, source_target_pairs={{0,24},{4,28},{8,16},{12,20},{16,8},{20,12},{24,0},{28,4},{1,25},{... | collective-permute-start | bytes 184328 | tf_op jit(solution)/shard_map/ppermute | solution.py:367
  5.5 5.4 %collective-permute-start.2 = (bf16[240,128]{1,0:T(8,128)(2,1)S(1)}, bf16[240,128]{1,0:T(8,128)(2,1)S(1)}, u32[]{:S(2)}, u32[]{:S(2)}) collective-permute-start(bf16[240,128]{1,0:T(8,128)(2,1)S(1)} %get-tuple-element.20), channel_id=1, source_target_pairs={{0,20},{4,16},{8,28},{12,24},{16,4},{20,0},{24,12},{28,8},{1,21},{... | collective-permute-start | bytes 184328 | tf_op jit(solution)/shard_map/ppermute | solution.py:367
  6.9 5.5 %collective-permute-start.3 = (bf16[240,128]{1,0:T(8,128)(2,1)S(1)}, bf16[240,128]{1,0:T(8,128)(2,1)S(1)}, u32[]{:S(2)}, u32[]{:S(2)}) collective-permute-start(bf16[240,128]{1,0:T(8,128)(2,1)S(1)} %get-tuple-element.21), channel_id=1, source_target_pairs={{0,16},{4,20},{8,24},{12,28},{16,0},{20,4},{24,8},{28,12},{1,17},{... | collective-permute-start | bytes 184328 | tf_op jit(solution)/shard_map/ppermute | solution.py:367
  7.1 3.3 %copy-start = (s32[6,3]{0,1:T(4,128)S(1)}, s32[6,3]{0,1:T(4,128)}, u32[]{:S(2)}) copy-start(s32[6,3]{0,1:T(4,128)} %param.11) | copy-start | bytes 220
  7.1 5.3 %collective-permute-start.4 = (bf16[240,128]{1,0:T(8,128)(2,1)S(1)}, bf16[240,128]{1,0:T(8,128)(2,1)S(1)}, u32[]{:S(2)}, u32[]{:S(2)}) collective-permute-start(bf16[240,128]{1,0:T(8,128)(2,1)S(1)} %get-tuple-element.22), channel_id=1, source_target_pairs={{0,12},{4,8},{8,4},{12,0},{16,28},{20,24},{24,20},{28,16},{1,13},{... | collective-permute-start | bytes 184328 | tf_op jit(solution)/shard_map/ppermute | solution.py:367
  8.3 4.6 %collective-permute-start.5 = (bf16[240,128]{1,0:T(8,128)(2,1)S(1)}, bf16[240,128]{1,0:T(8,128)(2,1)S(1)}, u32[]{:S(2)}, u32[]{:S(2)}) collective-permute-start(bf16[240,128]{1,0:T(8,128)(2,1)S(1)} %get-tuple-element.23), channel_id=1, source_target_pairs={{0,8},{4,12},{8,0},{12,4},{16,24},{20,28},{24,16},{28,20},{1,9},{5... | collective-permute-start | bytes 184328 | tf_op jit(solution)/shard_map/ppermute | solution.py:367
  10.4 2.5 %collective-permute-start.6 = (bf16[240,128]{1,0:T(8,128)(2,1)S(1)}, bf16[240,128]{1,0:T(8,128)(2,1)S(1)}, u32[]{:S(2)}, u32[]{:S(2)}) collective-permute-start(bf16[240,128]{1,0:T(8,128)(2,1)S(1)} %get-tuple-element.24), channel_id=1, source_target_pairs={{0,4},{4,0},{8,12},{12,8},{16,20},{20,16},{24,28},{28,24},{1,5},{5... | collective-permute-start | bytes 184328 | tf_op jit(solution)/shard_map/ppermute | solution.py:367
  20.8 5.6 %collective-permute-start.7 = (bf16[16,640]{1,0:T(8,128)(2,1)S(1)}, bf16[16,640]{1,0:T(8,128)(2,1)S(1)}, u32[]{:S(2)}, u32[]{:S(2)}) collective-permute-start(bf16[16,640]{1,0:T(8,128)(2,1)S(1)} %get-tuple-element.26), channel_id=1, source_target_pairs={{0,3},{1,2},{2,1},{3,0},{4,7},{5,6},{6,5},{7,4},{8,11},{9,10},{10,... | collective-permute-start | bytes 61448 | tf_op jit(solution)/shard_map/ppermute | solution.py:395
  24.5 4.7 %collective-permute-start.8 = (bf16[16,640]{1,0:T(8,128)(2,1)S(1)}, bf16[16,640]{1,0:T(8,128)(2,1)S(1)}, u32[]{:S(2)}, u32[]{:S(2)}) collective-permute-start(bf16[16,640]{1,0:T(8,128)(2,1)S(1)} %get-tuple-element.27), channel_id=1, source_target_pairs={{0,2},{1,3},{2,0},{3,1},{4,6},{5,7},{6,4},{7,5},{8,10},{9,11},{10,... | collective-permute-start | bytes 61448 | tf_op jit(solution)/shard_map/ppermute | solution.py:395
  24.5 4.7 %collective-permute-start.9 = (bf16[16,640]{1,0:T(8,128)(2,1)S(1)}, bf16[16,640]{1,0:T(8,128)(2,1)S(1)}, u32[]{:S(2)}, u32[]{:S(2)}) collective-permute-start(bf16[16,640]{1,0:T(8,128)(2,1)S(1)} %get-tuple-element.28), channel_id=1, source_target_pairs={{0,1},{1,0},{2,3},{3,2},{4,5},{5,4},{6,7},{7,6},{8,9},{9,8},{10,11... | collective-permute-start | bytes 61448 | tf_op jit(solution)/shard_map/ppermute | solution.py:395

commit v5 on v3

--- a/solution.py
+++ b/solution.py
@@ -35,6 +35,10 @@
     return [0] + list(range(n - 1, 0, -1))
 
 
+def chips(n):
+    return list(range(n - 2, 0, -2))
+
+
 def column_of(row):
     n = row.shape[1]
     eye = lax.broadcasted_iota(jnp.int32, (n, n), 0) == lax.broadcasted_iota(jnp.int32, (n, n), 1)
@@ -51,8 +55,9 @@
 def pack_kernel(dims, with_data, *refs):
     n, stations, slots, components, taps, most, rows = dims
     ins = refs[: 5 if with_data else 4]
-    send_refs = refs[len(ins) : len(ins) + n]
-    held = refs[len(ins) + n : -1]
+    own_ref, core_ref, *chip_refs = refs[len(ins) : len(ins) + 1 + n // 2]
+    held = refs[len(ins) + 1 + n // 2 : -1]
+    block_rows = own_ref.shape[0]
     sems = refs[-1]
     copies = [pltpu.make_async_copy(ins[i], held[i], sems.at[i]) for i in range(len(ins))]
     for copy in copies:
@@ -109,9 +114,12 @@
     if with_data:
         samples = held[0][...].astype(jnp.float32)
         samples = samples.reshape(samples.shape[0] * samples.shape[1], LANES)
-        extra = send_refs[0].shape[0] - (components * whole + tails) * rows - samples.shape[0]
+        extra = block_rows - (components * whole + tails) * rows - samples.shape[0]
         samples = jnp.concatenate([samples, jnp.zeros((extra, LANES), jnp.float32)], axis=0)
-    for g, send_ref in zip(partners(n), send_refs):
+    to = [(0, own_ref, 0), (1, core_ref, 0)]
+    for d, ref in zip(chips(n), chip_refs):
+        to += [(d, ref, 0), (d + 1, ref, block_rows)]
+    for g, send_ref, at in to:
         mine = slice(g * rows, (g + 1) * rows)
         pieces = [
             placed[c][mine, a * LANES : (a + 1) * LANES] for c in range(components) for a in range(whole)
@@ -119,7 +127,7 @@
         pieces += [ends[mine, e * LANES : (e + 1) * LANES] for e in range(tails)]
         if with_data:
             pieces.append(samples)
-        send_ref[...] = jnp.concatenate(pieces, axis=0).astype(jnp.bfloat16)
+        send_ref[at : at + block_rows, :] = jnp.concatenate(pieces, axis=0).astype(jnp.bfloat16)
 
 
 def correlate_kernel(dims, with_data, *refs):
@@ -128,7 +136,12 @@
     else:
         data_ref, mask_ref, *refs = refs
     n, stations, blocks, components, taps, most, rows, width, per_group = dims
-    recv_refs, refs = refs[:n], refs[n:]
+    own_ref, core_ref, *chip_refs = refs[:n]
+    refs = refs[n:]
+    block_rows = own_ref.shape[0]
+    come = [(0, own_ref, 0), (1, core_ref, 0)]
+    for i, d in enumerate(chips(n)):
+        come += [(d, chip_refs[i], 0), (d + 1, chip_refs[n // 2 - 1 + i], block_rows)]
     *out_refs, x_ref, dsh_ref, rd_ref, ws_ref, rw_ref, meta_ref, sh_ref, stack_ref = refs
     whole, tail, per_tail, tails = chunk_plan(taps, components)
     chunks = whole + 1
@@ -142,8 +155,9 @@
 
     if with_data:
         first = sent * rows
-        for d, recv_ref in zip(partners(n), recv_refs):
-            x_ref[lax.axis_index("tmpl") ^ d] = recv_ref[first:, :].astype(jnp.float32)[:series_rows]
+        for d, ref, at in come:
+            samples = ref[at + first : at + block_rows, :].astype(jnp.float32)
+            x_ref[lax.axis_index("tmpl") ^ d] = samples[:series_rows]
         x = jnp.concatenate([x_ref[i] for i in range(n)], axis=1)
     else:
         x = data_ref[...].astype(jnp.float32)
@@ -192,7 +206,7 @@
     )
     order = jnp.where(source == wanted, 1.0, 0.0).astype(jnp.bfloat16)
     lane = lax.broadcasted_iota(jnp.int32, (stations * here, LANES), 1)
-    blocks_in = [ref[: ceil_to(sent * rows, 16), :].astype(jnp.float32) for ref in recv_refs]
+    blocks_in = [ref[at : at + ceil_to(sent * rows, 16), :].astype(jnp.float32) for _, ref, at in come]
 
     def received(k):
         piece = jnp.concatenate([blocks_in[i][k * rows : (k + 1) * rows] for i in range(n)], axis=0)
@@ -313,17 +327,20 @@
         functools.partial(
             pack_kernel, (n, stations, slots, components, taps, most, rows), with_data
         ),
-        out_shape=[jax.ShapeDtypeStruct((block_rows, LANES), jnp.bfloat16)] * n,
+        out_shape=[jax.ShapeDtypeStruct((block_rows, LANES), jnp.bfloat16)] * 2
+        + [jax.ShapeDtypeStruct((2 * block_rows, LANES), jnp.bfloat16)] * (n // 2 - 1),
         in_specs=[pl.BlockSpec(memory_space=pltpu.HBM)] * len(ins),
         scratch_shapes=[pltpu.VMEM(x.shape, x.dtype) for x in ins]
         + [pltpu.SemaphoreType.DMA((len(ins),))],
         compiler_params=pltpu.CompilerParams(vmem_limit_bytes=24 << 20),
         name="pack",
     )(*ins)
-    received = [
-        lax.ppermute(block, "tmpl", [(i, i ^ d) for i in range(n)]) if d else block
-        for d, block in zip(partners(n), send)
-    ]
+    def swap(block, d):
+        return lax.ppermute(block, "tmpl", [(i, i ^ d) for i in range(n)])
+
+    own, for_core, *for_chips = send
+    from_chips = [swap(block, d) for d, block in zip(chips(n), for_chips)]
+    received = [own, swap(for_core, 1)] + from_chips + [swap(block, 1) for block in from_chips]
     if not with_data:
         samples = lax.all_gather(samples.reshape(series, width_here), "tmpl", axis=1, tiled=True)
     vmem = pl.BlockSpec(memory_space=pltpu.VMEM)

time: 28.8 us -> 29.1 us (1.010)
  waiting for transfers between devices: 7.13 us -> 10.5 us
  starting transfers between devices: 12.7 us -> 9.63 us
    ppermute x7, waiting for transfers between devices: 3.16 us -> 6.46 us  [swap(): return lax.ppermute(block, 'tmpl', [(i, i ^ d) for i in range(n)])]
    ppermute x7, starting transfers between devices: 8.2 us -> 5.13 us  [swap(): return lax.ppermute(block, 'tmpl', [(i, i ^ d) for i in range(n)])]
where the time goes in v5:
time: 29.1 us; the launch traced here: 28.9 us
  waiting for transfers between devices  10.5 us (36%)
  starting transfers between devices  9.63 us (33%)
  Pallas kernels  8.68 us (30%)
    pallas_call x1, Pallas kernels, body(): pl.pallas_call(functools.partial(correlate_kernel, (n, stations, blocks,...  6.5 us
    ppermute x7, waiting for transfers between devices, swap(): return lax.ppermute(block, 'tmpl', [(i, i ^ d) for i in range(n)])  6.46 us
    ppermute x7, starting transfers between devices, swap(): return lax.ppermute(block, 'tmpl', [(i, i ^ d) for i in range(n)])  5.13 us
    ppermute x3, starting transfers between devices, body(): lax.ppermute(part, 'stn', [(i, i ^ d) for i in range(owners)])  4.5 us
    ppermute x3, waiting for transfers between devices, body(): lax.ppermute(part, 'stn', [(i, i ^ d) for i in range(owners)])  4.04 us
    pallas_call x1, Pallas kernels, body(): pl.pallas_call(functools.partial(pack_kernel, (n, stations, slots, compon...  1.41 us
    pallas_call x1, Pallas kernels, body(): pl.pallas_call(functools.partial(finish_kernel, taps, blocks), out_shape=...  0.78 us
  transfers between devices with their start and end apart: 10, of which 6 were waited for; matrix products, arithmetic and copies ran while one was open for 0% of the time, Pallas kernels for 0%

profile of v5, /device:TPU:0, one launch (start us, length us, event | category | flops | bytes accessed | tf_op | source)
XLA Modules:
  0.0 28.9 jit_solution(14905768895065620104)
XLA Ops:
  0.0 1.4 %pack.1 = (bf16[240,128]{1,0:T(8,128)(2,1)S(1)}, bf16[240,128]{1,0:T(8,128)(2,1)S(1)}, bf16[480,128]{1,0:T(8,128)(2,1)S(1)}, bf16[480,128]{1,0:T(8,128)(2,1)S(1)}, bf16[480,128]{1,0:T(8,128)(2,1)S(1)}) custom-call(bf16[18,2,128]{2,1,0:T(2,128)(2,1)} %bitcast.8, bf16[18,16,300]{2,1,0:T(8,128)(2,1)} %bitcast.7, s32[6,1,16]{2,1,0:T(1,128)} %bitcast.9, ...), custom_call_target="tpu_custom_call" | custom-call | tf_op jit(solution)/shard_map/pack/pallas_call | solution.py:326
  1.4 4.0 %collective-permute-start.1 = (bf16[480,128]{1,0:T(8,128)(2,1)S(1)}, bf16[480,128]{1,0:T(8,128)(2,1)S(1)}, u32[]{:S(2)}, u32[]{:S(2)}) collective-permute-start(bf16[480,128]{1,0:T(8,128)(2,1)S(1)} %get-tuple-element.16), channel_id=1, source_target_pairs={{0,24},{4,28},{8,16},{12,20},{16,8},{20,12},{24,0},{28,4},{1,25},{... | collective-permute-start | bytes 368648 | tf_op jit(solution)/shard_map/ppermute | solution.py:339
  5.4 0.0 copy-start
  5.4 0.5 %collective-permute-start.2 = (bf16[480,128]{1,0:T(8,128)(2,1)S(1)}, bf16[480,128]{1,0:T(8,128)(2,1)S(1)}, u32[]{:S(2)}, u32[]{:S(2)}) collective-permute-start(bf16[480,128]{1,0:T(8,128)(2,1)S(1)} %get-tuple-element.17), channel_id=1, source_target_pairs={{0,16},{4,20},{8,24},{12,28},{16,0},{20,4},{24,8},{28,12},{1,17},{... | collective-permute-start | bytes 368648 | tf_op jit(solution)/shard_map/ppermute | solution.py:339
  5.9 0.1 collective-permute-start.3
  6.0 3.1 %collective-permute-done.1.refs_3_ = bf16[480,128]{1,0:T(8,128)(2,1)S(1)} collective-permute-done((bf16[480,128]{1,0:T(8,128)(2,1)S(1)}, bf16[480,128]{1,0:T(8,128)(2,1)S(1)}, u32[]{:S(2)}, u32[]{:S(2)}) %collective-permute-start.1) | collective-permute-done | bytes 122912 | tf_op jit(solution)/shard_map/ppermute | solution.py:339
  9.1 0.0 collective-permute-start.4
  9.1 2.2 %collective-permute-done.2.refs_4_ = bf16[480,128]{1,0:T(8,128)(2,1)S(1)} collective-permute-done((bf16[480,128]{1,0:T(8,128)(2,1)S(1)}, bf16[480,128]{1,0:T(8,128)(2,1)S(1)}, u32[]{:S(2)}, u32[]{:S(2)}) %collective-permute-start.2) | collective-permute-done | bytes 122912 | tf_op jit(solution)/shard_map/ppermute | solution.py:339
  11.3 0.0 collective-permute-start.5
  11.3 0.2 collective-permute-done.3.refs_5_
  11.6 0.3 collective-permute-start.6
  11.9 0.2 collective-permute-start
  12.1 0.0 copy-done
  12.1 0.1 copy.7.refs_0_
  12.2 0.9 %collective-permute-done.refs_2_ = bf16[240,128]{1,0:T(8,128)(2,1)S(1)} collective-permute-done((bf16[240,128]{1,0:T(8,128)(2,1)S(1)}, bf16[240,128]{1,0:T(8,128)(2,1)S(1)}, u32[]{:S(2)}, u32[]{:S(2)}) %collective-permute-start) | collective-permute-done | bytes 61472 | tf_op jit(solution)/shard_map/ppermute | solution.py:339
  13.1 0.0 collective-permute-done.4.refs_6_
  13.1 0.0 collective-permute-done.5.refs_7_
  13.1 0.0 collective-permute-done.6.refs_8_
  13.1 6.5 %correlate.1 = (bf16[16,640]{1,0:T(8,128)(2,1)S(1)}, bf16[16,640]{1,0:T(8,128)(2,1)S(1)}, bf16[16,640]{1,0:T(8,128)(2,1)S(1)}, bf16[16,640]{1,0:T(8,128)(2,1)S(1)}) custom-call(s32[6,3]{1,0:T(8,128)S(1)} %copy.7.refs_0_, bf16[240,128]{1,0:T(8,128)(2,1)S(1)} %get-tuple-element.14.refs_1_, bf16[240,128]{1,0:T(8,128)(2,1)S(1)} %collective-permute-done.refs_2_, ...), custom_call_target="tpu_custom_call" | custom-call | tf_op jit(solution)/shard_map/correlate/pallas_call | solution.py:347
  19.6 3.9 %collective-permute-start.7 = (bf16[16,640]{1,0:T(8,128)(2,1)S(1)}, bf16[16,640]{1,0:T(8,128)(2,1)S(1)}, u32[]{:S(2)}, u32[]{:S(2)}) collective-permute-start(bf16[16,640]{1,0:T(8,128)(2,1)S(1)} %get-tuple-element.20), channel_id=1, source_target_pairs={{0,3},{1,2},{2,1},{3,0},{4,7},{5,6},{6,5},{7,4},{8,11},{9,10},{10,... | collective-permute-start | bytes 61448 | tf_op jit(solution)/shard_map/ppermute | solution.py:369
  23.5 0.0 collective-permute-start.8
  23.5 0.6 %collective-permute-start.9 = (bf16[16,640]{1,0:T(8,128)(2,1)S(1)}, bf16[16,640]{1,0:T(8,128)(2,1)S(1)}, u32[]{:S(2)}, u32[]{:S(2)}) collective-permute-start(bf16[16,640]{1,0:T(8,128)(2,1)S(1)} %get-tuple-element.22), channel_id=1, source_target_pairs={{0,1},{1,0},{2,3},{3,2},{4,5},{5,4},{6,7},{7,6},{8,9},{9,8},{10,11... | collective-permute-start | bytes 61448 | tf_op jit(solution)/shard_map/ppermute | solution.py:369
  24.1 1.1 %collective-permute-done.7.refs_1_ = bf16[16,640]{1,0:T(8,128)(2,1)S(1)} collective-permute-done((bf16[16,640]{1,0:T(8,128)(2,1)S(1)}, bf16[16,640]{1,0:T(8,128)(2,1)S(1)}, u32[]{:S(2)}, u32[]{:S(2)}) %collective-permute-start.7) | collective-permute-done | bytes 20512 | tf_op jit(solution)/shard_map/ppermute | solution.py:369
  25.3 2.9 %collective-permute-done.8.refs_2_ = bf16[16,640]{1,0:T(8,128)(2,1)S(1)} collective-permute-done((bf16[16,640]{1,0:T(8,128)(2,1)S(1)}, bf16[16,640]{1,0:T(8,128)(2,1)S(1)}, u32[]{:S(2)}, u32[]{:S(2)}) %collective-permute-start.8) | collective-permute-done | bytes 20512 | tf_op jit(solution)/shard_map/ppermute | solution.py:369
  28.2 0.0 collective-permute-done.9.refs_3_
  28.2 0.8 %finish.1 = f32[2,16,256]{2,1,0:T(8,128)} custom-call(bf16[16,640]{1,0:T(8,128)(2,1)S(1)} %get-tuple-element.19.refs_0_, bf16[16,640]{1,0:T(8,128)(2,1)S(1)} %collective-permute-done.7.refs_1_, bf16[16,640]{1,0:T(8,128)(2,1)S(1)} %collective-permute-done.8.refs_2_, bf16[16,640]{1,0:T(8,128)(2,1)S(1)} %collective-permute-done.9.refs_3_), custom_call_target="tpu_custom_call" | custom-call | tf_op jit(solution)/shard_map/finish/pallas_call | solution.py:372
Async XLA Ops:
  1.4 7.7 %collective-permute-start.1 = (bf16[480,128]{1,0:T(8,128)(2,1)S(1)}, bf16[480,128]{1,0:T(8,128)(2,1)S(1)}, u32[]{:S(2)}, u32[]{:S(2)}) collective-permute-start(bf16[480,128]{1,0:T(8,128)(2,1)S(1)} %get-tuple-element.16), channel_id=1, source_target_pairs={{0,24},{4,28},{8,16},{12,20},{16,8},{20,12},{24,0},{28,4},{1,25},{... | collective-permute-start | bytes 368648 | tf_op jit(solution)/shard_map/ppermute | solution.py:339
  5.4 6.7 %copy-start = (s32[6,3]{0,1:T(4,128)S(1)}, s32[6,3]{0,1:T(4,128)}, u32[]{:S(2)}) copy-start(s32[6,3]{0,1:T(4,128)} %param.11) | copy-start | bytes 220
  5.4 6.0 %collective-permute-start.2 = (bf16[480,128]{1,0:T(8,128)(2,1)S(1)}, bf16[480,128]{1,0:T(8,128)(2,1)S(1)}, u32[]{:S(2)}, u32[]{:S(2)}) collective-permute-start(bf16[480,128]{1,0:T(8,128)(2,1)S(1)} %get-tuple-element.17), channel_id=1, source_target_pairs={{0,16},{4,20},{8,24},{12,28},{16,0},{20,4},{24,8},{28,12},{1,17},{... | collective-permute-start | bytes 368648 | tf_op jit(solution)/shard_map/ppermute | solution.py:339
  5.9 5.7 %collective-permute-start.3 = (bf16[480,128]{1,0:T(8,128)(2,1)S(1)}, bf16[480,128]{1,0:T(8,128)(2,1)S(1)}, u32[]{:S(2)}, u32[]{:S(2)}) collective-permute-start(bf16[480,128]{1,0:T(8,128)(2,1)S(1)} %get-tuple-element.18), channel_id=1, source_target_pairs={{0,8},{4,12},{8,0},{12,4},{16,24},{20,28},{24,16},{28,20},{1,9},{5... | collective-permute-start | bytes 368648 | tf_op jit(solution)/shard_map/ppermute | solution.py:339
  9.1 4.0 %collective-permute-start.4 = (bf16[480,128]{1,0:T(8,128)(2,1)S(1)}, bf16[480,128]{1,0:T(8,128)(2,1)S(1)}, u32[]{:S(2)}, u32[]{:S(2)}) collective-permute-start(bf16[480,128]{1,0:T(8,128)(2,1)S(1)} %collective-permute-done.1.refs_3_), channel_id=1, source_target_pairs={{0,4},{4,0},{8,12},{12,8},{16,20},{20,16},{24,28},{28,24},{1,5},{5... | collective-permute-start | bytes 368648 | tf_op jit(solution)/shard_map/ppermute | solution.py:339
  11.3 1.8 %collective-permute-start.5 = (bf16[480,128]{1,0:T(8,128)(2,1)S(1)}, bf16[480,128]{1,0:T(8,128)(2,1)S(1)}, u32[]{:S(2)}, u32[]{:S(2)}) collective-permute-start(bf16[480,128]{1,0:T(8,128)(2,1)S(1)} %collective-permute-done.2.refs_4_), channel_id=1, source_target_pairs={{0,4},{4,0},{8,12},{12,8},{16,20},{20,16},{24,28},{28,24},{1,5},{5... | collective-permute-start | bytes 368648 | tf_op jit(solution)/shard_map/ppermute | solution.py:339
  11.6 1.5 %collective-permute-start.6 = (bf16[480,128]{1,0:T(8,128)(2,1)S(1)}, bf16[480,128]{1,0:T(8,128)(2,1)S(1)}, u32[]{:S(2)}, u32[]{:S(2)}) collective-permute-start(bf16[480,128]{1,0:T(8,128)(2,1)S(1)} %collective-permute-done.3.refs_5_), channel_id=1, source_target_pairs={{0,4},{4,0},{8,12},{12,8},{16,20},{20,16},{24,28},{28,24},{1,5},{5... | collective-permute-start | bytes 368648 | tf_op jit(solution)/shard_map/ppermute | solution.py:339
  11.9 1.2 %collective-permute-start = (bf16[240,128]{1,0:T(8,128)(2,1)S(1)}, bf16[240,128]{1,0:T(8,128)(2,1)S(1)}, u32[]{:S(2)}, u32[]{:S(2)}) collective-permute-start(bf16[240,128]{1,0:T(8,128)(2,1)S(1)} %get-tuple-element.15), channel_id=1, source_target_pairs={{0,4},{4,0},{8,12},{12,8},{16,20},{20,16},{24,28},{28,24},{1,5},{5... | collective-permute-start | bytes 184328 | tf_op jit(solution)/shard_map/ppermute | solution.py:339
  19.6 5.6 %collective-permute-start.7 = (bf16[16,640]{1,0:T(8,128)(2,1)S(1)}, bf16[16,640]{1,0:T(8,128)(2,1)S(1)}, u32[]{:S(2)}, u32[]{:S(2)}) collective-permute-start(bf16[16,640]{1,0:T(8,128)(2,1)S(1)} %get-tuple-element.20), channel_id=1, source_target_pairs={{0,3},{1,2},{2,1},{3,0},{4,7},{5,6},{6,5},{7,4},{8,11},{9,10},{10,... | collective-permute-start | bytes 61448 | tf_op jit(solution)/shard_map/ppermute | solution.py:369
  23.5 4.7 %collective-permute-start.8 = (bf16[16,640]{1,0:T(8,128)(2,1)S(1)}, bf16[16,640]{1,0:T(8,128)(2,1)S(1)}, u32[]{:S(2)}, u32[]{:S(2)}) collective-permute-start(bf16[16,640]{1,0:T(8,128)(2,1)S(1)} %get-tuple-element.21), channel_id=1, source_target_pairs={{0,2},{1,3},{2,0},{3,1},{4,6},{5,7},{6,4},{7,5},{8,10},{9,11},{10,... | collective-permute-start | bytes 61448 | tf_op jit(solution)/shard_map/ppermute | solution.py:369
  23.5 4.7 %collective-permute-start.9 = (bf16[16,640]{1,0:T(8,128)(2,1)S(1)}, bf16[16,640]{1,0:T(8,128)(2,1)S(1)}, u32[]{:S(2)}, u32[]{:S(2)}) collective-permute-start(bf16[16,640]{1,0:T(8,128)(2,1)S(1)} %get-tuple-element.22), channel_id=1, source_target_pairs={{0,1},{1,0},{2,3},{3,2},{4,5},{5,4},{6,7},{7,6},{8,9},{9,8},{10,11... | collective-permute-start | bytes 61448 | tf_op jit(solution)/shard_map/ppermute | solution.py:369

commit v6 on v5

--- a/solution.py
+++ b/solution.py
@@ -45,11 +45,16 @@
     return jnp.sum(jnp.where(eye, jnp.broadcast_to(row, (n, n)), 0), axis=1, keepdims=True)
 
 
+SMALL = 8
+EXTRAS = 4
+
+
 def chunk_plan(taps, components):
     whole = taps // LANES
     tail = taps - whole * LANES
-    per_tail = (LANES - 3) // tail
-    return whole, tail, per_tail, ceil_to(components, per_tail) // per_tail
+    left = components * tail - LANES
+    assert 0 < left <= min(tail, SMALL - 3)
+    return whole, tail, left
 
 
 def pack_kernel(dims, with_data, *refs):
@@ -57,14 +62,13 @@
     ins = refs[: 5 if with_data else 4]
     own_ref, core_ref, *chip_refs = refs[len(ins) : len(ins) + 1 + n // 2]
     held = refs[len(ins) + 1 + n // 2 : -1]
-    block_rows = own_ref.shape[0]
     sems = refs[-1]
     copies = [pltpu.make_async_copy(ins[i], held[i], sems.at[i]) for i in range(len(ins))]
     for copy in copies:
         copy.start()
     waves_ref, group_ref, local_ref, moveout_ref = held[-4:]
     count = stations * slots
-    whole, tail, per_tail, tails = chunk_plan(taps, components)
+    whole, tail, left = chunk_plan(taps, components)
 
     def flat(ref, three):
         pieces = [ref[s] if three else ref[s : s + 1, :] for s in range(stations)]
@@ -87,10 +91,7 @@
     place = jnp.where(place, 1.0, 0.0).astype(jnp.bfloat16)
 
     lane = lax.broadcasted_iota(jnp.int32, (count, LANES), 1)
-    meta = jnp.where(lane == LANES - 1, column_of(local) + 1, 0)
-    meta = jnp.where(lane == LANES - 2, column_of(quotient(moveout, LANES)), meta)
-    meta = jnp.where(lane == LANES - 3, column_of(remainder(moveout, LANES)), meta)
-    meta = meta.astype(jnp.float32).astype(jnp.bfloat16)
+    meta = [column_of(local) + 1, column_of(quotient(moveout, LANES)), column_of(remainder(moveout, LANES))]
 
     for copy in copies[:-3]:
         copy.wait()
@@ -102,32 +103,42 @@
         jnp.dot(place, waves[c][:, : whole * LANES], preferred_element_type=jnp.float32)
         for c in range(components)
     ]
-    ends = []
-    for e in range(tails):
-        pieces = [waves[c][:, whole * LANES :] for c in range(e * per_tail, min((e + 1) * per_tail, components))]
-        used = tail * len(pieces)
-        pieces.append(
-            meta[:, used:] if e == 0 else jnp.zeros((count, LANES - used), jnp.bfloat16)
-        )
-        ends.append(jnp.concatenate(pieces, axis=1))
+    ends = [waves[c][:, whole * LANES :] for c in range(components - 1)]
+    ends.append(waves[-1][:, whole * LANES : taps - left])
     ends = jnp.dot(place, jnp.concatenate(ends, axis=1), preferred_element_type=jnp.float32)
+    small = [waves[-1][:, taps - left + v : taps - left + v + 1] for v in range(left)] + meta
+    spread = jnp.zeros((count, LANES), jnp.float32)
+    for v, column in enumerate(small):
+        spread = jnp.where(remainder(lane, SMALL) == v, column.astype(jnp.float32), spread)
+    spread = jnp.dot(place, spread.astype(jnp.bfloat16), preferred_element_type=jnp.float32)
+    each = LANES // SMALL
+    within = remainder(lax.broadcasted_iota(jnp.int32, (rows, LANES), 0), each)
+    within = within == quotient(lax.broadcasted_iota(jnp.int32, (rows, LANES), 1), SMALL)
     if with_data:
         samples = held[0][...].astype(jnp.float32)
         samples = samples.reshape(samples.shape[0] * samples.shape[1], LANES)
-        extra = block_rows - (components * whole + tails) * rows - samples.shape[0]
-        samples = jnp.concatenate([samples, jnp.zeros((extra, LANES), jnp.float32)], axis=0)
-    to = [(0, own_ref, 0), (1, core_ref, 0)]
-    for d, ref in zip(chips(n), chip_refs):
-        to += [(d, ref, 0), (d + 1, ref, block_rows)]
-    for g, send_ref, at in to:
-        mine = slice(g * rows, (g + 1) * rows)
-        pieces = [
-            placed[c][mine, a * LANES : (a + 1) * LANES] for c in range(components) for a in range(whole)
-        ]
-        pieces += [ends[mine, e * LANES : (e + 1) * LANES] for e in range(tails)]
-        if with_data:
-            pieces.append(samples)
-        send_ref[at : at + block_rows, :] = jnp.concatenate(pieces, axis=0).astype(jnp.bfloat16)
+        samples = jnp.concatenate([samples, jnp.zeros((EXTRAS, LANES), jnp.float32)], axis=0)
+    else:
+        samples = jnp.zeros((8, LANES), jnp.float32)
+    line = lax.broadcasted_iota(jnp.int32, samples.shape, 0)
+    messages = [(own_ref, [0]), (core_ref, [1])]
+    messages += [(ref, [d, d + 1]) for d, ref in zip(chips(n), chip_refs)]
+    for send_ref, groups in messages:
+        pieces, last = [], samples
+        for g in groups:
+            mine = slice(g * rows, (g + 1) * rows)
+            for c in range(components):
+                pieces += [placed[c][mine, a * LANES : (a + 1) * LANES] for a in range(whole)]
+            pieces.append(ends[mine])
+            kept = jnp.where(within, spread[mine], 0.0)
+            for e in range(-(-rows // each)):
+                packed = jnp.sum(kept[e * each : (e + 1) * each], axis=0, keepdims=True)
+                last = jnp.where(line == samples.shape[0] - EXTRAS + 2 * (g % 2) + e, packed, last)
+        pieces.append(last)
+        extra = send_ref.shape[0] - sum(piece.shape[0] for piece in pieces)
+        if extra:
+            pieces.append(jnp.zeros((extra, LANES), jnp.float32))
+        send_ref[...] = jnp.concatenate(pieces, axis=0).astype(jnp.bfloat16)
 
 
 def correlate_kernel(dims, with_data, *refs):
@@ -138,14 +149,16 @@
     n, stations, blocks, components, taps, most, rows, width, per_group = dims
     own_ref, core_ref, *chip_refs = refs[:n]
     refs = refs[n:]
-    block_rows = own_ref.shape[0]
-    come = [(0, own_ref, 0), (1, core_ref, 0)]
-    for i, d in enumerate(chips(n)):
-        come += [(d, chip_refs[i], 0), (d + 1, chip_refs[n // 2 - 1 + i], block_rows)]
+    come = [(own_ref, 0, 1), (core_ref, 0, 1)]
+    for i in range(n // 2 - 1):
+        come += [(chip_refs[i], 0, 2), (chip_refs[n // 2 - 1 + i], 1, 2)]
+    distances = [0, 1]
+    for d in chips(n):
+        distances += [d, d + 1]
     *out_refs, x_ref, dsh_ref, rd_ref, ws_ref, rw_ref, meta_ref, sh_ref, stack_ref = refs
-    whole, tail, per_tail, tails = chunk_plan(taps, components)
+    whole, tail, left = chunk_plan(taps, components)
     chunks = whole + 1
-    sent = components * whole + tails
+    sent = components * whole + 1
     total = n * rows
     here = n * most
     lag_tiles = ceil_to(width - taps + 1, LANES) // LANES
@@ -153,11 +166,17 @@
     series = stations * components * blocks
     series_rows = ceil_to(series, 8)
 
+    def lines(ref, start, count):
+        first = start // 16 * 16
+        return ref[first : ceil_to(start + count, 16), :].astype(jnp.float32)[start - first :][:count]
+
+    last_rows = series + EXTRAS if with_data else 8
+    blocks_in = [lines(ref, half * sent * rows, sent * rows) for ref, half, _ in come]
+    lasts = [lines(ref, count * sent * rows, last_rows) for ref, _, count in come]
+
     if with_data:
-        first = sent * rows
-        for d, ref, at in come:
-            samples = ref[at + first : at + block_rows, :].astype(jnp.float32)
-            x_ref[lax.axis_index("tmpl") ^ d] = samples[:series_rows]
+        for d, last in zip(distances, lasts):
+            x_ref[lax.axis_index("tmpl") ^ d] = last
         x = jnp.concatenate([x_ref[i] for i in range(n)], axis=1)
     else:
         x = data_ref[...].astype(jnp.float32)
@@ -206,18 +225,34 @@
     )
     order = jnp.where(source == wanted, 1.0, 0.0).astype(jnp.bfloat16)
     lane = lax.broadcasted_iota(jnp.int32, (stations * here, LANES), 1)
-    blocks_in = [ref[at : at + ceil_to(sent * rows, 16), :].astype(jnp.float32) for _, ref, at in come]
-
     def received(k):
         piece = jnp.concatenate([blocks_in[i][k * rows : (k + 1) * rows] for i in range(n)], axis=0)
         return jnp.dot(order, piece.astype(jnp.bfloat16), preferred_element_type=jnp.float32)
 
-    ends = [received(components * whole + e) for e in range(tails)]
-    meta_ref[...] = ends[0]
+    each = LANES // SMALL
+    target = lax.broadcasted_iota(jnp.int32, (stations * here, n * 8), 0)
+    place = quotient(target, here) * most + remainder(target, most)
+    sender = quotient(remainder(target, here), most)
+    line = sender * 8 + (8 - EXTRAS) + 2 * remainder(sender, 2) + quotient(place, each)
+    line = lax.broadcasted_iota(jnp.int32, (stations * here, n * 8), 1) == line
+    small = jnp.concatenate([last[last_rows - 8 :] for last in lasts], axis=0).astype(jnp.bfloat16)
+    small = jnp.dot(
+        jnp.where(line, 1.0, 0.0).astype(jnp.bfloat16), small, preferred_element_type=jnp.float32
+    )
+    target = lax.broadcasted_iota(jnp.int32, (stations * here, LANES), 0)
+    place = remainder(quotient(target, here) * most + remainder(target, most), each)
+    small = jnp.where(quotient(lane, SMALL) == place, small, 0.0).astype(jnp.bfloat16)
+    fold = lax.broadcasted_iota(jnp.int32, (LANES, LANES), 0)
+    fold = remainder(fold, SMALL) == lax.broadcasted_iota(jnp.int32, (LANES, LANES), 1)
+    fold = jnp.where(fold, 1.0, 0.0).astype(jnp.bfloat16)
+    meta_ref[...] = jnp.dot(small, fold, preferred_element_type=jnp.float32)
+
+    ends = received(components * whole)
     for c in range(components):
         pieces = [received(c * whole + a) for a in range(whole)]
-        end, before = ends[c // per_tail], (c % per_tail) * tail
-        end = pltpu.roll(end, LANES - before, 1) if before else end
+        end = pltpu.roll(ends, LANES - c * tail, 1) if c else ends
+        if c == components - 1:
+            end = jnp.where(lane < tail - left, end, pltpu.roll(meta_ref[...], tail - left, 1))
         pieces.append(jnp.where(lane < tail, end, 0.0))
         squares = functools.reduce(lambda p, q: p + q, [piece * piece for piece in pieces])
         for a in range(chunks):
@@ -234,8 +269,8 @@
     for s in range(stations):
         rows_here = slice(s * here, (s + 1) * here)
         meta = meta_ref[rows_here, :]
-        tiles_over = meta[:, LANES - 2 : LANES - 1].astype(jnp.int32)
-        lanes_over = meta[:, LANES - 3 : LANES - 2].astype(jnp.int32)
+        tiles_over = meta[:, left + 1 : left + 2].astype(jnp.int32)
+        lanes_over = meta[:, left + 2 : left + 3].astype(jnp.int32)
         index = lane_here + lanes_over
         within = index < LANES
         index = jnp.bitwise_and(index, LANES - 1)
@@ -278,7 +313,7 @@
     slot = lax.broadcasted_iota(jnp.int32, (stations * here, LANES), 0)
     half = (slot < stations * here // 2) == (lane < LANES // 2)
     sh_ref[:, blocks * NK :] = jnp.where(half, 1.0, 0.0).astype(jnp.bfloat16)
-    local = meta_ref[:, LANES - 1 :].astype(jnp.int32) - 1
+    local = meta_ref[:, left : left + 1].astype(jnp.int32) - 1
     template = lax.broadcasted_iota(jnp.int32, (stations * here, per_group), 1)
     onehot = jnp.where(local == template, 1.0, 0.0).astype(jnp.bfloat16)
     stack_ref[...] = lax.dot_general(
@@ -310,7 +345,7 @@
     width = width_here * n
     most = max(2, 2 * slots // n)
     rows = ceil_to(stations * most, 8)
-    whole, tail, per_tail, tails = chunk_plan(taps, components)
+    whole, tail, left = chunk_plan(taps, components)
     series = stations * components * blocks
     series_rows = ceil_to(series, 8)
     with_data = width_here == LANES
@@ -319,16 +354,16 @@
     waves = jnp.transpose(waves, (0, 2, 1, 3)).reshape(stations * components, slots, taps)
     groups = jnp.transpose(slot_group, (0, 2, 1))
     samples = jnp.transpose(data, (1, 2, 0, 3)).reshape(stations * components, blocks, width_here)
-    block_rows = (components * whole + tails) * rows + (series_rows if with_data else 0)
-    block_rows = ceil_to(block_rows, 16)
+    last_rows = series + EXTRAS if with_data else 8
+    message_rows = [ceil_to(k * (components * whole + 1) * rows + last_rows, 16) for k in (1, 1)]
+    message_rows += [ceil_to(2 * (components * whole + 1) * rows + last_rows, 16)] * (n // 2 - 1)
     ins = ([samples] if with_data else []) + [waves, groups, slot_local, moveout]
     ins = [pltpu.with_memory_space_constraint(x, pltpu.HBM) for x in ins]
     send = pl.pallas_call(
         functools.partial(
             pack_kernel, (n, stations, slots, components, taps, most, rows), with_data
         ),
-        out_shape=[jax.ShapeDtypeStruct((block_rows, LANES), jnp.bfloat16)] * 2
-        + [jax.ShapeDtypeStruct((2 * block_rows, LANES), jnp.bfloat16)] * (n // 2 - 1),
+        out_shape=[jax.ShapeDtypeStruct((k, LANES), jnp.bfloat16) for k in message_rows],
         in_specs=[pl.BlockSpec(memory_space=pltpu.HBM)] * len(ins),
         scratch_shapes=[pltpu.VMEM(x.shape, x.dtype) for x in ins]
         + [pltpu.SemaphoreType.DMA((len(ins),))],
@@ -340,7 +375,10 @@
 
     own, for_core, *for_chips = send
     from_chips = [swap(block, d) for d, block in zip(chips(n), for_chips)]
-    received = [own, swap(for_core, 1)] + from_chips + [swap(block, 1) for block in from_chips]
+    from_core = swap(for_core, 1)
+    if from_chips:
+        from_chips[0], from_core = lax.optimization_barrier((from_chips[0], from_core))
+    received = [own, from_core] + from_chips + [swap(block, 1) for block in from_chips]
     if not with_data:
         samples = lax.all_gather(samples.reshape(series, width_here), "tmpl", axis=1, tiled=True)
     vmem = pl.BlockSpec(memory_space=pltpu.VMEM)

time: 29.1 us -> 28 us (0.962)
  waiting for transfers between devices: 10.5 us -> 9.59 us
  starting transfers between devices: 9.63 us -> 9.26 us
    ppermute x7, waiting for transfers between devices: 6.46 us -> 5.59 us  [swap(): return lax.ppermute(block, 'tmpl', [(i, i ^ d) for i in range(n)])]
    ppermute x7, starting transfers between devices: 5.13 us -> 4.8 us  [swap(): return lax.ppermute(block, 'tmpl', [(i, i ^ d) for i in range(n)])]
  transfers between devices with their start and end apart: 10 -> 10, of which waited for: 6 -> 8; matrix products, arithmetic and copies ran while one was open for 0% -> 0% of each run, Pallas kernels for 0% -> 0%
where the time goes in v6:
time: 28 us; the launch traced here: 27.8 us
  waiting for transfers between devices  9.59 us (34%)
  starting transfers between devices  9.26 us (33%)
  Pallas kernels  8.83 us (32%)
    pallas_call x1, Pallas kernels, body(): pl.pallas_call(functools.partial(correlate_kernel, (n, stations, blocks,...  6.61 us
    ppermute x7, waiting for transfers between devices, swap(): return lax.ppermute(block, 'tmpl', [(i, i ^ d) for i in range(n)])  5.59 us
    ppermute x7, starting transfers between devices, swap(): return lax.ppermute(block, 'tmpl', [(i, i ^ d) for i in range(n)])  4.8 us
    ppermute x3, starting transfers between devices, body(): lax.ppermute(part, 'stn', [(i, i ^ d) for i in range(owners)])  4.45 us
    ppermute x3, waiting for transfers between devices, body(): lax.ppermute(part, 'stn', [(i, i ^ d) for i in range(owners)])  4.01 us
    pallas_call x1, Pallas kernels, body(): pl.pallas_call(functools.partial(pack_kernel, (n, stations, slots, compon...  1.45 us
    pallas_call x1, Pallas kernels, body(): pl.pallas_call(functools.partial(finish_kernel, taps, blocks), out_shape=...  0.78 us
  transfers between devices with their start and end apart: 10, of which 8 were waited for; matrix products, arithmetic and copies ran while one was open for 0% of the time, Pallas kernels for 0%

profile of v6, /device:TPU:0, one launch (start us, length us, event | category | flops | bytes accessed | tf_op | source)
XLA Modules:
  0.0 27.8 jit_solution(16941109811329390537)
XLA Ops:
  0.0 1.4 %pack.1 = (bf16[208,128]{1,0:T(8,128)(2,1)S(1)}, bf16[208,128]{1,0:T(8,128)(2,1)S(1)}, bf16[384,128]{1,0:T(8,128)(2,1)S(1)}, bf16[384,128]{1,0:T(8,128)(2,1)S(1)}, bf16[384,128]{1,0:T(8,128)(2,1)S(1)}) custom-call(bf16[18,2,128]{2,1,0:T(2,128)(2,1)} %bitcast.8, bf16[18,16,300]{2,1,0:T(8,128)(2,1)} %bitcast.7, s32[6,1,16]{2,1,0:T(1,128)} %bitcast.9, ...), custom_call_target="tpu_custom_call" | custom-call | tf_op jit(solution)/shard_map/pack/pallas_call | solution.py:362
  1.5 4.0 %collective-permute-start = (bf16[384,128]{1,0:T(8,128)(2,1)S(1)}, bf16[384,128]{1,0:T(8,128)(2,1)S(1)}, u32[]{:S(2)}, u32[]{:S(2)}) collective-permute-start(bf16[384,128]{1,0:T(8,128)(2,1)S(1)} %get-tuple-element.17), channel_id=1, source_target_pairs={{0,24},{4,28},{8,16},{12,20},{16,8},{20,12},{24,0},{28,4},{1,25},{... | collective-permute-start | bytes 294920 | tf_op jit(solution)/shard_map/ppermute | solution.py:374
  5.4 0.0 copy-start
  5.4 0.5 %collective-permute-start.2 = (bf16[384,128]{1,0:T(8,128)(2,1)S(1)}, bf16[384,128]{1,0:T(8,128)(2,1)S(1)}, u32[]{:S(2)}, u32[]{:S(2)}) collective-permute-start(bf16[384,128]{1,0:T(8,128)(2,1)S(1)} %get-tuple-element.21), channel_id=1, source_target_pairs={{0,16},{4,20},{8,24},{12,28},{16,0},{20,4},{24,8},{28,12},{1,17},{... | collective-permute-start | bytes 294920 | tf_op jit(solution)/shard_map/ppermute | solution.py:374
  5.9 0.1 collective-permute-start.3
  6.1 0.0 collective-permute-start.1
  6.1 1.2 %collective-permute-done.1.refs_2_ = bf16[208,128]{1,0:T(8,128)(2,1)S(1)} collective-permute-done((bf16[208,128]{1,0:T(8,128)(2,1)S(1)}, bf16[208,128]{1,0:T(8,128)(2,1)S(1)}, u32[]{:S(2)}, u32[]{:S(2)}) %collective-permute-start.1) | collective-permute-done | bytes 53280 | tf_op jit(solution)/shard_map/ppermute | solution.py:374
  7.3 1.3 %collective-permute-done.refs_3_ = bf16[384,128]{1,0:T(8,128)(2,1)S(1)} collective-permute-done((bf16[384,128]{1,0:T(8,128)(2,1)S(1)}, bf16[384,128]{1,0:T(8,128)(2,1)S(1)}, u32[]{:S(2)}, u32[]{:S(2)}) %collective-permute-start) | collective-permute-done | bytes 98336 | tf_op jit(solution)/shard_map/ppermute | solution.py:374
  8.6 0.0 collective-permute-start.4
  8.6 1.7 %collective-permute-done.2.refs_4_ = bf16[384,128]{1,0:T(8,128)(2,1)S(1)} collective-permute-done((bf16[384,128]{1,0:T(8,128)(2,1)S(1)}, bf16[384,128]{1,0:T(8,128)(2,1)S(1)}, u32[]{:S(2)}, u32[]{:S(2)}) %collective-permute-start.2) | collective-permute-done | bytes 98336 | tf_op jit(solution)/shard_map/ppermute | solution.py:374
  10.3 0.0 collective-permute-start.5
  10.3 0.3 %collective-permute-done.3.refs_5_ = bf16[384,128]{1,0:T(8,128)(2,1)S(1)} collective-permute-done((bf16[384,128]{1,0:T(8,128)(2,1)S(1)}, bf16[384,128]{1,0:T(8,128)(2,1)S(1)}, u32[]{:S(2)}, u32[]{:S(2)}) %collective-permute-start.3) | collective-permute-done | bytes 98336 | tf_op jit(solution)/shard_map/ppermute | solution.py:374
  10.6 0.2 collective-permute-start.6
  10.8 0.0 copy-done
  10.8 0.1 copy.7.refs_0_
  10.9 0.0 collective-permute-done.4.refs_6_
  10.9 0.7 %collective-permute-done.5.refs_7_ = bf16[384,128]{1,0:T(8,128)(2,1)S(1)} collective-permute-done((bf16[384,128]{1,0:T(8,128)(2,1)S(1)}, bf16[384,128]{1,0:T(8,128)(2,1)S(1)}, u32[]{:S(2)}, u32[]{:S(2)}) %collective-permute-start.5) | collective-permute-done | bytes 98336 | tf_op jit(solution)/shard_map/ppermute | solution.py:374
  11.6 0.3 %collective-permute-done.6.refs_8_ = bf16[384,128]{1,0:T(8,128)(2,1)S(1)} collective-permute-done((bf16[384,128]{1,0:T(8,128)(2,1)S(1)}, bf16[384,128]{1,0:T(8,128)(2,1)S(1)}, u32[]{:S(2)}, u32[]{:S(2)}) %collective-permute-start.6) | collective-permute-done | bytes 98336 | tf_op jit(solution)/shard_map/ppermute | solution.py:374
  11.9 6.6 %correlate.1 = (bf16[16,640]{1,0:T(8,128)(2,1)S(1)}, bf16[16,640]{1,0:T(8,128)(2,1)S(1)}, bf16[16,640]{1,0:T(8,128)(2,1)S(1)}, bf16[16,640]{1,0:T(8,128)(2,1)S(1)}) custom-call(s32[6,3]{1,0:T(8,128)S(1)} %copy.7.refs_0_, bf16[208,128]{1,0:T(8,128)(2,1)S(1)} %get-tuple-element.16.refs_1_, bf16[208,128]{1,0:T(8,128)(2,1)S(1)} %collective-permute-done.1.refs_2_, ...), custom_call_target="tpu_custom_call" | custom-call | tf_op jit(solution)/shard_map/correlate/pallas_call | solution.py:385
  18.6 3.8 %collective-permute-start.7 = (bf16[16,640]{1,0:T(8,128)(2,1)S(1)}, bf16[16,640]{1,0:T(8,128)(2,1)S(1)}, u32[]{:S(2)}, u32[]{:S(2)}) collective-permute-start(bf16[16,640]{1,0:T(8,128)(2,1)S(1)} %get-tuple-element.24), channel_id=1, source_target_pairs={{0,3},{1,2},{2,1},{3,0},{4,7},{5,6},{6,5},{7,4},{8,11},{9,10},{10,... | collective-permute-start | bytes 61448 | tf_op jit(solution)/shard_map/ppermute | solution.py:407
  22.3 0.0 collective-permute-start.8
  22.3 0.7 %collective-permute-start.9 = (bf16[16,640]{1,0:T(8,128)(2,1)S(1)}, bf16[16,640]{1,0:T(8,128)(2,1)S(1)}, u32[]{:S(2)}, u32[]{:S(2)}) collective-permute-start(bf16[16,640]{1,0:T(8,128)(2,1)S(1)} %get-tuple-element.26), channel_id=1, source_target_pairs={{0,1},{1,0},{2,3},{3,2},{4,5},{5,4},{6,7},{7,6},{8,9},{9,8},{10,11... | collective-permute-start | bytes 61448 | tf_op jit(solution)/shard_map/ppermute | solution.py:407
  23.0 1.2 %collective-permute-done.7.refs_1_ = bf16[16,640]{1,0:T(8,128)(2,1)S(1)} collective-permute-done((bf16[16,640]{1,0:T(8,128)(2,1)S(1)}, bf16[16,640]{1,0:T(8,128)(2,1)S(1)}, u32[]{:S(2)}, u32[]{:S(2)}) %collective-permute-start.7) | collective-permute-done | bytes 20512 | tf_op jit(solution)/shard_map/ppermute | solution.py:407
  24.2 2.8 %collective-permute-done.8.refs_2_ = bf16[16,640]{1,0:T(8,128)(2,1)S(1)} collective-permute-done((bf16[16,640]{1,0:T(8,128)(2,1)S(1)}, bf16[16,640]{1,0:T(8,128)(2,1)S(1)}, u32[]{:S(2)}, u32[]{:S(2)}) %collective-permute-start.8) | collective-permute-done | bytes 20512 | tf_op jit(solution)/shard_map/ppermute | solution.py:407
  27.0 0.0 collective-permute-done.9.refs_3_
  27.0 0.8 %finish.1 = f32[2,16,256]{2,1,0:T(8,128)} custom-call(bf16[16,640]{1,0:T(8,128)(2,1)S(1)} %get-tuple-element.23.refs_0_, bf16[16,640]{1,0:T(8,128)(2,1)S(1)} %collective-permute-done.7.refs_1_, bf16[16,640]{1,0:T(8,128)(2,1)S(1)} %collective-permute-done.8.refs_2_, bf16[16,640]{1,0:T(8,128)(2,1)S(1)} %collective-permute-done.9.refs_3_), custom_call_target="tpu_custom_call" | custom-call | tf_op jit(solution)/shard_map/finish/pallas_call | solution.py:410
Async XLA Ops:
  1.5 7.1 %collective-permute-start = (bf16[384,128]{1,0:T(8,128)(2,1)S(1)}, bf16[384,128]{1,0:T(8,128)(2,1)S(1)}, u32[]{:S(2)}, u32[]{:S(2)}) collective-permute-start(bf16[384,128]{1,0:T(8,128)(2,1)S(1)} %get-tuple-element.17), channel_id=1, source_target_pairs={{0,24},{4,28},{8,16},{12,20},{16,8},{20,12},{24,0},{28,4},{1,25},{... | collective-permute-start | bytes 294920 | tf_op jit(solution)/shard_map/ppermute | solution.py:374
  5.4 5.4 %copy-start = (s32[6,3]{0,1:T(4,128)S(1)}, s32[6,3]{0,1:T(4,128)}, u32[]{:S(2)}) copy-start(s32[6,3]{0,1:T(4,128)} %param.11) | copy-start | bytes 220
  5.4 4.9 %collective-permute-start.2 = (bf16[384,128]{1,0:T(8,128)(2,1)S(1)}, bf16[384,128]{1,0:T(8,128)(2,1)S(1)}, u32[]{:S(2)}, u32[]{:S(2)}) collective-permute-start(bf16[384,128]{1,0:T(8,128)(2,1)S(1)} %get-tuple-element.21), channel_id=1, source_target_pairs={{0,16},{4,20},{8,24},{12,28},{16,0},{20,4},{24,8},{28,12},{1,17},{... | collective-permute-start | bytes 294920 | tf_op jit(solution)/shard_map/ppermute | solution.py:374
  5.9 4.7 %collective-permute-start.3 = (bf16[384,128]{1,0:T(8,128)(2,1)S(1)}, bf16[384,128]{1,0:T(8,128)(2,1)S(1)}, u32[]{:S(2)}, u32[]{:S(2)}) collective-permute-start(bf16[384,128]{1,0:T(8,128)(2,1)S(1)} %get-tuple-element.22), channel_id=1, source_target_pairs={{0,8},{4,12},{8,0},{12,4},{16,24},{20,28},{24,16},{28,20},{1,9},{5... | collective-permute-start | bytes 294920 | tf_op jit(solution)/shard_map/ppermute | solution.py:374
  6.1 1.2 %collective-permute-start.1 = (bf16[208,128]{1,0:T(8,128)(2,1)S(1)}, bf16[208,128]{1,0:T(8,128)(2,1)S(1)}, u32[]{:S(2)}, u32[]{:S(2)}) collective-permute-start(bf16[208,128]{1,0:T(8,128)(2,1)S(1)} %get-tuple-element.18), channel_id=1, source_target_pairs={{0,4},{4,0},{8,12},{12,8},{16,20},{20,16},{24,28},{28,24},{1,5},{5... | collective-permute-start | bytes 159752 | tf_op jit(solution)/shard_map/ppermute | solution.py:374
  8.6 2.3 %collective-permute-start.4 = (bf16[384,128]{1,0:T(8,128)(2,1)S(1)}, bf16[384,128]{1,0:T(8,128)(2,1)S(1)}, u32[]{:S(2)}, u32[]{:S(2)}) collective-permute-start(bf16[384,128]{1,0:T(8,128)(2,1)S(1)} %collective-permute-done.refs_3_), channel_id=1, source_target_pairs={{0,4},{4,0},{8,12},{12,8},{16,20},{20,16},{24,28},{28,24},{1,5},{5... | collective-permute-start | bytes 294920 | tf_op jit(solution)/shard_map/ppermute | solution.py:374
  10.3 1.3 %collective-permute-start.5 = (bf16[384,128]{1,0:T(8,128)(2,1)S(1)}, bf16[384,128]{1,0:T(8,128)(2,1)S(1)}, u32[]{:S(2)}, u32[]{:S(2)}) collective-permute-start(bf16[384,128]{1,0:T(8,128)(2,1)S(1)} %collective-permute-done.2.refs_4_), channel_id=1, source_target_pairs={{0,4},{4,0},{8,12},{12,8},{16,20},{20,16},{24,28},{28,24},{1,5},{5... | collective-permute-start | bytes 294920 | tf_op jit(solution)/shard_map/ppermute | solution.py:374
  10.6 1.3 %collective-permute-start.6 = (bf16[384,128]{1,0:T(8,128)(2,1)S(1)}, bf16[384,128]{1,0:T(8,128)(2,1)S(1)}, u32[]{:S(2)}, u32[]{:S(2)}) collective-permute-start(bf16[384,128]{1,0:T(8,128)(2,1)S(1)} %collective-permute-done.3.refs_5_), channel_id=1, source_target_pairs={{0,4},{4,0},{8,12},{12,8},{16,20},{20,16},{24,28},{28,24},{1,5},{5... | collective-permute-start | bytes 294920 | tf_op jit(solution)/shard_map/ppermute | solution.py:374
  18.6 5.6 %collective-permute-start.7 = (bf16[16,640]{1,0:T(8,128)(2,1)S(1)}, bf16[16,640]{1,0:T(8,128)(2,1)S(1)}, u32[]{:S(2)}, u32[]{:S(2)}) collective-permute-start(bf16[16,640]{1,0:T(8,128)(2,1)S(1)} %get-tuple-element.24), channel_id=1, source_target_pairs={{0,3},{1,2},{2,1},{3,0},{4,7},{5,6},{6,5},{7,4},{8,11},{9,10},{10,... | collective-permute-start | bytes 61448 | tf_op jit(solution)/shard_map/ppermute | solution.py:407
  22.3 4.7 %collective-permute-start.8 = (bf16[16,640]{1,0:T(8,128)(2,1)S(1)}, bf16[16,640]{1,0:T(8,128)(2,1)S(1)}, u32[]{:S(2)}, u32[]{:S(2)}) collective-permute-start(bf16[16,640]{1,0:T(8,128)(2,1)S(1)} %get-tuple-element.25), channel_id=1, source_target_pairs={{0,2},{1,3},{2,0},{3,1},{4,6},{5,7},{6,4},{7,5},{8,10},{9,11},{10,... | collective-permute-start | bytes 61448 | tf_op jit(solution)/shard_map/ppermute | solution.py:407
  22.3 4.7 %collective-permute-start.9 = (bf16[16,640]{1,0:T(8,128)(2,1)S(1)}, bf16[16,640]{1,0:T(8,128)(2,1)S(1)}, u32[]{:S(2)}, u32[]{:S(2)}) collective-permute-start(bf16[16,640]{1,0:T(8,128)(2,1)S(1)} %get-tuple-element.26), channel_id=1, source_target_pairs={{0,1},{1,0},{2,3},{3,2},{4,5},{5,4},{6,7},{7,6},{8,9},{9,8},{10,11... | collective-permute-start | bytes 61448 | tf_op jit(solution)/shard_map/ppermute | solution.py:407

commit v7 on v6

--- a/solution.py
+++ b/solution.py
@@ -186,22 +186,22 @@
         for t in range(width // LANES):
             dsh_ref[t, r * series_rows : (r + 1) * series_rows, :] = moved[:, t * LANES : (t + 1) * LANES]
 
-    def ahead(values, by):
-        return pltpu.roll(values, width - by, 1)
-
-    sums = {1: x * x}
-    size = 1
-    while 2 * size <= taps:
-        sums[2 * size] = sums[size] + ahead(sums[size], size)
-        size = 2 * size
-    power = sums[size]
-    start = size
-    while start < taps:
-        size = size // 2
-        if taps - start >= size:
-            power = power + ahead(sums[size], start)
-            start += size
-    scale = lax.rsqrt(power / taps + epsilon)
+    squares = jnp.concatenate([x * x, jnp.zeros((series_rows, chunks * LANES), jnp.float32)], axis=1)
+    rounded = squares.astype(jnp.bfloat16).astype(jnp.float32)
+    rest = squares - rounded
+    reach = (chunks + 1) * LANES
+    sample = lax.broadcasted_iota(jnp.int32, (reach, LANES), 0)
+    sample = sample - lax.broadcasted_iota(jnp.int32, (reach, LANES), 1)
+    ones = jnp.where((sample >= 0) & (sample < taps), 1.0, 0.0).astype(jnp.bfloat16)
+    spans = [
+        part[:, t * LANES : t * LANES + reach] for t in range(lag_tiles) for part in (rounded, rest)
+    ]
+    power = jnp.dot(jnp.concatenate(spans, axis=0).astype(jnp.bfloat16), ones, preferred_element_type=jnp.float32)
+    power = [
+        power[2 * t * series_rows : (2 * t + 1) * series_rows]
+        + power[(2 * t + 1) * series_rows : (2 * t + 2) * series_rows]
+        for t in range(lag_tiles)
+    ]
     row = lax.broadcasted_iota(jnp.int32, (series_rows, LANES), 0)
     factor = jnp.zeros((series_rows, LANES), jnp.float32)
     for s in range(stations):
@@ -214,7 +214,7 @@
             value = value / jnp.full((series_rows, LANES), total_used).astype(jnp.float32)
             factor = jnp.where(mine, value, factor)
     for t in range(lag_tiles):
-        rd_ref[:, t * LANES : (t + 1) * LANES] = scale[:, t * LANES : (t + 1) * LANES] * factor
+        rd_ref[:, t * LANES : (t + 1) * LANES] = lax.rsqrt(power[t] / taps + epsilon) * factor
 
     target = lax.broadcasted_iota(jnp.int32, (stations * here, total), 0)
     source = lax.broadcasted_iota(jnp.int32, (stations * here, total), 1)
@@ -269,10 +269,10 @@
     for s in range(stations):
         rows_here = slice(s * here, (s + 1) * here)
         meta = meta_ref[rows_here, :]
-        tiles_over = meta[:, left + 1 : left + 2].astype(jnp.int32)
-        lanes_over = meta[:, left + 2 : left + 3].astype(jnp.int32)
+        tiles_over = jnp.broadcast_to(meta[:, left + 1 : left + 2], (here, LANES)).astype(jnp.int32)
+        lanes_over = jnp.broadcast_to(meta[:, left + 2 : left + 3], (here, LANES)).astype(jnp.int32)
         index = lane_here + lanes_over
-        within = index < LANES
+        within = lane_here >= lanes_over
         index = jnp.bitwise_and(index, LANES - 1)
         for b in range(blocks):
             total_corr = [jnp.zeros((here, LANES), jnp.float32) for _ in range(lag_tiles)]
@@ -304,9 +304,10 @@
                 for h in range(1, lag_tiles - NK // LANES):
                     if t + h < lag_tiles:
                         window = jnp.where(tiles_over == h, total_corr[t + h], window)
-                windows.append(jnp.take_along_axis(window, index, axis=1))
+                windows.append(window)
             for t in range(NK // LANES):
                 aligned = jnp.where(within, windows[t], windows[t + 1])
+                aligned = jnp.take_along_axis(aligned, index, axis=1)
                 at = b * NK + t * LANES
                 sh_ref[rows_here, at : at + LANES] = aligned.astype(jnp.bfloat16)
 

time: 28 us -> 26.5 us (0.946)
  Pallas kernels: 8.83 us -> 7.38 us
    pallas_call x1, Pallas kernels: 6.61 us -> 5.16 us  [body(): pl.pallas_call(functools.partial(correlate_kernel, (n, stations, blocks,...]
where the time goes in v7:
time: 26.5 us; the launch traced here: 26.4 us
  waiting for transfers between devices  9.59 us (36%)
  starting transfers between devices  9.26 us (35%)
  Pallas kernels  7.38 us (28%)
    ppermute x7, waiting for transfers between devices, swap(): return lax.ppermute(block, 'tmpl', [(i, i ^ d) for i in range(n)])  5.59 us
    pallas_call x1, Pallas kernels, body(): pl.pallas_call(functools.partial(correlate_kernel, (n, stations, blocks,...  5.16 us
    ppermute x7, starting transfers between devices, swap(): return lax.ppermute(block, 'tmpl', [(i, i ^ d) for i in range(n)])  4.8 us
    ppermute x3, starting transfers between devices, body(): lax.ppermute(part, 'stn', [(i, i ^ d) for i in range(owners)])  4.45 us
    ppermute x3, waiting for transfers between devices, body(): lax.ppermute(part, 'stn', [(i, i ^ d) for i in range(owners)])  4 us
    pallas_call x1, Pallas kernels, body(): pl.pallas_call(functools.partial(pack_kernel, (n, stations, slots, compon...  1.45 us
    pallas_call x1, Pallas kernels, body(): pl.pallas_call(functools.partial(finish_kernel, taps, blocks), out_shape=...  0.78 us
  transfers between devices with their start and end apart: 10, of which 8 were waited for; matrix products, arithmetic and copies ran while one was open for 0% of the time, Pallas kernels for 0%

profile of v7, /device:TPU:0, one launch (start us, length us, event | category | flops | bytes accessed | tf_op | source)
XLA Modules:
  0.0 26.4 jit_solution(10981143474184673646)
XLA Ops:
  0.0 1.4 %pack.1 = (bf16[208,128]{1,0:T(8,128)(2,1)S(1)}, bf16[208,128]{1,0:T(8,128)(2,1)S(1)}, bf16[384,128]{1,0:T(8,128)(2,1)S(1)}, bf16[384,128]{1,0:T(8,128)(2,1)S(1)}, bf16[384,128]{1,0:T(8,128)(2,1)S(1)}) custom-call(bf16[18,2,128]{2,1,0:T(2,128)(2,1)} %bitcast.8, bf16[18,16,300]{2,1,0:T(8,128)(2,1)} %bitcast.7, s32[6,1,16]{2,1,0:T(1,128)} %bitcast.9, ...), custom_call_target="tpu_custom_call" | custom-call | tf_op jit(solution)/shard_map/pack/pallas_call | solution.py:363
  1.5 4.0 %collective-permute-start = (bf16[384,128]{1,0:T(8,128)(2,1)S(1)}, bf16[384,128]{1,0:T(8,128)(2,1)S(1)}, u32[]{:S(2)}, u32[]{:S(2)}) collective-permute-start(bf16[384,128]{1,0:T(8,128)(2,1)S(1)} %get-tuple-element.17), channel_id=1, source_target_pairs={{0,24},{4,28},{8,16},{12,20},{16,8},{20,12},{24,0},{28,4},{1,25},{... | collective-permute-start | bytes 294920 | tf_op jit(solution)/shard_map/ppermute | solution.py:375
  5.4 0.0 copy-start
  5.4 0.5 %collective-permute-start.2 = (bf16[384,128]{1,0:T(8,128)(2,1)S(1)}, bf16[384,128]{1,0:T(8,128)(2,1)S(1)}, u32[]{:S(2)}, u32[]{:S(2)}) collective-permute-start(bf16[384,128]{1,0:T(8,128)(2,1)S(1)} %get-tuple-element.21), channel_id=1, source_target_pairs={{0,16},{4,20},{8,24},{12,28},{16,0},{20,4},{24,8},{28,12},{1,17},{... | collective-permute-start | bytes 294920 | tf_op jit(solution)/shard_map/ppermute | solution.py:375
  5.9 0.1 collective-permute-start.3
  6.1 0.0 collective-permute-start.1
  6.1 1.2 %collective-permute-done.1.refs_2_ = bf16[208,128]{1,0:T(8,128)(2,1)S(1)} collective-permute-done((bf16[208,128]{1,0:T(8,128)(2,1)S(1)}, bf16[208,128]{1,0:T(8,128)(2,1)S(1)}, u32[]{:S(2)}, u32[]{:S(2)}) %collective-permute-start.1) | collective-permute-done | bytes 53280 | tf_op jit(solution)/shard_map/ppermute | solution.py:375
  7.3 1.3 %collective-permute-done.refs_3_ = bf16[384,128]{1,0:T(8,128)(2,1)S(1)} collective-permute-done((bf16[384,128]{1,0:T(8,128)(2,1)S(1)}, bf16[384,128]{1,0:T(8,128)(2,1)S(1)}, u32[]{:S(2)}, u32[]{:S(2)}) %collective-permute-start) | collective-permute-done | bytes 98336 | tf_op jit(solution)/shard_map/ppermute | solution.py:375
  8.6 0.0 collective-permute-start.4
  8.6 1.7 %collective-permute-done.2.refs_4_ = bf16[384,128]{1,0:T(8,128)(2,1)S(1)} collective-permute-done((bf16[384,128]{1,0:T(8,128)(2,1)S(1)}, bf16[384,128]{1,0:T(8,128)(2,1)S(1)}, u32[]{:S(2)}, u32[]{:S(2)}) %collective-permute-start.2) | collective-permute-done | bytes 98336 | tf_op jit(solution)/shard_map/ppermute | solution.py:375
  10.3 0.0 collective-permute-start.5
  10.3 0.3 %collective-permute-done.3.refs_5_ = bf16[384,128]{1,0:T(8,128)(2,1)S(1)} collective-permute-done((bf16[384,128]{1,0:T(8,128)(2,1)S(1)}, bf16[384,128]{1,0:T(8,128)(2,1)S(1)}, u32[]{:S(2)}, u32[]{:S(2)}) %collective-permute-start.3) | collective-permute-done | bytes 98336 | tf_op jit(solution)/shard_map/ppermute | solution.py:375
  10.6 0.2 collective-permute-start.6
  10.8 0.0 copy-done
  10.8 0.1 copy.7.refs_0_
  10.9 0.0 collective-permute-done.4.refs_6_
  10.9 0.7 %collective-permute-done.5.refs_7_ = bf16[384,128]{1,0:T(8,128)(2,1)S(1)} collective-permute-done((bf16[384,128]{1,0:T(8,128)(2,1)S(1)}, bf16[384,128]{1,0:T(8,128)(2,1)S(1)}, u32[]{:S(2)}, u32[]{:S(2)}) %collective-permute-start.5) | collective-permute-done | bytes 98336 | tf_op jit(solution)/shard_map/ppermute | solution.py:375
  11.6 0.3 %collective-permute-done.6.refs_8_ = bf16[384,128]{1,0:T(8,128)(2,1)S(1)} collective-permute-done((bf16[384,128]{1,0:T(8,128)(2,1)S(1)}, bf16[384,128]{1,0:T(8,128)(2,1)S(1)}, u32[]{:S(2)}, u32[]{:S(2)}) %collective-permute-start.6) | collective-permute-done | bytes 98336 | tf_op jit(solution)/shard_map/ppermute | solution.py:375
  11.9 5.2 %correlate.1 = (bf16[16,640]{1,0:T(8,128)(2,1)S(1)}, bf16[16,640]{1,0:T(8,128)(2,1)S(1)}, bf16[16,640]{1,0:T(8,128)(2,1)S(1)}, bf16[16,640]{1,0:T(8,128)(2,1)S(1)}) custom-call(s32[6,3]{1,0:T(8,128)S(1)} %copy.7.refs_0_, bf16[208,128]{1,0:T(8,128)(2,1)S(1)} %get-tuple-element.16.refs_1_, bf16[208,128]{1,0:T(8,128)(2,1)S(1)} %collective-permute-done.1.refs_2_, ...), custom_call_target="tpu_custom_call" | custom-call | tf_op jit(solution)/shard_map/correlate/pallas_call | solution.py:386
  17.1 3.8 %collective-permute-start.7 = (bf16[16,640]{1,0:T(8,128)(2,1)S(1)}, bf16[16,640]{1,0:T(8,128)(2,1)S(1)}, u32[]{:S(2)}, u32[]{:S(2)}) collective-permute-start(bf16[16,640]{1,0:T(8,128)(2,1)S(1)} %get-tuple-element.24), channel_id=1, source_target_pairs={{0,3},{1,2},{2,1},{3,0},{4,7},{5,6},{6,5},{7,4},{8,11},{9,10},{10,... | collective-permute-start | bytes 61448 | tf_op jit(solution)/shard_map/ppermute | solution.py:408
  20.9 0.0 collective-permute-start.8
  20.9 0.7 %collective-permute-start.9 = (bf16[16,640]{1,0:T(8,128)(2,1)S(1)}, bf16[16,640]{1,0:T(8,128)(2,1)S(1)}, u32[]{:S(2)}, u32[]{:S(2)}) collective-permute-start(bf16[16,640]{1,0:T(8,128)(2,1)S(1)} %get-tuple-element.26), channel_id=1, source_target_pairs={{0,1},{1,0},{2,3},{3,2},{4,5},{5,4},{6,7},{7,6},{8,9},{9,8},{10,11... | collective-permute-start | bytes 61448 | tf_op jit(solution)/shard_map/ppermute | solution.py:408
  21.6 1.2 %collective-permute-done.7.refs_1_ = bf16[16,640]{1,0:T(8,128)(2,1)S(1)} collective-permute-done((bf16[16,640]{1,0:T(8,128)(2,1)S(1)}, bf16[16,640]{1,0:T(8,128)(2,1)S(1)}, u32[]{:S(2)}, u32[]{:S(2)}) %collective-permute-start.7) | collective-permute-done | bytes 20512 | tf_op jit(solution)/shard_map/ppermute | solution.py:408
  22.8 2.8 %collective-permute-done.8.refs_2_ = bf16[16,640]{1,0:T(8,128)(2,1)S(1)} collective-permute-done((bf16[16,640]{1,0:T(8,128)(2,1)S(1)}, bf16[16,640]{1,0:T(8,128)(2,1)S(1)}, u32[]{:S(2)}, u32[]{:S(2)}) %collective-permute-start.8) | collective-permute-done | bytes 20512 | tf_op jit(solution)/shard_map/ppermute | solution.py:408
  25.6 0.0 collective-permute-done.9.refs_3_
  25.6 0.8 %finish.1 = f32[2,16,256]{2,1,0:T(8,128)} custom-call(bf16[16,640]{1,0:T(8,128)(2,1)S(1)} %get-tuple-element.23.refs_0_, bf16[16,640]{1,0:T(8,128)(2,1)S(1)} %collective-permute-done.7.refs_1_, bf16[16,640]{1,0:T(8,128)(2,1)S(1)} %collective-permute-done.8.refs_2_, bf16[16,640]{1,0:T(8,128)(2,1)S(1)} %collective-permute-done.9.refs_3_), custom_call_target="tpu_custom_call" | custom-call | tf_op jit(solution)/shard_map/finish/pallas_call | solution.py:411
Async XLA Ops:
  1.5 7.1 %collective-permute-start = (bf16[384,128]{1,0:T(8,128)(2,1)S(1)}, bf16[384,128]{1,0:T(8,128)(2,1)S(1)}, u32[]{:S(2)}, u32[]{:S(2)}) collective-permute-start(bf16[384,128]{1,0:T(8,128)(2,1)S(1)} %get-tuple-element.17), channel_id=1, source_target_pairs={{0,24},{4,28},{8,16},{12,20},{16,8},{20,12},{24,0},{28,4},{1,25},{... | collective-permute-start | bytes 294920 | tf_op jit(solution)/shard_map/ppermute | solution.py:375
  5.4 5.4 %copy-start = (s32[6,3]{0,1:T(4,128)S(1)}, s32[6,3]{0,1:T(4,128)}, u32[]{:S(2)}) copy-start(s32[6,3]{0,1:T(4,128)} %param.11) | copy-start | bytes 220
  5.4 4.9 %collective-permute-start.2 = (bf16[384,128]{1,0:T(8,128)(2,1)S(1)}, bf16[384,128]{1,0:T(8,128)(2,1)S(1)}, u32[]{:S(2)}, u32[]{:S(2)}) collective-permute-start(bf16[384,128]{1,0:T(8,128)(2,1)S(1)} %get-tuple-element.21), channel_id=1, source_target_pairs={{0,16},{4,20},{8,24},{12,28},{16,0},{20,4},{24,8},{28,12},{1,17},{... | collective-permute-start | bytes 294920 | tf_op jit(solution)/shard_map/ppermute | solution.py:375
  5.9 4.7 %collective-permute-start.3 = (bf16[384,128]{1,0:T(8,128)(2,1)S(1)}, bf16[384,128]{1,0:T(8,128)(2,1)S(1)}, u32[]{:S(2)}, u32[]{:S(2)}) collective-permute-start(bf16[384,128]{1,0:T(8,128)(2,1)S(1)} %get-tuple-element.22), channel_id=1, source_target_pairs={{0,8},{4,12},{8,0},{12,4},{16,24},{20,28},{24,16},{28,20},{1,9},{5... | collective-permute-start | bytes 294920 | tf_op jit(solution)/shard_map/ppermute | solution.py:375
  6.1 1.2 %collective-permute-start.1 = (bf16[208,128]{1,0:T(8,128)(2,1)S(1)}, bf16[208,128]{1,0:T(8,128)(2,1)S(1)}, u32[]{:S(2)}, u32[]{:S(2)}) collective-permute-start(bf16[208,128]{1,0:T(8,128)(2,1)S(1)} %get-tuple-element.18), channel_id=1, source_target_pairs={{0,4},{4,0},{8,12},{12,8},{16,20},{20,16},{24,28},{28,24},{1,5},{5... | collective-permute-start | bytes 159752 | tf_op jit(solution)/shard_map/ppermute | solution.py:375
  8.6 2.3 %collective-permute-start.4 = (bf16[384,128]{1,0:T(8,128)(2,1)S(1)}, bf16[384,128]{1,0:T(8,128)(2,1)S(1)}, u32[]{:S(2)}, u32[]{:S(2)}) collective-permute-start(bf16[384,128]{1,0:T(8,128)(2,1)S(1)} %collective-permute-done.refs_3_), channel_id=1, source_target_pairs={{0,4},{4,0},{8,12},{12,8},{16,20},{20,16},{24,28},{28,24},{1,5},{5... | collective-permute-start | bytes 294920 | tf_op jit(solution)/shard_map/ppermute | solution.py:375
  10.3 1.3 %collective-permute-start.5 = (bf16[384,128]{1,0:T(8,128)(2,1)S(1)}, bf16[384,128]{1,0:T(8,128)(2,1)S(1)}, u32[]{:S(2)}, u32[]{:S(2)}) collective-permute-start(bf16[384,128]{1,0:T(8,128)(2,1)S(1)} %collective-permute-done.2.refs_4_), channel_id=1, source_target_pairs={{0,4},{4,0},{8,12},{12,8},{16,20},{20,16},{24,28},{28,24},{1,5},{5... | collective-permute-start | bytes 294920 | tf_op jit(solution)/shard_map/ppermute | solution.py:375
  10.6 1.3 %collective-permute-start.6 = (bf16[384,128]{1,0:T(8,128)(2,1)S(1)}, bf16[384,128]{1,0:T(8,128)(2,1)S(1)}, u32[]{:S(2)}, u32[]{:S(2)}) collective-permute-start(bf16[384,128]{1,0:T(8,128)(2,1)S(1)} %collective-permute-done.3.refs_5_), channel_id=1, source_target_pairs={{0,4},{4,0},{8,12},{12,8},{16,20},{20,16},{24,28},{28,24},{1,5},{5... | collective-permute-start | bytes 294920 | tf_op jit(solution)/shard_map/ppermute | solution.py:375
  17.1 5.6 %collective-permute-start.7 = (bf16[16,640]{1,0:T(8,128)(2,1)S(1)}, bf16[16,640]{1,0:T(8,128)(2,1)S(1)}, u32[]{:S(2)}, u32[]{:S(2)}) collective-permute-start(bf16[16,640]{1,0:T(8,128)(2,1)S(1)} %get-tuple-element.24), channel_id=1, source_target_pairs={{0,3},{1,2},{2,1},{3,0},{4,7},{5,6},{6,5},{7,4},{8,11},{9,10},{10,... | collective-permute-start | bytes 61448 | tf_op jit(solution)/shard_map/ppermute | solution.py:408
  20.9 4.7 %collective-permute-start.8 = (bf16[16,640]{1,0:T(8,128)(2,1)S(1)}, bf16[16,640]{1,0:T(8,128)(2,1)S(1)}, u32[]{:S(2)}, u32[]{:S(2)}) collective-permute-start(bf16[16,640]{1,0:T(8,128)(2,1)S(1)} %get-tuple-element.25), channel_id=1, source_target_pairs={{0,2},{1,3},{2,0},{3,1},{4,6},{5,7},{6,4},{7,5},{8,10},{9,11},{10,... | collective-permute-start | bytes 61448 | tf_op jit(solution)/shard_map/ppermute | solution.py:408
  20.9 4.7 %collective-permute-start.9 = (bf16[16,640]{1,0:T(8,128)(2,1)S(1)}, bf16[16,640]{1,0:T(8,128)(2,1)S(1)}, u32[]{:S(2)}, u32[]{:S(2)}) collective-permute-start(bf16[16,640]{1,0:T(8,128)(2,1)S(1)} %get-tuple-element.26), channel_id=1, source_target_pairs={{0,1},{1,0},{2,3},{3,2},{4,5},{5,4},{6,7},{7,6},{8,9},{9,8},{10,11... | collective-permute-start | bytes 61448 | tf_op jit(solution)/shard_map/ppermute | solution.py:408

commit v8 on v7

--- a/solution.py
+++ b/solution.py
@@ -31,8 +31,12 @@
     return values & (divisor - 1)
 
 
-def partners(n):
-    return [0] + list(range(n - 1, 0, -1))
+def halvings(n):
+    order, step = [0], n
+    while step > 1:
+        step = step // 2
+        order = order + [d + n // (2 * step) for d in order]
+    return [int(format(d, "b").zfill(n.bit_length() - 1)[::-1], 2) if n > 1 else 0 for d in order]
 
 
 def chips(n):
@@ -147,6 +151,7 @@
     else:
         data_ref, mask_ref, *refs = refs
     n, stations, blocks, components, taps, most, rows, width, per_group = dims
+    keep = max(1, per_group // TPD // 2)
     own_ref, core_ref, *chip_refs = refs[:n]
     refs = refs[n:]
     come = [(own_ref, 0, 1), (core_ref, 0, 1)]
@@ -321,10 +326,24 @@
         onehot, sh_ref[...], (((0,), (0,)), ((), ())), preferred_element_type=jnp.float32
     )
     me = lax.axis_index("stn")
-    for d, out_ref in zip(partners(len(out_refs)), out_refs):
-        owner = me ^ d
-        theirs = pl.ds(pl.multiple_of(owner * TPD, TPD), TPD)
-        out_ref[...] = stack_ref[theirs, :].astype(jnp.bfloat16)
+    for i, d in enumerate(halvings(per_group // TPD)):
+        theirs = pl.ds(pl.multiple_of((me ^ d) * TPD, TPD), TPD)
+        out_ref = out_refs[i // keep]
+        at = i % keep * TPD
+        out_ref[at : at + TPD, :] = stack_ref[theirs, :].astype(out_ref.dtype)
+
+
+def add_kernel(blocks, kept_ref, came_ref, keep_ref, send_ref):
+    total = kept_ref[...] + came_ref[...].astype(jnp.float32)
+    count = total[:, blocks * NK :]
+    count = count + pltpu.roll(count, LANES // 2, 1)
+    high = jnp.floor(count * (1.0 / LANES)) * LANES
+    lane = lax.broadcasted_iota(jnp.int32, count.shape, 1)
+    count = jnp.where(lane < LANES // 2, count - high, high)
+    total = jnp.concatenate([total[:, : blocks * NK], count], axis=1)
+    half = keep_ref.shape[0]
+    keep_ref[...] = total[:half]
+    send_ref[...] = total[half:].astype(send_ref.dtype)
 
 
 def finish_kernel(taps, blocks, *refs):
@@ -343,6 +362,7 @@
     n = lax.axis_size("tmpl")
     owners = lax.axis_size("stn")
     per_group = TPD * owners
+    keep = max(1, owners // 2)
     width = width_here * n
     most = max(2, 2 * slots // n)
     rows = ceil_to(stations * most, 8)
@@ -389,7 +409,10 @@
             (n, stations, blocks, components, taps, most, rows, width, per_group),
             with_data,
         ),
-        out_shape=[jax.ShapeDtypeStruct((TPD, blocks * NK + LANES), jnp.bfloat16)] * owners,
+        out_shape=[
+            jax.ShapeDtypeStruct((keep * TPD, blocks * NK + LANES), held)
+            for held in ([jnp.float32, jnp.bfloat16] if owners > 1 else [jnp.float32])
+        ],
         in_specs=[vmem] * (0 if with_data else 1) + [pl.BlockSpec(memory_space=pltpu.SMEM)] + [vmem] * n,
         scratch_shapes=[
             pltpu.VMEM((width // LANES, series_rows, LANES), jnp.float32),
@@ -404,14 +427,29 @@
         compiler_params=pltpu.CompilerParams(vmem_limit_bytes=40 << 20),
         name="correlate",
     )(*([] if with_data else [samples]), chan_mask, *received)
-    parts = [
-        lax.ppermute(part, "stn", [(i, i ^ d) for i in range(owners)]) if d else part
-        for d, part in zip(partners(owners), partial_stacks)
-    ]
+    small = pltpu.CompilerParams(vmem_limit_bytes=4 << 20)
+    parts = list(partial_stacks)
+    distance = 1
+    while distance < owners:
+        step = [(i, i ^ distance) for i in range(owners)]
+        parts[1] = lax.ppermute(parts[1], "stn", step)
+        distance = 2 * distance
+        if distance < owners:
+            keep = keep // 2
+            parts = pl.pallas_call(
+                functools.partial(add_kernel, blocks),
+                out_shape=[
+                    jax.ShapeDtypeStruct((keep * TPD, blocks * NK + LANES), held)
+                    for held in (jnp.float32, jnp.bfloat16)
+                ],
+                compiler_params=small,
+                name="add",
+            )(*parts)
+            parts = list(parts)
     return pl.pallas_call(
         functools.partial(finish_kernel, taps, blocks),
         out_shape=jax.ShapeDtypeStruct((blocks, TPD, NK), jnp.float32),
-        compiler_params=pltpu.CompilerParams(vmem_limit_bytes=4 << 20),
+        compiler_params=small,
         name="finish",
     )(*parts)
 

time: 26.5 us -> 26.9 us (1.015)
  waiting for transfers between devices: 9.59 us -> 9.87 us
    ppermute x3 -> x2, waiting for transfers between devices: 4 us -> 4.29 us  [body(): parts[1] = lax.ppermute(parts[1], 'stn', step)]
    ppermute x3 -> x2, starting transfers between devices: 4.45 us -> 4.47 us  [body(): parts[1] = lax.ppermute(parts[1], 'stn', step)]
  transfers between devices with their start and end apart: 10 -> 9, of which waited for: 8 -> 8; matrix products, arithmetic and copies ran while one was open for 0% -> 0% of each run, Pallas kernels for 0% -> 0%
where the time goes in v8:
time: 26.9 us; the launch traced here: 26.7 us
  waiting for transfers between devices  9.87 us (37%)
  starting transfers between devices  9.27 us (34%)
  Pallas kernels  7.46 us (28%)
    ppermute x7, waiting for transfers between devices, swap(): return lax.ppermute(block, 'tmpl', [(i, i ^ d) for i in range(n)])  5.59 us
    pallas_call x1, Pallas kernels, body(): pl.pallas_call(functools.partial(correlate_kernel, (n, stations, blocks,...  5.16 us
    ppermute x7, starting transfers between devices, swap(): return lax.ppermute(block, 'tmpl', [(i, i ^ d) for i in range(n)])  4.8 us
    ppermute x2, starting transfers between devices, body(): parts[1] = lax.ppermute(parts[1], 'stn', step)  4.47 us
    ppermute x2, waiting for transfers between devices, body(): parts[1] = lax.ppermute(parts[1], 'stn', step)  4.29 us
    pallas_call x1, Pallas kernels, body(): pl.pallas_call(functools.partial(pack_kernel, (n, stations, slots, compon...  1.45 us
    pallas_call x1, Pallas kernels, body(): pl.pallas_call(functools.partial(finish_kernel, taps, blocks), out_shape=...  0.77 us
  transfers between devices with their start and end apart: 9, of which 8 were waited for; matrix products, arithmetic and copies ran while one was open for 0% of the time, Pallas kernels for 0%

profile of v8, /device:TPU:0, one launch (start us, length us, event | category | flops | bytes accessed | tf_op | source)
XLA Modules:
  0.0 26.7 jit_solution(10382338715291406046)
XLA Ops:
  0.0 1.4 %pack.1 = (bf16[208,128]{1,0:T(8,128)(2,1)S(1)}, bf16[208,128]{1,0:T(8,128)(2,1)S(1)}, bf16[384,128]{1,0:T(8,128)(2,1)S(1)}, bf16[384,128]{1,0:T(8,128)(2,1)S(1)}, bf16[384,128]{1,0:T(8,128)(2,1)S(1)}) custom-call(bf16[18,2,128]{2,1,0:T(2,128)(2,1)} %bitcast.8, bf16[18,16,300]{2,1,0:T(8,128)(2,1)} %bitcast.7, s32[6,1,16]{2,1,0:T(1,128)} %bitcast.9, ...), custom_call_target="tpu_custom_call" | custom-call | tf_op jit(solution)/shard_map/pack/pallas_call | solution.py:383
  1.5 4.0 %collective-permute-start = (bf16[384,128]{1,0:T(8,128)(2,1)S(1)}, bf16[384,128]{1,0:T(8,128)(2,1)S(1)}, u32[]{:S(2)}, u32[]{:S(2)}) collective-permute-start(bf16[384,128]{1,0:T(8,128)(2,1)S(1)} %get-tuple-element.17), channel_id=1, source_target_pairs={{0,24},{4,28},{8,16},{12,20},{16,8},{20,12},{24,0},{28,4},{1,25},{... | collective-permute-start | bytes 294920 | tf_op jit(solution)/shard_map/ppermute | solution.py:395
  5.4 0.0 copy-start
  5.4 0.5 %collective-permute-start.2 = (bf16[384,128]{1,0:T(8,128)(2,1)S(1)}, bf16[384,128]{1,0:T(8,128)(2,1)S(1)}, u32[]{:S(2)}, u32[]{:S(2)}) collective-permute-start(bf16[384,128]{1,0:T(8,128)(2,1)S(1)} %get-tuple-element.21), channel_id=1, source_target_pairs={{0,16},{4,20},{8,24},{12,28},{16,0},{20,4},{24,8},{28,12},{1,17},{... | collective-permute-start | bytes 294920 | tf_op jit(solution)/shard_map/ppermute | solution.py:395
  5.9 0.1 collective-permute-start.3
  6.1 0.0 collective-permute-start.1
  6.1 1.2 %collective-permute-done.1.refs_2_ = bf16[208,128]{1,0:T(8,128)(2,1)S(1)} collective-permute-done((bf16[208,128]{1,0:T(8,128)(2,1)S(1)}, bf16[208,128]{1,0:T(8,128)(2,1)S(1)}, u32[]{:S(2)}, u32[]{:S(2)}) %collective-permute-start.1) | collective-permute-done | bytes 53280 | tf_op jit(solution)/shard_map/ppermute | solution.py:395
  7.3 1.3 %collective-permute-done.refs_3_ = bf16[384,128]{1,0:T(8,128)(2,1)S(1)} collective-permute-done((bf16[384,128]{1,0:T(8,128)(2,1)S(1)}, bf16[384,128]{1,0:T(8,128)(2,1)S(1)}, u32[]{:S(2)}, u32[]{:S(2)}) %collective-permute-start) | collective-permute-done | bytes 98336 | tf_op jit(solution)/shard_map/ppermute | solution.py:395
  8.6 0.0 collective-permute-start.4
  8.6 1.7 %collective-permute-done.2.refs_4_ = bf16[384,128]{1,0:T(8,128)(2,1)S(1)} collective-permute-done((bf16[384,128]{1,0:T(8,128)(2,1)S(1)}, bf16[384,128]{1,0:T(8,128)(2,1)S(1)}, u32[]{:S(2)}, u32[]{:S(2)}) %collective-permute-start.2) | collective-permute-done | bytes 98336 | tf_op jit(solution)/shard_map/ppermute | solution.py:395
  10.3 0.0 collective-permute-start.5
  10.3 0.3 %collective-permute-done.3.refs_5_ = bf16[384,128]{1,0:T(8,128)(2,1)S(1)} collective-permute-done((bf16[384,128]{1,0:T(8,128)(2,1)S(1)}, bf16[384,128]{1,0:T(8,128)(2,1)S(1)}, u32[]{:S(2)}, u32[]{:S(2)}) %collective-permute-start.3) | collective-permute-done | bytes 98336 | tf_op jit(solution)/shard_map/ppermute | solution.py:395
  10.6 0.2 collective-permute-start.6
  10.8 0.0 copy-done
  10.8 0.1 copy.7.refs_0_
  10.9 0.0 collective-permute-done.4.refs_6_
  10.9 0.7 %collective-permute-done.5.refs_7_ = bf16[384,128]{1,0:T(8,128)(2,1)S(1)} collective-permute-done((bf16[384,128]{1,0:T(8,128)(2,1)S(1)}, bf16[384,128]{1,0:T(8,128)(2,1)S(1)}, u32[]{:S(2)}, u32[]{:S(2)}) %collective-permute-start.5) | collective-permute-done | bytes 98336 | tf_op jit(solution)/shard_map/ppermute | solution.py:395
  11.6 0.3 %collective-permute-done.6.refs_8_ = bf16[384,128]{1,0:T(8,128)(2,1)S(1)} collective-permute-done((bf16[384,128]{1,0:T(8,128)(2,1)S(1)}, bf16[384,128]{1,0:T(8,128)(2,1)S(1)}, u32[]{:S(2)}, u32[]{:S(2)}) %collective-permute-start.6) | collective-permute-done | bytes 98336 | tf_op jit(solution)/shard_map/ppermute | solution.py:395
  11.9 5.2 %correlate.1 = (f32[32,640]{1,0:T(8,128)S(1)}, bf16[32,640]{1,0:T(8,128)(2,1)S(1)}) custom-call(s32[6,3]{1,0:T(8,128)S(1)} %copy.7.refs_0_, bf16[208,128]{1,0:T(8,128)(2,1)S(1)} %get-tuple-element.16.refs_1_, bf16[208,128]{1,0:T(8,128)(2,1)S(1)} %collective-permute-done.1.refs_2_, bf16[384,128]{1,0:T(8,128)(2,1)S(1)} %collective-permute-done.refs_3_, ...), custom_call_target="tpu_custom_call" | custom-call | tf_op jit(solution)/shard_map/correlate/pallas_call | solution.py:406
  17.1 1.8 %collective-permute-start.7 = (bf16[32,640]{1,0:T(8,128)(2,1)S(1)}, bf16[32,640]{1,0:T(8,128)(2,1)S(1)}, u32[]{:S(2)}, u32[]{:S(2)}) collective-permute-start(bf16[32,640]{1,0:T(8,128)(2,1)S(1)} %get-tuple-element.24), channel_id=1, source_target_pairs={{0,1},{1,0},{2,3},{3,2},{4,5},{5,4},{6,7},{7,6},{8,9},{9,8},{10,11... | collective-permute-start | bytes 122888 | tf_op jit(solution)/shard_map/ppermute | solution.py:435
  18.9 2.3 %collective-permute-done.7.came_ref = bf16[32,640]{1,0:T(8,128)(2,1)S(1)} collective-permute-done((bf16[32,640]{1,0:T(8,128)(2,1)S(1)}, bf16[32,640]{1,0:T(8,128)(2,1)S(1)}, u32[]{:S(2)}, u32[]{:S(2)}) %collective-permute-start.7) | collective-permute-done | bytes 40992 | tf_op jit(solution)/shard_map/ppermute | solution.py:435
  21.2 0.1 add.1
  21.3 2.7 %collective-permute-start.8 = (bf16[16,640]{1,0:T(8,128)(2,1)S(1)}, bf16[16,640]{1,0:T(8,128)(2,1)S(1)}, u32[]{:S(2)}, u32[]{:S(2)}) collective-permute-start(bf16[16,640]{1,0:T(8,128)(2,1)S(1)} %get-tuple-element.26), channel_id=1, source_target_pairs={{0,2},{1,3},{2,0},{3,1},{4,6},{5,7},{6,4},{7,5},{8,10},{9,11},{10,... | collective-permute-start | bytes 61448 | tf_op jit(solution)/shard_map/ppermute | solution.py:435
  24.0 2.0 %collective-permute-done.8.refs_1_ = bf16[16,640]{1,0:T(8,128)(2,1)S(1)} collective-permute-done((bf16[16,640]{1,0:T(8,128)(2,1)S(1)}, bf16[16,640]{1,0:T(8,128)(2,1)S(1)}, u32[]{:S(2)}, u32[]{:S(2)}) %collective-permute-start.8) | collective-permute-done | bytes 20512 | tf_op jit(solution)/shard_map/ppermute | solution.py:435
  26.0 0.8 %finish.1 = f32[2,16,256]{2,1,0:T(8,128)} custom-call(f32[16,640]{1,0:T(8,128)S(1)} %get-tuple-element.25.refs_0_, bf16[16,640]{1,0:T(8,128)(2,1)S(1)} %collective-permute-done.8.refs_1_), custom_call_target="tpu_custom_call" | custom-call | tf_op jit(solution)/shard_map/finish/pallas_call | solution.py:449
Async XLA Ops:
  1.5 7.1 %collective-permute-start = (bf16[384,128]{1,0:T(8,128)(2,1)S(1)}, bf16[384,128]{1,0:T(8,128)(2,1)S(1)}, u32[]{:S(2)}, u32[]{:S(2)}) collective-permute-start(bf16[384,128]{1,0:T(8,128)(2,1)S(1)} %get-tuple-element.17), channel_id=1, source_target_pairs={{0,24},{4,28},{8,16},{12,20},{16,8},{20,12},{24,0},{28,4},{1,25},{... | collective-permute-start | bytes 294920 | tf_op jit(solution)/shard_map/ppermute | solution.py:395
  5.4 5.4 %copy-start = (s32[6,3]{0,1:T(4,128)S(1)}, s32[6,3]{0,1:T(4,128)}, u32[]{:S(2)}) copy-start(s32[6,3]{0,1:T(4,128)} %param.11) | copy-start | bytes 220
  5.4 4.9 %collective-permute-start.2 = (bf16[384,128]{1,0:T(8,128)(2,1)S(1)}, bf16[384,128]{1,0:T(8,128)(2,1)S(1)}, u32[]{:S(2)}, u32[]{:S(2)}) collective-permute-start(bf16[384,128]{1,0:T(8,128)(2,1)S(1)} %get-tuple-element.21), channel_id=1, source_target_pairs={{0,16},{4,20},{8,24},{12,28},{16,0},{20,4},{24,8},{28,12},{1,17},{... | collective-permute-start | bytes 294920 | tf_op jit(solution)/shard_map/ppermute | solution.py:395
  5.9 4.7 %collective-permute-start.3 = (bf16[384,128]{1,0:T(8,128)(2,1)S(1)}, bf16[384,128]{1,0:T(8,128)(2,1)S(1)}, u32[]{:S(2)}, u32[]{:S(2)}) collective-permute-start(bf16[384,128]{1,0:T(8,128)(2,1)S(1)} %get-tuple-element.22), channel_id=1, source_target_pairs={{0,8},{4,12},{8,0},{12,4},{16,24},{20,28},{24,16},{28,20},{1,9},{5... | collective-permute-start | bytes 294920 | tf_op jit(solution)/shard_map/ppermute | solution.py:395
  6.1 1.2 %collective-permute-start.1 = (bf16[208,128]{1,0:T(8,128)(2,1)S(1)}, bf16[208,128]{1,0:T(8,128)(2,1)S(1)}, u32[]{:S(2)}, u32[]{:S(2)}) collective-permute-start(bf16[208,128]{1,0:T(8,128)(2,1)S(1)} %get-tuple-element.18), channel_id=1, source_target_pairs={{0,4},{4,0},{8,12},{12,8},{16,20},{20,16},{24,28},{28,24},{1,5},{5... | collective-permute-start | bytes 159752 | tf_op jit(solution)/shard_map/ppermute | solution.py:395
  8.6 2.3 %collective-permute-start.4 = (bf16[384,128]{1,0:T(8,128)(2,1)S(1)}, bf16[384,128]{1,0:T(8,128)(2,1)S(1)}, u32[]{:S(2)}, u32[]{:S(2)}) collective-permute-start(bf16[384,128]{1,0:T(8,128)(2,1)S(1)} %collective-permute-done.refs_3_), channel_id=1, source_target_pairs={{0,4},{4,0},{8,12},{12,8},{16,20},{20,16},{24,28},{28,24},{1,5},{5... | collective-permute-start | bytes 294920 | tf_op jit(solution)/shard_map/ppermute | solution.py:395
  10.3 1.3 %collective-permute-start.5 = (bf16[384,128]{1,0:T(8,128)(2,1)S(1)}, bf16[384,128]{1,0:T(8,128)(2,1)S(1)}, u32[]{:S(2)}, u32[]{:S(2)}) collective-permute-start(bf16[384,128]{1,0:T(8,128)(2,1)S(1)} %collective-permute-done.2.refs_4_), channel_id=1, source_target_pairs={{0,4},{4,0},{8,12},{12,8},{16,20},{20,16},{24,28},{28,24},{1,5},{5... | collective-permute-start | bytes 294920 | tf_op jit(solution)/shard_map/ppermute | solution.py:395
  10.6 1.3 %collective-permute-start.6 = (bf16[384,128]{1,0:T(8,128)(2,1)S(1)}, bf16[384,128]{1,0:T(8,128)(2,1)S(1)}, u32[]{:S(2)}, u32[]{:S(2)}) collective-permute-start(bf16[384,128]{1,0:T(8,128)(2,1)S(1)} %collective-permute-done.3.refs_5_), channel_id=1, source_target_pairs={{0,4},{4,0},{8,12},{12,8},{16,20},{20,16},{24,28},{28,24},{1,5},{5... | collective-permute-start | bytes 294920 | tf_op jit(solution)/shard_map/ppermute | solution.py:395
  17.1 4.1 %collective-permute-start.7 = (bf16[32,640]{1,0:T(8,128)(2,1)S(1)}, bf16[32,640]{1,0:T(8,128)(2,1)S(1)}, u32[]{:S(2)}, u32[]{:S(2)}) collective-permute-start(bf16[32,640]{1,0:T(8,128)(2,1)S(1)} %get-tuple-element.24), channel_id=1, source_target_pairs={{0,1},{1,0},{2,3},{3,2},{4,5},{5,4},{6,7},{7,6},{8,9},{9,8},{10,11... | collective-permute-start | bytes 122888 | tf_op jit(solution)/shard_map/ppermute | solution.py:435
  21.3 4.7 %collective-permute-start.8 = (bf16[16,640]{1,0:T(8,128)(2,1)S(1)}, bf16[16,640]{1,0:T(8,128)(2,1)S(1)}, u32[]{:S(2)}, u32[]{:S(2)}) collective-permute-start(bf16[16,640]{1,0:T(8,128)(2,1)S(1)} %get-tuple-element.26), channel_id=1, source_target_pairs={{0,2},{1,3},{2,0},{3,1},{4,6},{5,7},{6,4},{7,5},{8,10},{9,11},{10,... | collective-permute-start | bytes 61448 | tf_op jit(solution)/shard_map/ppermute | solution.py:435

commit v9 on v7

--- a/solution.py
+++ b/solution.py
@@ -29,10 +29,6 @@
     if divisor & (divisor - 1):
         return values % divisor
     return values & (divisor - 1)
-
-
-def partners(n):
-    return [0] + list(range(n - 1, 0, -1))
 
 
 def chips(n):
@@ -247,6 +243,16 @@
     fold = jnp.where(fold, 1.0, 0.0).astype(jnp.bfloat16)
     meta_ref[...] = jnp.dot(small, fold, preferred_element_type=jnp.float32)
 
+    wanted = lax.broadcasted_iota(jnp.int32, (8, LANES), 1) == left
+    local = lax.dot_general(
+        jnp.where(wanted, 1.0, 0.0).astype(jnp.bfloat16),
+        meta_ref[...].astype(jnp.bfloat16),
+        (((1,), (1,)), ((), ())),
+        preferred_element_type=jnp.float32,
+    )
+    template = lax.broadcasted_iota(jnp.int32, (per_group, stations * here), 0) + 1
+    onehot = jnp.where(local[:1].astype(jnp.int32) == template, 1.0, 0.0).astype(jnp.bfloat16)
+
     ends = received(components * whole)
     for c in range(components):
         pieces = [received(c * whole + a) for a in range(whole)]
@@ -314,15 +320,10 @@
     slot = lax.broadcasted_iota(jnp.int32, (stations * here, LANES), 0)
     half = (slot < stations * here // 2) == (lane < LANES // 2)
     sh_ref[:, blocks * NK :] = jnp.where(half, 1.0, 0.0).astype(jnp.bfloat16)
-    local = meta_ref[:, left : left + 1].astype(jnp.int32) - 1
-    template = lax.broadcasted_iota(jnp.int32, (stations * here, per_group), 1)
-    onehot = jnp.where(local == template, 1.0, 0.0).astype(jnp.bfloat16)
-    stack_ref[...] = lax.dot_general(
-        onehot, sh_ref[...], (((0,), (0,)), ((), ())), preferred_element_type=jnp.float32
-    )
+    stack_ref[...] = jnp.dot(onehot, sh_ref[...], preferred_element_type=jnp.float32)
     me = lax.axis_index("stn")
-    for d, out_ref in zip(partners(len(out_refs)), out_refs):
-        owner = me ^ d
+    for d, out_ref in enumerate(out_refs):
+        owner = lax.rem(me + d, len(out_refs))
         theirs = pl.ds(pl.multiple_of(owner * TPD, TPD), TPD)
         out_ref[...] = stack_ref[theirs, :].astype(jnp.bfloat16)
 
@@ -405,8 +406,8 @@
         name="correlate",
     )(*([] if with_data else [samples]), chan_mask, *received)
     parts = [
-        lax.ppermute(part, "stn", [(i, i ^ d) for i in range(owners)]) if d else part
-        for d, part in zip(partners(owners), partial_stacks)
+        lax.ppermute(part, "stn", [(i, (i + d) % owners) for i in range(owners)]) if d else part
+        for d, part in enumerate(partial_stacks)
     ]
     return pl.pallas_call(
         functools.partial(finish_kernel, taps, blocks),

time: 26.5 us -> 26.2 us (0.989)
  waiting for transfers between devices: 9.59 us -> 8.02 us
  starting transfers between devices: 9.26 us -> 10.5 us
    ppermute x3, waiting for transfers between devices: 4 us -> 2.43 us  [body(): lax.ppermute(part, 'stn', [(i, (i + d) % owners) for i in range(owners)])]
    ppermute x3, starting transfers between devices: 4.45 us -> 5.68 us  [body(): lax.ppermute(part, 'stn', [(i, (i + d) % owners) for i in range(owners)])]
  transfers between devices with their start and end apart: 10 -> 10, of which waited for: 8 -> 9; matrix products, arithmetic and copies ran while one was open for 0% -> 0% of each run, Pallas kernels for 0% -> 0%
where the time goes in v9:
time: 26.2 us; the launch traced here: 26 us
  starting transfers between devices  10.5 us (40%)
  waiting for transfers between devices  8.02 us (31%)
  Pallas kernels  7.36 us (28%)
    ppermute x3, starting transfers between devices, body(): lax.ppermute(part, 'stn', [(i, (i + d) % owners) for i in range(owners)])  5.68 us
    ppermute x7, waiting for transfers between devices, swap(): return lax.ppermute(block, 'tmpl', [(i, i ^ d) for i in range(n)])  5.59 us
    pallas_call x1, Pallas kernels, body(): pl.pallas_call(functools.partial(correlate_kernel, (n, stations, blocks,...  5.13 us
    ppermute x7, starting transfers between devices, swap(): return lax.ppermute(block, 'tmpl', [(i, i ^ d) for i in range(n)])  4.8 us
    ppermute x3, waiting for transfers between devices, body(): lax.ppermute(part, 'stn', [(i, (i + d) % owners) for i in range(owners)])  2.43 us
    pallas_call x1, Pallas kernels, body(): pl.pallas_call(functools.partial(pack_kernel, (n, stations, slots, compon...  1.45 us
    pallas_call x1, Pallas kernels, body(): pl.pallas_call(functools.partial(finish_kernel, taps, blocks), out_shape=...  0.78 us
  transfers between devices with their start and end apart: 10, of which 9 were waited for; matrix products, arithmetic and copies ran while one was open for 0% of the time, Pallas kernels for 0%

profile of v9, /device:TPU:0, one launch (start us, length us, event | category | flops | bytes accessed | tf_op | source)
XLA Modules:
  0.0 26.0 jit_solution(4235293020429619281)
XLA Ops:
  0.0 1.4 %pack.1 = (bf16[208,128]{1,0:T(8,128)(2,1)S(1)}, bf16[208,128]{1,0:T(8,128)(2,1)S(1)}, bf16[384,128]{1,0:T(8,128)(2,1)S(1)}, bf16[384,128]{1,0:T(8,128)(2,1)S(1)}, bf16[384,128]{1,0:T(8,128)(2,1)S(1)}) custom-call(bf16[18,2,128]{2,1,0:T(2,128)(2,1)} %bitcast.8, bf16[18,16,300]{2,1,0:T(8,128)(2,1)} %bitcast.7, s32[6,1,16]{2,1,0:T(1,128)} %bitcast.9, ...), custom_call_target="tpu_custom_call" | custom-call | tf_op jit(solution)/shard_map/pack/pallas_call | solution.py:364
  1.5 4.0 %collective-permute-start = (bf16[384,128]{1,0:T(8,128)(2,1)S(1)}, bf16[384,128]{1,0:T(8,128)(2,1)S(1)}, u32[]{:S(2)}, u32[]{:S(2)}) collective-permute-start(bf16[384,128]{1,0:T(8,128)(2,1)S(1)} %get-tuple-element.17), channel_id=1, source_target_pairs={{0,24},{4,28},{8,16},{12,20},{16,8},{20,12},{24,0},{28,4},{1,25},{... | collective-permute-start | bytes 294920 | tf_op jit(solution)/shard_map/ppermute | solution.py:376
  5.4 0.0 copy-start
  5.4 0.5 %collective-permute-start.2 = (bf16[384,128]{1,0:T(8,128)(2,1)S(1)}, bf16[384,128]{1,0:T(8,128)(2,1)S(1)}, u32[]{:S(2)}, u32[]{:S(2)}) collective-permute-start(bf16[384,128]{1,0:T(8,128)(2,1)S(1)} %get-tuple-element.21), channel_id=1, source_target_pairs={{0,16},{4,20},{8,24},{12,28},{16,0},{20,4},{24,8},{28,12},{1,17},{... | collective-permute-start | bytes 294920 | tf_op jit(solution)/shard_map/ppermute | solution.py:376
  5.9 0.1 collective-permute-start.3
  6.1 0.0 collective-permute-start.1
  6.1 1.2 %collective-permute-done.1.refs_2_ = bf16[208,128]{1,0:T(8,128)(2,1)S(1)} collective-permute-done((bf16[208,128]{1,0:T(8,128)(2,1)S(1)}, bf16[208,128]{1,0:T(8,128)(2,1)S(1)}, u32[]{:S(2)}, u32[]{:S(2)}) %collective-permute-start.1) | collective-permute-done | bytes 53280 | tf_op jit(solution)/shard_map/ppermute | solution.py:376
  7.3 1.3 %collective-permute-done.refs_3_ = bf16[384,128]{1,0:T(8,128)(2,1)S(1)} collective-permute-done((bf16[384,128]{1,0:T(8,128)(2,1)S(1)}, bf16[384,128]{1,0:T(8,128)(2,1)S(1)}, u32[]{:S(2)}, u32[]{:S(2)}) %collective-permute-start) | collective-permute-done | bytes 98336 | tf_op jit(solution)/shard_map/ppermute | solution.py:376
  8.6 0.0 collective-permute-start.4
  8.6 1.7 %collective-permute-done.2.refs_4_ = bf16[384,128]{1,0:T(8,128)(2,1)S(1)} collective-permute-done((bf16[384,128]{1,0:T(8,128)(2,1)S(1)}, bf16[384,128]{1,0:T(8,128)(2,1)S(1)}, u32[]{:S(2)}, u32[]{:S(2)}) %collective-permute-start.2) | collective-permute-done | bytes 98336 | tf_op jit(solution)/shard_map/ppermute | solution.py:376
  10.3 0.0 collective-permute-start.5
  10.3 0.3 %collective-permute-done.3.refs_5_ = bf16[384,128]{1,0:T(8,128)(2,1)S(1)} collective-permute-done((bf16[384,128]{1,0:T(8,128)(2,1)S(1)}, bf16[384,128]{1,0:T(8,128)(2,1)S(1)}, u32[]{:S(2)}, u32[]{:S(2)}) %collective-permute-start.3) | collective-permute-done | bytes 98336 | tf_op jit(solution)/shard_map/ppermute | solution.py:376
  10.6 0.2 collective-permute-start.6
  10.8 0.0 copy-done
  10.8 0.1 copy.7.refs_0_
  10.9 0.0 collective-permute-done.4.refs_6_
  10.9 0.7 %collective-permute-done.5.refs_7_ = bf16[384,128]{1,0:T(8,128)(2,1)S(1)} collective-permute-done((bf16[384,128]{1,0:T(8,128)(2,1)S(1)}, bf16[384,128]{1,0:T(8,128)(2,1)S(1)}, u32[]{:S(2)}, u32[]{:S(2)}) %collective-permute-start.5) | collective-permute-done | bytes 98336 | tf_op jit(solution)/shard_map/ppermute | solution.py:376
  11.6 0.3 %collective-permute-done.6.refs_8_ = bf16[384,128]{1,0:T(8,128)(2,1)S(1)} collective-permute-done((bf16[384,128]{1,0:T(8,128)(2,1)S(1)}, bf16[384,128]{1,0:T(8,128)(2,1)S(1)}, u32[]{:S(2)}, u32[]{:S(2)}) %collective-permute-start.6) | collective-permute-done | bytes 98336 | tf_op jit(solution)/shard_map/ppermute | solution.py:376
  11.9 5.1 %correlate.1 = (bf16[16,640]{1,0:T(8,128)(2,1)S(1)}, bf16[16,640]{1,0:T(8,128)(2,1)S(1)}, bf16[16,640]{1,0:T(8,128)(2,1)S(1)}, bf16[16,640]{1,0:T(8,128)(2,1)S(1)}) custom-call(s32[6,3]{1,0:T(8,128)S(1)} %copy.7.refs_0_, bf16[208,128]{1,0:T(8,128)(2,1)S(1)} %get-tuple-element.16.refs_1_, bf16[208,128]{1,0:T(8,128)(2,1)S(1)} %collective-permute-done.1.refs_2_, ...), custom_call_target="tpu_custom_call" | custom-call | tf_op jit(solution)/shard_map/correlate/pallas_call | solution.py:387
  17.1 1.7 %collective-permute-start.7 = (bf16[16,640]{1,0:T(8,128)(2,1)S(1)}, bf16[16,640]{1,0:T(8,128)(2,1)S(1)}, u32[]{:S(2)}, u32[]{:S(2)}) collective-permute-start(bf16[16,640]{1,0:T(8,128)(2,1)S(1)} %get-tuple-element.24), channel_id=1, source_target_pairs={{0,1},{1,2},{2,3},{3,0},{4,5},{5,6},{6,7},{7,4},{8,9},{9,10},{10,1... | collective-permute-start | bytes 61448 | tf_op jit(solution)/shard_map/ppermute | solution.py:409
  18.8 2.6 %collective-permute-start.8 = (bf16[16,640]{1,0:T(8,128)(2,1)S(1)}, bf16[16,640]{1,0:T(8,128)(2,1)S(1)}, u32[]{:S(2)}, u32[]{:S(2)}) collective-permute-start(bf16[16,640]{1,0:T(8,128)(2,1)S(1)} %get-tuple-element.25), channel_id=1, source_target_pairs={{0,2},{1,3},{2,0},{3,1},{4,6},{5,7},{6,4},{7,5},{8,10},{9,11},{10,... | collective-permute-start | bytes 61448 | tf_op jit(solution)/shard_map/ppermute | solution.py:409
  21.4 1.3 %collective-permute-start.9 = (bf16[16,640]{1,0:T(8,128)(2,1)S(1)}, bf16[16,640]{1,0:T(8,128)(2,1)S(1)}, u32[]{:S(2)}, u32[]{:S(2)}) collective-permute-start(bf16[16,640]{1,0:T(8,128)(2,1)S(1)} %get-tuple-element.26), channel_id=1, source_target_pairs={{0,3},{1,0},{2,1},{3,2},{4,7},{5,4},{6,5},{7,6},{8,11},{9,8},{10,9... | collective-permute-start | bytes 61448 | tf_op jit(solution)/shard_map/ppermute | solution.py:409
  22.8 0.1 collective-permute-done.7.refs_1_
  22.8 0.9 %collective-permute-done.8.refs_2_ = bf16[16,640]{1,0:T(8,128)(2,1)S(1)} collective-permute-done((bf16[16,640]{1,0:T(8,128)(2,1)S(1)}, bf16[16,640]{1,0:T(8,128)(2,1)S(1)}, u32[]{:S(2)}, u32[]{:S(2)}) %collective-permute-start.8) | collective-permute-done | bytes 20512 | tf_op jit(solution)/shard_map/ppermute | solution.py:409
  23.7 1.5 %collective-permute-done.9.refs_3_ = bf16[16,640]{1,0:T(8,128)(2,1)S(1)} collective-permute-done((bf16[16,640]{1,0:T(8,128)(2,1)S(1)}, bf16[16,640]{1,0:T(8,128)(2,1)S(1)}, u32[]{:S(2)}, u32[]{:S(2)}) %collective-permute-start.9) | collective-permute-done | bytes 20512 | tf_op jit(solution)/shard_map/ppermute | solution.py:409
  25.2 0.8 %finish.1 = f32[2,16,256]{2,1,0:T(8,128)} custom-call(bf16[16,640]{1,0:T(8,128)(2,1)S(1)} %get-tuple-element.23.refs_0_, bf16[16,640]{1,0:T(8,128)(2,1)S(1)} %collective-permute-done.7.refs_1_, bf16[16,640]{1,0:T(8,128)(2,1)S(1)} %collective-permute-done.8.refs_2_, bf16[16,640]{1,0:T(8,128)(2,1)S(1)} %collective-permute-done.9.refs_3_), custom_call_target="tpu_custom_call" | custom-call | tf_op jit(solution)/shard_map/finish/pallas_call | solution.py:412
Async XLA Ops:
  1.5 7.1 %collective-permute-start = (bf16[384,128]{1,0:T(8,128)(2,1)S(1)}, bf16[384,128]{1,0:T(8,128)(2,1)S(1)}, u32[]{:S(2)}, u32[]{:S(2)}) collective-permute-start(bf16[384,128]{1,0:T(8,128)(2,1)S(1)} %get-tuple-element.17), channel_id=1, source_target_pairs={{0,24},{4,28},{8,16},{12,20},{16,8},{20,12},{24,0},{28,4},{1,25},{... | collective-permute-start | bytes 294920 | tf_op jit(solution)/shard_map/ppermute | solution.py:376
  5.4 5.4 %copy-start = (s32[6,3]{0,1:T(4,128)S(1)}, s32[6,3]{0,1:T(4,128)}, u32[]{:S(2)}) copy-start(s32[6,3]{0,1:T(4,128)} %param.11) | copy-start | bytes 220
  5.4 4.9 %collective-permute-start.2 = (bf16[384,128]{1,0:T(8,128)(2,1)S(1)}, bf16[384,128]{1,0:T(8,128)(2,1)S(1)}, u32[]{:S(2)}, u32[]{:S(2)}) collective-permute-start(bf16[384,128]{1,0:T(8,128)(2,1)S(1)} %get-tuple-element.21), channel_id=1, source_target_pairs={{0,16},{4,20},{8,24},{12,28},{16,0},{20,4},{24,8},{28,12},{1,17},{... | collective-permute-start | bytes 294920 | tf_op jit(solution)/shard_map/ppermute | solution.py:376
  5.9 4.7 %collective-permute-start.3 = (bf16[384,128]{1,0:T(8,128)(2,1)S(1)}, bf16[384,128]{1,0:T(8,128)(2,1)S(1)}, u32[]{:S(2)}, u32[]{:S(2)}) collective-permute-start(bf16[384,128]{1,0:T(8,128)(2,1)S(1)} %get-tuple-element.22), channel_id=1, source_target_pairs={{0,8},{4,12},{8,0},{12,4},{16,24},{20,28},{24,16},{28,20},{1,9},{5... | collective-permute-start | bytes 294920 | tf_op jit(solution)/shard_map/ppermute | solution.py:376
  6.1 1.2 %collective-permute-start.1 = (bf16[208,128]{1,0:T(8,128)(2,1)S(1)}, bf16[208,128]{1,0:T(8,128)(2,1)S(1)}, u32[]{:S(2)}, u32[]{:S(2)}) collective-permute-start(bf16[208,128]{1,0:T(8,128)(2,1)S(1)} %get-tuple-element.18), channel_id=1, source_target_pairs={{0,4},{4,0},{8,12},{12,8},{16,20},{20,16},{24,28},{28,24},{1,5},{5... | collective-permute-start | bytes 159752 | tf_op jit(solution)/shard_map/ppermute | solution.py:376
  8.6 2.3 %collective-permute-start.4 = (bf16[384,128]{1,0:T(8,128)(2,1)S(1)}, bf16[384,128]{1,0:T(8,128)(2,1)S(1)}, u32[]{:S(2)}, u32[]{:S(2)}) collective-permute-start(bf16[384,128]{1,0:T(8,128)(2,1)S(1)} %collective-permute-done.refs_3_), channel_id=1, source_target_pairs={{0,4},{4,0},{8,12},{12,8},{16,20},{20,16},{24,28},{28,24},{1,5},{5... | collective-permute-start | bytes 294920 | tf_op jit(solution)/shard_map/ppermute | solution.py:376
  10.3 1.3 %collective-permute-start.5 = (bf16[384,128]{1,0:T(8,128)(2,1)S(1)}, bf16[384,128]{1,0:T(8,128)(2,1)S(1)}, u32[]{:S(2)}, u32[]{:S(2)}) collective-permute-start(bf16[384,128]{1,0:T(8,128)(2,1)S(1)} %collective-permute-done.2.refs_4_), channel_id=1, source_target_pairs={{0,4},{4,0},{8,12},{12,8},{16,20},{20,16},{24,28},{28,24},{1,5},{5... | collective-permute-start | bytes 294920 | tf_op jit(solution)/shard_map/ppermute | solution.py:376
  10.6 1.3 %collective-permute-start.6 = (bf16[384,128]{1,0:T(8,128)(2,1)S(1)}, bf16[384,128]{1,0:T(8,128)(2,1)S(1)}, u32[]{:S(2)}, u32[]{:S(2)}) collective-permute-start(bf16[384,128]{1,0:T(8,128)(2,1)S(1)} %collective-permute-done.3.refs_5_), channel_id=1, source_target_pairs={{0,4},{4,0},{8,12},{12,8},{16,20},{20,16},{24,28},{28,24},{1,5},{5... | collective-permute-start | bytes 294920 | tf_op jit(solution)/shard_map/ppermute | solution.py:376
  17.1 5.7 %collective-permute-start.7 = (bf16[16,640]{1,0:T(8,128)(2,1)S(1)}, bf16[16,640]{1,0:T(8,128)(2,1)S(1)}, u32[]{:S(2)}, u32[]{:S(2)}) collective-permute-start(bf16[16,640]{1,0:T(8,128)(2,1)S(1)} %get-tuple-element.24), channel_id=1, source_target_pairs={{0,1},{1,2},{2,3},{3,0},{4,5},{5,6},{6,7},{7,4},{8,9},{9,10},{10,1... | collective-permute-start | bytes 61448 | tf_op jit(solution)/shard_map/ppermute | solution.py:409
  18.8 4.9 %collective-permute-start.8 = (bf16[16,640]{1,0:T(8,128)(2,1)S(1)}, bf16[16,640]{1,0:T(8,128)(2,1)S(1)}, u32[]{:S(2)}, u32[]{:S(2)}) collective-permute-start(bf16[16,640]{1,0:T(8,128)(2,1)S(1)} %get-tuple-element.25), channel_id=1, source_target_pairs={{0,2},{1,3},{2,0},{3,1},{4,6},{5,7},{6,4},{7,5},{8,10},{9,11},{10,... | collective-permute-start | bytes 61448 | tf_op jit(solution)/shard_map/ppermute | solution.py:409
  21.4 3.8 %collective-permute-start.9 = (bf16[16,640]{1,0:T(8,128)(2,1)S(1)}, bf16[16,640]{1,0:T(8,128)(2,1)S(1)}, u32[]{:S(2)}, u32[]{:S(2)}) collective-permute-start(bf16[16,640]{1,0:T(8,128)(2,1)S(1)} %get-tuple-element.26), channel_id=1, source_target_pairs={{0,3},{1,0},{2,1},{3,2},{4,7},{5,4},{6,5},{7,6},{8,11},{9,8},{10,9... | collective-permute-start | bytes 61448 | tf_op jit(solution)/shard_map/ppermute | solution.py:409

commit v10 on v9

--- a/solution.py
+++ b/solution.py
@@ -29,6 +29,10 @@
     if divisor & (divisor - 1):
         return values % divisor
     return values & (divisor - 1)
+
+
+def rotations(n):
+    return [0] + [d for d in [n // 2] if d] + [d for d in range(1, n) if d != n // 2]
 
 
 def chips(n):
@@ -322,7 +326,7 @@
     sh_ref[:, blocks * NK :] = jnp.where(half, 1.0, 0.0).astype(jnp.bfloat16)
     stack_ref[...] = jnp.dot(onehot, sh_ref[...], preferred_element_type=jnp.float32)
     me = lax.axis_index("stn")
-    for d, out_ref in enumerate(out_refs):
+    for d, out_ref in zip(rotations(len(out_refs)), out_refs):
         owner = lax.rem(me + d, len(out_refs))
         theirs = pl.ds(pl.multiple_of(owner * TPD, TPD), TPD)
         out_ref[...] = stack_ref[theirs, :].astype(jnp.bfloat16)
@@ -407,7 +411,7 @@
     )(*([] if with_data else [samples]), chan_mask, *received)
     parts = [
         lax.ppermute(part, "stn", [(i, (i + d) % owners) for i in range(owners)]) if d else part
-        for d, part in enumerate(partial_stacks)
+        for d, part in zip(rotations(owners), partial_stacks)
     ]
     return pl.pallas_call(
         functools.partial(finish_kernel, taps, blocks),

time: 26.2 us -> 26.4 us (level)
  starting transfers between devices: 10.5 us -> 11.4 us
  waiting for transfers between devices: 8.02 us -> 7.34 us
    ppermute x3, starting transfers between devices: 5.68 us -> 6.6 us  [body(): lax.ppermute(part, 'stn', [(i, (i + d) % owners) for i in range(owners)])]
    ppermute x3, waiting for transfers between devices: 2.43 us -> 1.76 us  [body(): lax.ppermute(part, 'stn', [(i, (i + d) % owners) for i in range(owners)])]
  transfers between devices with their start and end apart: 10 -> 10, of which waited for: 9 -> 7; matrix products, arithmetic and copies ran while one was open for 0% -> 0% of each run, Pallas kernels for 0% -> 0%
where the time goes in v10:
time: 26.4 us; the launch traced here: 26.2 us
  starting transfers between devices  11.4 us (43%)
  Pallas kernels  7.36 us (28%)
  waiting for transfers between devices  7.34 us (28%)
    ppermute x3, starting transfers between devices, body(): lax.ppermute(part, 'stn', [(i, (i + d) % owners) for i in range(owners)])  6.6 us
    ppermute x7, waiting for transfers between devices, swap(): return lax.ppermute(block, 'tmpl', [(i, i ^ d) for i in range(n)])  5.59 us
    pallas_call x1, Pallas kernels, body(): pl.pallas_call(functools.partial(correlate_kernel, (n, stations, blocks,...  5.13 us
    ppermute x7, starting transfers between devices, swap(): return lax.ppermute(block, 'tmpl', [(i, i ^ d) for i in range(n)])  4.8 us
    ppermute x3, waiting for transfers between devices, body(): lax.ppermute(part, 'stn', [(i, (i + d) % owners) for i in range(owners)])  1.76 us
    pallas_call x1, Pallas kernels, body(): pl.pallas_call(functools.partial(pack_kernel, (n, stations, slots, compon...  1.45 us
    pallas_call x1, Pallas kernels, body(): pl.pallas_call(functools.partial(finish_kernel, taps, blocks), out_shape=...  0.78 us
  transfers between devices with their start and end apart: 10, of which 7 were waited for; matrix products, arithmetic and copies ran while one was open for 0% of the time, Pallas kernels for 0%

profile of v10, /device:TPU:0, one launch (start us, length us, event | category | flops | bytes accessed | tf_op | source)
XLA Modules:
  0.0 26.2 jit_solution(18350166176121711132)
XLA Ops:
  0.0 1.4 %pack.1 = (bf16[208,128]{1,0:T(8,128)(2,1)S(1)}, bf16[208,128]{1,0:T(8,128)(2,1)S(1)}, bf16[384,128]{1,0:T(8,128)(2,1)S(1)}, bf16[384,128]{1,0:T(8,128)(2,1)S(1)}, bf16[384,128]{1,0:T(8,128)(2,1)S(1)}) custom-call(bf16[18,2,128]{2,1,0:T(2,128)(2,1)} %bitcast.8, bf16[18,16,300]{2,1,0:T(8,128)(2,1)} %bitcast.7, s32[6,1,16]{2,1,0:T(1,128)} %bitcast.9, ...), custom_call_target="tpu_custom_call" | custom-call | tf_op jit(solution)/shard_map/pack/pallas_call | solution.py:368
  1.5 4.0 %collective-permute-start = (bf16[384,128]{1,0:T(8,128)(2,1)S(1)}, bf16[384,128]{1,0:T(8,128)(2,1)S(1)}, u32[]{:S(2)}, u32[]{:S(2)}) collective-permute-start(bf16[384,128]{1,0:T(8,128)(2,1)S(1)} %get-tuple-element.17), channel_id=1, source_target_pairs={{0,24},{4,28},{8,16},{12,20},{16,8},{20,12},{24,0},{28,4},{1,25},{... | collective-permute-start | bytes 294920 | tf_op jit(solution)/shard_map/ppermute | solution.py:380
  5.4 0.0 copy-start
  5.4 0.5 %collective-permute-start.2 = (bf16[384,128]{1,0:T(8,128)(2,1)S(1)}, bf16[384,128]{1,0:T(8,128)(2,1)S(1)}, u32[]{:S(2)}, u32[]{:S(2)}) collective-permute-start(bf16[384,128]{1,0:T(8,128)(2,1)S(1)} %get-tuple-element.21), channel_id=1, source_target_pairs={{0,16},{4,20},{8,24},{12,28},{16,0},{20,4},{24,8},{28,12},{1,17},{... | collective-permute-start | bytes 294920 | tf_op jit(solution)/shard_map/ppermute | solution.py:380
  5.9 0.1 collective-permute-start.3
  6.1 0.0 collective-permute-start.1
  6.1 1.2 %collective-permute-done.1.refs_2_ = bf16[208,128]{1,0:T(8,128)(2,1)S(1)} collective-permute-done((bf16[208,128]{1,0:T(8,128)(2,1)S(1)}, bf16[208,128]{1,0:T(8,128)(2,1)S(1)}, u32[]{:S(2)}, u32[]{:S(2)}) %collective-permute-start.1) | collective-permute-done | bytes 53280 | tf_op jit(solution)/shard_map/ppermute | solution.py:380
  7.3 1.3 %collective-permute-done.refs_3_ = bf16[384,128]{1,0:T(8,128)(2,1)S(1)} collective-permute-done((bf16[384,128]{1,0:T(8,128)(2,1)S(1)}, bf16[384,128]{1,0:T(8,128)(2,1)S(1)}, u32[]{:S(2)}, u32[]{:S(2)}) %collective-permute-start) | collective-permute-done | bytes 98336 | tf_op jit(solution)/shard_map/ppermute | solution.py:380
  8.6 0.0 collective-permute-start.4
  8.6 1.7 %collective-permute-done.2.refs_4_ = bf16[384,128]{1,0:T(8,128)(2,1)S(1)} collective-permute-done((bf16[384,128]{1,0:T(8,128)(2,1)S(1)}, bf16[384,128]{1,0:T(8,128)(2,1)S(1)}, u32[]{:S(2)}, u32[]{:S(2)}) %collective-permute-start.2) | collective-permute-done | bytes 98336 | tf_op jit(solution)/shard_map/ppermute | solution.py:380
  10.3 0.0 collective-permute-start.5
  10.3 0.3 %collective-permute-done.3.refs_5_ = bf16[384,128]{1,0:T(8,128)(2,1)S(1)} collective-permute-done((bf16[384,128]{1,0:T(8,128)(2,1)S(1)}, bf16[384,128]{1,0:T(8,128)(2,1)S(1)}, u32[]{:S(2)}, u32[]{:S(2)}) %collective-permute-start.3) | collective-permute-done | bytes 98336 | tf_op jit(solution)/shard_map/ppermute | solution.py:380
  10.6 0.2 collective-permute-start.6
  10.8 0.0 copy-done
  10.8 0.1 copy.7.refs_0_
  10.9 0.0 collective-permute-done.4.refs_6_
  10.9 0.7 %collective-permute-done.5.refs_7_ = bf16[384,128]{1,0:T(8,128)(2,1)S(1)} collective-permute-done((bf16[384,128]{1,0:T(8,128)(2,1)S(1)}, bf16[384,128]{1,0:T(8,128)(2,1)S(1)}, u32[]{:S(2)}, u32[]{:S(2)}) %collective-permute-start.5) | collective-permute-done | bytes 98336 | tf_op jit(solution)/shard_map/ppermute | solution.py:380
  11.6 0.3 %collective-permute-done.6.refs_8_ = bf16[384,128]{1,0:T(8,128)(2,1)S(1)} collective-permute-done((bf16[384,128]{1,0:T(8,128)(2,1)S(1)}, bf16[384,128]{1,0:T(8,128)(2,1)S(1)}, u32[]{:S(2)}, u32[]{:S(2)}) %collective-permute-start.6) | collective-permute-done | bytes 98336 | tf_op jit(solution)/shard_map/ppermute | solution.py:380
  11.9 5.1 %correlate.1 = (bf16[16,640]{1,0:T(8,128)(2,1)S(1)}, bf16[16,640]{1,0:T(8,128)(2,1)S(1)}, bf16[16,640]{1,0:T(8,128)(2,1)S(1)}, bf16[16,640]{1,0:T(8,128)(2,1)S(1)}) custom-call(s32[6,3]{1,0:T(8,128)S(1)} %copy.7.refs_0_, bf16[208,128]{1,0:T(8,128)(2,1)S(1)} %get-tuple-element.16.refs_1_, bf16[208,128]{1,0:T(8,128)(2,1)S(1)} %collective-permute-done.1.refs_2_, ...), custom_call_target="tpu_custom_call" | custom-call | tf_op jit(solution)/shard_map/correlate/pallas_call | solution.py:391
  17.1 2.8 %collective-permute-start.7 = (bf16[16,640]{1,0:T(8,128)(2,1)S(1)}, bf16[16,640]{1,0:T(8,128)(2,1)S(1)}, u32[]{:S(2)}, u32[]{:S(2)}) collective-permute-start(bf16[16,640]{1,0:T(8,128)(2,1)S(1)} %get-tuple-element.24), channel_id=1, source_target_pairs={{0,2},{1,3},{2,0},{3,1},{4,6},{5,7},{6,4},{7,5},{8,10},{9,11},{10,... | collective-permute-start | bytes 61448 | tf_op jit(solution)/shard_map/ppermute | solution.py:413
  19.9 1.6 %collective-permute-start.8 = (bf16[16,640]{1,0:T(8,128)(2,1)S(1)}, bf16[16,640]{1,0:T(8,128)(2,1)S(1)}, u32[]{:S(2)}, u32[]{:S(2)}) collective-permute-start(bf16[16,640]{1,0:T(8,128)(2,1)S(1)} %get-tuple-element.25), channel_id=1, source_target_pairs={{0,1},{1,2},{2,3},{3,0},{4,5},{5,6},{6,7},{7,4},{8,9},{9,10},{10,1... | collective-permute-start | bytes 61448 | tf_op jit(solution)/shard_map/ppermute | solution.py:413
  21.4 2.2 %collective-permute-start.9 = (bf16[16,640]{1,0:T(8,128)(2,1)S(1)}, bf16[16,640]{1,0:T(8,128)(2,1)S(1)}, u32[]{:S(2)}, u32[]{:S(2)}) collective-permute-start(bf16[16,640]{1,0:T(8,128)(2,1)S(1)} %get-tuple-element.26), channel_id=1, source_target_pairs={{0,3},{1,0},{2,1},{3,2},{4,7},{5,4},{6,5},{7,6},{8,11},{9,8},{10,9... | collective-permute-start | bytes 61448 | tf_op jit(solution)/shard_map/ppermute | solution.py:413
  23.7 0.0 collective-permute-done.7.refs_1_
  23.7 1.8 %collective-permute-done.8.refs_2_ = bf16[16,640]{1,0:T(8,128)(2,1)S(1)} collective-permute-done((bf16[16,640]{1,0:T(8,128)(2,1)S(1)}, bf16[16,640]{1,0:T(8,128)(2,1)S(1)}, u32[]{:S(2)}, u32[]{:S(2)}) %collective-permute-start.8) | collective-permute-done | bytes 20512 | tf_op jit(solution)/shard_map/ppermute | solution.py:413
  25.4 0.0 collective-permute-done.9.refs_3_
  25.4 0.8 %finish.1 = f32[2,16,256]{2,1,0:T(8,128)} custom-call(bf16[16,640]{1,0:T(8,128)(2,1)S(1)} %get-tuple-element.23.refs_0_, bf16[16,640]{1,0:T(8,128)(2,1)S(1)} %collective-permute-done.7.refs_1_, bf16[16,640]{1,0:T(8,128)(2,1)S(1)} %collective-permute-done.8.refs_2_, bf16[16,640]{1,0:T(8,128)(2,1)S(1)} %collective-permute-done.9.refs_3_), custom_call_target="tpu_custom_call" | custom-call | tf_op jit(solution)/shard_map/finish/pallas_call | solution.py:416
Async XLA Ops:
  1.5 7.1 %collective-permute-start = (bf16[384,128]{1,0:T(8,128)(2,1)S(1)}, bf16[384,128]{1,0:T(8,128)(2,1)S(1)}, u32[]{:S(2)}, u32[]{:S(2)}) collective-permute-start(bf16[384,128]{1,0:T(8,128)(2,1)S(1)} %get-tuple-element.17), channel_id=1, source_target_pairs={{0,24},{4,28},{8,16},{12,20},{16,8},{20,12},{24,0},{28,4},{1,25},{... | collective-permute-start | bytes 294920 | tf_op jit(solution)/shard_map/ppermute | solution.py:380
  5.4 5.4 %copy-start = (s32[6,3]{0,1:T(4,128)S(1)}, s32[6,3]{0,1:T(4,128)}, u32[]{:S(2)}) copy-start(s32[6,3]{0,1:T(4,128)} %param.11) | copy-start | bytes 220
  5.4 4.9 %collective-permute-start.2 = (bf16[384,128]{1,0:T(8,128)(2,1)S(1)}, bf16[384,128]{1,0:T(8,128)(2,1)S(1)}, u32[]{:S(2)}, u32[]{:S(2)}) collective-permute-start(bf16[384,128]{1,0:T(8,128)(2,1)S(1)} %get-tuple-element.21), channel_id=1, source_target_pairs={{0,16},{4,20},{8,24},{12,28},{16,0},{20,4},{24,8},{28,12},{1,17},{... | collective-permute-start | bytes 294920 | tf_op jit(solution)/shard_map/ppermute | solution.py:380
  5.9 4.7 %collective-permute-start.3 = (bf16[384,128]{1,0:T(8,128)(2,1)S(1)}, bf16[384,128]{1,0:T(8,128)(2,1)S(1)}, u32[]{:S(2)}, u32[]{:S(2)}) collective-permute-start(bf16[384,128]{1,0:T(8,128)(2,1)S(1)} %get-tuple-element.22), channel_id=1, source_target_pairs={{0,8},{4,12},{8,0},{12,4},{16,24},{20,28},{24,16},{28,20},{1,9},{5... | collective-permute-start | bytes 294920 | tf_op jit(solution)/shard_map/ppermute | solution.py:380
  6.1 1.2 %collective-permute-start.1 = (bf16[208,128]{1,0:T(8,128)(2,1)S(1)}, bf16[208,128]{1,0:T(8,128)(2,1)S(1)}, u32[]{:S(2)}, u32[]{:S(2)}) collective-permute-start(bf16[208,128]{1,0:T(8,128)(2,1)S(1)} %get-tuple-element.18), channel_id=1, source_target_pairs={{0,4},{4,0},{8,12},{12,8},{16,20},{20,16},{24,28},{28,24},{1,5},{5... | collective-permute-start | bytes 159752 | tf_op jit(solution)/shard_map/ppermute | solution.py:380
  8.6 2.3 %collective-permute-start.4 = (bf16[384,128]{1,0:T(8,128)(2,1)S(1)}, bf16[384,128]{1,0:T(8,128)(2,1)S(1)}, u32[]{:S(2)}, u32[]{:S(2)}) collective-permute-start(bf16[384,128]{1,0:T(8,128)(2,1)S(1)} %collective-permute-done.refs_3_), channel_id=1, source_target_pairs={{0,4},{4,0},{8,12},{12,8},{16,20},{20,16},{24,28},{28,24},{1,5},{5... | collective-permute-start | bytes 294920 | tf_op jit(solution)/shard_map/ppermute | solution.py:380
  10.3 1.3 %collective-permute-start.5 = (bf16[384,128]{1,0:T(8,128)(2,1)S(1)}, bf16[384,128]{1,0:T(8,128)(2,1)S(1)}, u32[]{:S(2)}, u32[]{:S(2)}) collective-permute-start(bf16[384,128]{1,0:T(8,128)(2,1)S(1)} %collective-permute-done.2.refs_4_), channel_id=1, source_target_pairs={{0,4},{4,0},{8,12},{12,8},{16,20},{20,16},{24,28},{28,24},{1,5},{5... | collective-permute-start | bytes 294920 | tf_op jit(solution)/shard_map/ppermute | solution.py:380
  10.6 1.3 %collective-permute-start.6 = (bf16[384,128]{1,0:T(8,128)(2,1)S(1)}, bf16[384,128]{1,0:T(8,128)(2,1)S(1)}, u32[]{:S(2)}, u32[]{:S(2)}) collective-permute-start(bf16[384,128]{1,0:T(8,128)(2,1)S(1)} %collective-permute-done.3.refs_5_), channel_id=1, source_target_pairs={{0,4},{4,0},{8,12},{12,8},{16,20},{20,16},{24,28},{28,24},{1,5},{5... | collective-permute-start | bytes 294920 | tf_op jit(solution)/shard_map/ppermute | solution.py:380
  17.1 6.6 %collective-permute-start.7 = (bf16[16,640]{1,0:T(8,128)(2,1)S(1)}, bf16[16,640]{1,0:T(8,128)(2,1)S(1)}, u32[]{:S(2)}, u32[]{:S(2)}) collective-permute-start(bf16[16,640]{1,0:T(8,128)(2,1)S(1)} %get-tuple-element.24), channel_id=1, source_target_pairs={{0,2},{1,3},{2,0},{3,1},{4,6},{5,7},{6,4},{7,5},{8,10},{9,11},{10,... | collective-permute-start | bytes 61448 | tf_op jit(solution)/shard_map/ppermute | solution.py:413
  19.9 5.6 %collective-permute-start.8 = (bf16[16,640]{1,0:T(8,128)(2,1)S(1)}, bf16[16,640]{1,0:T(8,128)(2,1)S(1)}, u32[]{:S(2)}, u32[]{:S(2)}) collective-permute-start(bf16[16,640]{1,0:T(8,128)(2,1)S(1)} %get-tuple-element.25), channel_id=1, source_target_pairs={{0,1},{1,2},{2,3},{3,0},{4,5},{5,6},{6,7},{7,4},{8,9},{9,10},{10,1... | collective-permute-start | bytes 61448 | tf_op jit(solution)/shard_map/ppermute | solution.py:413
  21.4 4.0 %collective-permute-start.9 = (bf16[16,640]{1,0:T(8,128)(2,1)S(1)}, bf16[16,640]{1,0:T(8,128)(2,1)S(1)}, u32[]{:S(2)}, u32[]{:S(2)}) collective-permute-start(bf16[16,640]{1,0:T(8,128)(2,1)S(1)} %get-tuple-element.26), channel_id=1, source_target_pairs={{0,3},{1,0},{2,1},{3,2},{4,7},{5,4},{6,5},{7,6},{8,11},{9,8},{10,9... | collective-permute-start | bytes 61448 | tf_op jit(solution)/shard_map/ppermute | solution.py:413

commit v11 on v10

--- a/solution.py
+++ b/solution.py
@@ -32,7 +32,7 @@
 
 
 def rotations(n):
-    return [0] + [d for d in [n // 2] if d] + [d for d in range(1, n) if d != n // 2]
+    return [0] + list(range(n - 1, 0, -1))
 
 
 def chips(n):

time: 26.4 us -> 27.4 us (1.038)
  waiting for transfers between devices: 7.34 us -> 10.2 us
  starting transfers between devices: 11.4 us -> 9.59 us
    ppermute x3, waiting for transfers between devices: 1.76 us -> 4.57 us  [body(): lax.ppermute(part, 'stn', [(i, (i + d) % owners) for i in range(owners)])]
    ppermute x3, starting transfers between devices: 6.6 us -> 4.78 us  [body(): lax.ppermute(part, 'stn', [(i, (i + d) % owners) for i in range(owners)])]
  transfers between devices with their start and end apart: 10 -> 10, of which waited for: 7 -> 9; matrix products, arithmetic and copies ran while one was open for 0% -> 0% of each run, Pallas kernels for 0% -> 0%
where the time goes in v11:
time: 27.4 us; the launch traced here: 27.2 us
  waiting for transfers between devices  10.2 us (37%)
  starting transfers between devices  9.59 us (35%)
  Pallas kernels  7.36 us (27%)
    ppermute x7, waiting for transfers between devices, swap(): return lax.ppermute(block, 'tmpl', [(i, i ^ d) for i in range(n)])  5.59 us
    pallas_call x1, Pallas kernels, body(): pl.pallas_call(functools.partial(correlate_kernel, (n, stations, blocks,...  5.13 us
    ppermute x7, starting transfers between devices, swap(): return lax.ppermute(block, 'tmpl', [(i, i ^ d) for i in range(n)])  4.8 us
    ppermute x3, starting transfers between devices, body(): lax.ppermute(part, 'stn', [(i, (i + d) % owners) for i in range(owners)])  4.78 us
    ppermute x3, waiting for transfers between devices, body(): lax.ppermute(part, 'stn', [(i, (i + d) % owners) for i in range(owners)])  4.57 us
    pallas_call x1, Pallas kernels, body(): pl.pallas_call(functools.partial(pack_kernel, (n, stations, slots, compon...  1.45 us
    pallas_call x1, Pallas kernels, body(): pl.pallas_call(functools.partial(finish_kernel, taps, blocks), out_shape=...  0.78 us
  transfers between devices with their start and end apart: 10, of which 9 were waited for; matrix products, arithmetic and copies ran while one was open for 0% of the time, Pallas kernels for 0%

profile of v11, /device:TPU:0, one launch (start us, length us, event | category | flops | bytes accessed | tf_op | source)
XLA Modules:
  0.0 27.2 jit_solution(1044783984768661082)
XLA Ops:
  0.0 1.4 %pack.1 = (bf16[208,128]{1,0:T(8,128)(2,1)S(1)}, bf16[208,128]{1,0:T(8,128)(2,1)S(1)}, bf16[384,128]{1,0:T(8,128)(2,1)S(1)}, bf16[384,128]{1,0:T(8,128)(2,1)S(1)}, bf16[384,128]{1,0:T(8,128)(2,1)S(1)}) custom-call(bf16[18,2,128]{2,1,0:T(2,128)(2,1)} %bitcast.8, bf16[18,16,300]{2,1,0:T(8,128)(2,1)} %bitcast.7, s32[6,1,16]{2,1,0:T(1,128)} %bitcast.9, ...), custom_call_target="tpu_custom_call" | custom-call | tf_op jit(solution)/shard_map/pack/pallas_call | solution.py:368
  1.5 4.0 %collective-permute-start = (bf16[384,128]{1,0:T(8,128)(2,1)S(1)}, bf16[384,128]{1,0:T(8,128)(2,1)S(1)}, u32[]{:S(2)}, u32[]{:S(2)}) collective-permute-start(bf16[384,128]{1,0:T(8,128)(2,1)S(1)} %get-tuple-element.17), channel_id=1, source_target_pairs={{0,24},{4,28},{8,16},{12,20},{16,8},{20,12},{24,0},{28,4},{1,25},{... | collective-permute-start | bytes 294920 | tf_op jit(solution)/shard_map/ppermute | solution.py:380
  5.4 0.0 copy-start
  5.4 0.5 %collective-permute-start.2 = (bf16[384,128]{1,0:T(8,128)(2,1)S(1)}, bf16[384,128]{1,0:T(8,128)(2,1)S(1)}, u32[]{:S(2)}, u32[]{:S(2)}) collective-permute-start(bf16[384,128]{1,0:T(8,128)(2,1)S(1)} %get-tuple-element.21), channel_id=1, source_target_pairs={{0,16},{4,20},{8,24},{12,28},{16,0},{20,4},{24,8},{28,12},{1,17},{... | collective-permute-start | bytes 294920 | tf_op jit(solution)/shard_map/ppermute | solution.py:380
  5.9 0.1 collective-permute-start.3
  6.1 0.0 collective-permute-start.1
  6.1 1.2 %collective-permute-done.1.refs_2_ = bf16[208,128]{1,0:T(8,128)(2,1)S(1)} collective-permute-done((bf16[208,128]{1,0:T(8,128)(2,1)S(1)}, bf16[208,128]{1,0:T(8,128)(2,1)S(1)}, u32[]{:S(2)}, u32[]{:S(2)}) %collective-permute-start.1) | collective-permute-done | bytes 53280 | tf_op jit(solution)/shard_map/ppermute | solution.py:380
  7.3 1.3 %collective-permute-done.refs_3_ = bf16[384,128]{1,0:T(8,128)(2,1)S(1)} collective-permute-done((bf16[384,128]{1,0:T(8,128)(2,1)S(1)}, bf16[384,128]{1,0:T(8,128)(2,1)S(1)}, u32[]{:S(2)}, u32[]{:S(2)}) %collective-permute-start) | collective-permute-done | bytes 98336 | tf_op jit(solution)/shard_map/ppermute | solution.py:380
  8.6 0.0 collective-permute-start.4
  8.6 1.7 %collective-permute-done.2.refs_4_ = bf16[384,128]{1,0:T(8,128)(2,1)S(1)} collective-permute-done((bf16[384,128]{1,0:T(8,128)(2,1)S(1)}, bf16[384,128]{1,0:T(8,128)(2,1)S(1)}, u32[]{:S(2)}, u32[]{:S(2)}) %collective-permute-start.2) | collective-permute-done | bytes 98336 | tf_op jit(solution)/shard_map/ppermute | solution.py:380
  10.3 0.0 collective-permute-start.5
  10.3 0.3 %collective-permute-done.3.refs_5_ = bf16[384,128]{1,0:T(8,128)(2,1)S(1)} collective-permute-done((bf16[384,128]{1,0:T(8,128)(2,1)S(1)}, bf16[384,128]{1,0:T(8,128)(2,1)S(1)}, u32[]{:S(2)}, u32[]{:S(2)}) %collective-permute-start.3) | collective-permute-done | bytes 98336 | tf_op jit(solution)/shard_map/ppermute | solution.py:380
  10.6 0.2 collective-permute-start.6
  10.8 0.0 copy-done
  10.8 0.1 copy.7.refs_0_
  10.9 0.0 collective-permute-done.4.refs_6_
  10.9 0.7 %collective-permute-done.5.refs_7_ = bf16[384,128]{1,0:T(8,128)(2,1)S(1)} collective-permute-done((bf16[384,128]{1,0:T(8,128)(2,1)S(1)}, bf16[384,128]{1,0:T(8,128)(2,1)S(1)}, u32[]{:S(2)}, u32[]{:S(2)}) %collective-permute-start.5) | collective-permute-done | bytes 98336 | tf_op jit(solution)/shard_map/ppermute | solution.py:380
  11.6 0.3 %collective-permute-done.6.refs_8_ = bf16[384,128]{1,0:T(8,128)(2,1)S(1)} collective-permute-done((bf16[384,128]{1,0:T(8,128)(2,1)S(1)}, bf16[384,128]{1,0:T(8,128)(2,1)S(1)}, u32[]{:S(2)}, u32[]{:S(2)}) %collective-permute-start.6) | collective-permute-done | bytes 98336 | tf_op jit(solution)/shard_map/ppermute | solution.py:380
  11.9 5.1 %correlate.1 = (bf16[16,640]{1,0:T(8,128)(2,1)S(1)}, bf16[16,640]{1,0:T(8,128)(2,1)S(1)}, bf16[16,640]{1,0:T(8,128)(2,1)S(1)}, bf16[16,640]{1,0:T(8,128)(2,1)S(1)}) custom-call(s32[6,3]{1,0:T(8,128)S(1)} %copy.7.refs_0_, bf16[208,128]{1,0:T(8,128)(2,1)S(1)} %get-tuple-element.16.refs_1_, bf16[208,128]{1,0:T(8,128)(2,1)S(1)} %collective-permute-done.1.refs_2_, ...), custom_call_target="tpu_custom_call" | custom-call | tf_op jit(solution)/shard_map/correlate/pallas_call | solution.py:391
  17.1 3.8 %collective-permute-start.7 = (bf16[16,640]{1,0:T(8,128)(2,1)S(1)}, bf16[16,640]{1,0:T(8,128)(2,1)S(1)}, u32[]{:S(2)}, u32[]{:S(2)}) collective-permute-start(bf16[16,640]{1,0:T(8,128)(2,1)S(1)} %get-tuple-element.24), channel_id=1, source_target_pairs={{0,3},{1,0},{2,1},{3,2},{4,7},{5,4},{6,5},{7,6},{8,11},{9,8},{10,9... | collective-permute-start | bytes 61448 | tf_op jit(solution)/shard_map/ppermute | solution.py:413
  20.9 0.0 collective-permute-start.8
  20.9 1.0 %collective-permute-start.9 = (bf16[16,640]{1,0:T(8,128)(2,1)S(1)}, bf16[16,640]{1,0:T(8,128)(2,1)S(1)}, u32[]{:S(2)}, u32[]{:S(2)}) collective-permute-start(bf16[16,640]{1,0:T(8,128)(2,1)S(1)} %get-tuple-element.26), channel_id=1, source_target_pairs={{0,1},{1,2},{2,3},{3,0},{4,5},{5,6},{6,7},{7,4},{8,9},{9,10},{10,1... | collective-permute-start | bytes 61448 | tf_op jit(solution)/shard_map/ppermute | solution.py:413
  21.9 0.5 %collective-permute-done.7.refs_1_ = bf16[16,640]{1,0:T(8,128)(2,1)S(1)} collective-permute-done((bf16[16,640]{1,0:T(8,128)(2,1)S(1)}, bf16[16,640]{1,0:T(8,128)(2,1)S(1)}, u32[]{:S(2)}, u32[]{:S(2)}) %collective-permute-start.7) | collective-permute-done | bytes 20512 | tf_op jit(solution)/shard_map/ppermute | solution.py:413
  22.3 3.4 %collective-permute-done.8.refs_2_ = bf16[16,640]{1,0:T(8,128)(2,1)S(1)} collective-permute-done((bf16[16,640]{1,0:T(8,128)(2,1)S(1)}, bf16[16,640]{1,0:T(8,128)(2,1)S(1)}, u32[]{:S(2)}, u32[]{:S(2)}) %collective-permute-start.8) | collective-permute-done | bytes 20512 | tf_op jit(solution)/shard_map/ppermute | solution.py:413
  25.8 0.7 %collective-permute-done.9.refs_3_ = bf16[16,640]{1,0:T(8,128)(2,1)S(1)} collective-permute-done((bf16[16,640]{1,0:T(8,128)(2,1)S(1)}, bf16[16,640]{1,0:T(8,128)(2,1)S(1)}, u32[]{:S(2)}, u32[]{:S(2)}) %collective-permute-start.9) | collective-permute-done | bytes 20512 | tf_op jit(solution)/shard_map/ppermute | solution.py:413
  26.4 0.8 %finish.1 = f32[2,16,256]{2,1,0:T(8,128)} custom-call(bf16[16,640]{1,0:T(8,128)(2,1)S(1)} %get-tuple-element.23.refs_0_, bf16[16,640]{1,0:T(8,128)(2,1)S(1)} %collective-permute-done.7.refs_1_, bf16[16,640]{1,0:T(8,128)(2,1)S(1)} %collective-permute-done.8.refs_2_, bf16[16,640]{1,0:T(8,128)(2,1)S(1)} %collective-permute-done.9.refs_3_), custom_call_target="tpu_custom_call" | custom-call | tf_op jit(solution)/shard_map/finish/pallas_call | solution.py:416
Async XLA Ops:
  1.5 7.1 %collective-permute-start = (bf16[384,128]{1,0:T(8,128)(2,1)S(1)}, bf16[384,128]{1,0:T(8,128)(2,1)S(1)}, u32[]{:S(2)}, u32[]{:S(2)}) collective-permute-start(bf16[384,128]{1,0:T(8,128)(2,1)S(1)} %get-tuple-element.17), channel_id=1, source_target_pairs={{0,24},{4,28},{8,16},{12,20},{16,8},{20,12},{24,0},{28,4},{1,25},{... | collective-permute-start | bytes 294920 | tf_op jit(solution)/shard_map/ppermute | solution.py:380
  5.4 5.4 %copy-start = (s32[6,3]{0,1:T(4,128)S(1)}, s32[6,3]{0,1:T(4,128)}, u32[]{:S(2)}) copy-start(s32[6,3]{0,1:T(4,128)} %param.11) | copy-start | bytes 220
  5.4 4.9 %collective-permute-start.2 = (bf16[384,128]{1,0:T(8,128)(2,1)S(1)}, bf16[384,128]{1,0:T(8,128)(2,1)S(1)}, u32[]{:S(2)}, u32[]{:S(2)}) collective-permute-start(bf16[384,128]{1,0:T(8,128)(2,1)S(1)} %get-tuple-element.21), channel_id=1, source_target_pairs={{0,16},{4,20},{8,24},{12,28},{16,0},{20,4},{24,8},{28,12},{1,17},{... | collective-permute-start | bytes 294920 | tf_op jit(solution)/shard_map/ppermute | solution.py:380
  5.9 4.7 %collective-permute-start.3 = (bf16[384,128]{1,0:T(8,128)(2,1)S(1)}, bf16[384,128]{1,0:T(8,128)(2,1)S(1)}, u32[]{:S(2)}, u32[]{:S(2)}) collective-permute-start(bf16[384,128]{1,0:T(8,128)(2,1)S(1)} %get-tuple-element.22), channel_id=1, source_target_pairs={{0,8},{4,12},{8,0},{12,4},{16,24},{20,28},{24,16},{28,20},{1,9},{5... | collective-permute-start | bytes 294920 | tf_op jit(solution)/shard_map/ppermute | solution.py:380
  6.1 1.2 %collective-permute-start.1 = (bf16[208,128]{1,0:T(8,128)(2,1)S(1)}, bf16[208,128]{1,0:T(8,128)(2,1)S(1)}, u32[]{:S(2)}, u32[]{:S(2)}) collective-permute-start(bf16[208,128]{1,0:T(8,128)(2,1)S(1)} %get-tuple-element.18), channel_id=1, source_target_pairs={{0,4},{4,0},{8,12},{12,8},{16,20},{20,16},{24,28},{28,24},{1,5},{5... | collective-permute-start | bytes 159752 | tf_op jit(solution)/shard_map/ppermute | solution.py:380
  8.6 2.3 %collective-permute-start.4 = (bf16[384,128]{1,0:T(8,128)(2,1)S(1)}, bf16[384,128]{1,0:T(8,128)(2,1)S(1)}, u32[]{:S(2)}, u32[]{:S(2)}) collective-permute-start(bf16[384,128]{1,0:T(8,128)(2,1)S(1)} %collective-permute-done.refs_3_), channel_id=1, source_target_pairs={{0,4},{4,0},{8,12},{12,8},{16,20},{20,16},{24,28},{28,24},{1,5},{5... | collective-permute-start | bytes 294920 | tf_op jit(solution)/shard_map/ppermute | solution.py:380
  10.3 1.3 %collective-permute-start.5 = (bf16[384,128]{1,0:T(8,128)(2,1)S(1)}, bf16[384,128]{1,0:T(8,128)(2,1)S(1)}, u32[]{:S(2)}, u32[]{:S(2)}) collective-permute-start(bf16[384,128]{1,0:T(8,128)(2,1)S(1)} %collective-permute-done.2.refs_4_), channel_id=1, source_target_pairs={{0,4},{4,0},{8,12},{12,8},{16,20},{20,16},{24,28},{28,24},{1,5},{5... | collective-permute-start | bytes 294920 | tf_op jit(solution)/shard_map/ppermute | solution.py:380
  10.6 1.3 %collective-permute-start.6 = (bf16[384,128]{1,0:T(8,128)(2,1)S(1)}, bf16[384,128]{1,0:T(8,128)(2,1)S(1)}, u32[]{:S(2)}, u32[]{:S(2)}) collective-permute-start(bf16[384,128]{1,0:T(8,128)(2,1)S(1)} %collective-permute-done.3.refs_5_), channel_id=1, source_target_pairs={{0,4},{4,0},{8,12},{12,8},{16,20},{20,16},{24,28},{28,24},{1,5},{5... | collective-permute-start | bytes 294920 | tf_op jit(solution)/shard_map/ppermute | solution.py:380
  17.1 5.3 %collective-permute-start.7 = (bf16[16,640]{1,0:T(8,128)(2,1)S(1)}, bf16[16,640]{1,0:T(8,128)(2,1)S(1)}, u32[]{:S(2)}, u32[]{:S(2)}) collective-permute-start(bf16[16,640]{1,0:T(8,128)(2,1)S(1)} %get-tuple-element.24), channel_id=1, source_target_pairs={{0,3},{1,0},{2,1},{3,2},{4,7},{5,4},{6,5},{7,6},{8,11},{9,8},{10,9... | collective-permute-start | bytes 61448 | tf_op jit(solution)/shard_map/ppermute | solution.py:413
  20.9 4.9 %collective-permute-start.8 = (bf16[16,640]{1,0:T(8,128)(2,1)S(1)}, bf16[16,640]{1,0:T(8,128)(2,1)S(1)}, u32[]{:S(2)}, u32[]{:S(2)}) collective-permute-start(bf16[16,640]{1,0:T(8,128)(2,1)S(1)} %get-tuple-element.25), channel_id=1, source_target_pairs={{0,2},{1,3},{2,0},{3,1},{4,6},{5,7},{6,4},{7,5},{8,10},{9,11},{10,... | collective-permute-start | bytes 61448 | tf_op jit(solution)/shard_map/ppermute | solution.py:413
  20.9 5.6 %collective-permute-start.9 = (bf16[16,640]{1,0:T(8,128)(2,1)S(1)}, bf16[16,640]{1,0:T(8,128)(2,1)S(1)}, u32[]{:S(2)}, u32[]{:S(2)}) collective-permute-start(bf16[16,640]{1,0:T(8,128)(2,1)S(1)} %get-tuple-element.26), channel_id=1, source_target_pairs={{0,1},{1,2},{2,3},{3,0},{4,5},{5,6},{6,7},{7,4},{8,9},{9,10},{10,1... | collective-permute-start | bytes 61448 | tf_op jit(solution)/shard_map/ppermute | solution.py:413
